TPU v7x, 128 devices: a whole 4x4x4 slice. The times are simulated.
128 devices in a mesh: aux: 16 (over y, x), orb: 8 (over z, core).
Axes of the slice: x: 4, y: 4, z: 4, core: 2. Of those that a mesh axis runs over, the one named last changes fastest.
Arguments:
- three_center: bfloat16 [64, 8, 64, 32, 128], P('aux'), may hold values from -0.5 to 0.5
- orbitals: bfloat16 [32768, 1024], P('aux', 'orb'), may hold values from -6 to 6
- partners: int32 [64, 8, 4], P('aux'), may hold values from 0 to 1023, as said below
- pair_owner: int32 [64, 56], P('aux'), may hold values from 0 to 2047, as said below
Outputs:
- exchange: float32 [2048, 1024], P(('aux', 'orb'))
Inputs may be any that keep to these rules, and one draw needn't show every extreme that they name: `partners`: basis block b is held by index b // 64 of aux. Of the 128 partner entries of the auxiliary blocks of one index of aux, at most 16 name blocks held by one index of aux; in every draw each index of aux has exactly 16 entries naming blocks of one index of aux. `pair_owner`: exchange block q belongs to owner device q // 16 (owners numbered aux index times the size of orb plus orb index). Of the 224 entries of the auxiliary blocks of one index of aux, at most 3 name blocks of one owner device; in every draw one owner device receives exactly 3 entries from every index of aux.
All inputs are finite; a program needn't handle non-finite values.
Results may differ from a plain program's by a relative error of at most 0.004.
Values may be sent and summed in bfloat16 or wider, within the bound.
No kernel may reach another device: no remote copies, remote signals or barrier semaphores. Data moves between devices by JAX's collectives and lax.ppermute only.
A program may use at most 128 MiB of HBM per device.

v0:
```python
import jax
import jax.numpy as jnp
import numpy as np
from jax import lax
from jax.sharding import PartitionSpec as P

OWN_DEV = 16


def cross_slots(count):
    return np.array(
        [
            first * count + second
            for first in range(count)
            for second in range(count)
            if first != second
        ],
        dtype=np.int32,
    )


def placement_of(table, owned, dev_count):
    owner = table // owned
    hits = (owner[..., None] == jnp.arange(dev_count, dtype=jnp.int32)).astype(jnp.int32)
    before = jnp.cumsum(hits, axis=1) - hits
    rank = jnp.sum(before * hits, axis=-1)
    return (owner, rank, table % owned)


def body(three_center, orbitals, partners, pair_owner):
    aux_count = lax.axis_size("aux")
    orb_count = lax.axis_size("orb")
    dev_count = aux_count * orb_count
    local_blocks, slots, aux_width, width = (
        three_center.shape[0],
        three_center.shape[1],
        three_center.shape[2],
        three_center.shape[3],
    )
    block_area = width * width
    occ_local = orbitals.shape[1]
    every_coeff = lax.all_gather(orbitals, "aux", axis=0, tiled=True)
    coeff_blocks = every_coeff.reshape(-1, width, occ_local)
    picked = coeff_blocks[partners].reshape(local_blocks, slots, -1, occ_local)
    half = jnp.einsum(
        "psaml,pslo->psamo", three_center, picked, preferred_element_type=jnp.float32
    ).astype(jnp.bfloat16)
    blocks = jnp.einsum("psamo,ptano->pstmn", half, half, preferred_element_type=jnp.float32)
    blocks = blocks.reshape(local_blocks, slots * slots, block_area)
    factor = 1.0 / np.sqrt(aux_width * occ_local * orb_count)
    partial_value = blocks[:, cross_slots(slots), :].reshape(-1, block_area) * factor
    owners_flat = pair_owner.reshape(-1)
    entries = owners_flat.shape[0]
    capacity = 2 * entries // dev_count
    owner, rank, unused_local = placement_of(owners_flat[None, :], OWN_DEV, dev_count)
    slot_ids = owner[0] * capacity + rank[0]
    packer = (
        jnp.arange(dev_count * capacity, dtype=jnp.int32)[:, None] == slot_ids[None, :]
    ).astype(jnp.float32)
    outgoing = jnp.dot(packer, partial_value, precision=lax.Precision.HIGHEST).reshape(
        aux_count, orb_count, capacity, block_area
    )
    table = lax.all_gather(pair_owner, "aux", axis=0, tiled=True).reshape(aux_count, -1)
    src_owner, src_rank, src_local = placement_of(table, OWN_DEV, dev_count)
    myself = lax.axis_index("aux") * orb_count + lax.axis_index("orb")
    mine = src_owner == myself
    by_rank = (
        mine[..., None] & (src_rank[..., None] == jnp.arange(capacity, dtype=jnp.int32))
    ).astype(jnp.float32)
    by_pair = (src_local[..., None] == jnp.arange(OWN_DEV, dtype=jnp.int32)).astype(jnp.float32)
    collect = jnp.einsum("aer,aeq->arq", by_rank, by_pair, precision=lax.Precision.HIGHEST)
    flat_out = outgoing.reshape(dev_count, capacity, block_area)
    incoming = lax.all_to_all(flat_out, ("aux", "orb"), split_axis=0, concat_axis=0, tiled=True)
    incoming = incoming.reshape(aux_count, orb_count, capacity, block_area)
    return jnp.einsum("arq,aorx->qx", collect, incoming, precision=lax.Precision.HIGHEST)


def solution(mesh):
    in_specs = (
        P("aux", None, None, None, None),
        P("aux", "orb"),
        P("aux", None, None),
        P("aux", None),
    )
    out_specs = P(("aux", "orb"), None)
    return jax.shard_map(body, mesh=mesh, in_specs=in_specs, out_specs=out_specs, check_vma=False)
```

profile of v0, /device:TPU:0, one launch (start us, length us, event | category | flops | bytes accessed | tf_op | source)
XLA Modules:
  0.0 216.4 jit_solution(3689314592297795310)
XLA Ops:
  6.5 0.0 all-gather.3.cloned.1.call-start
  6.5 0.7 all-gather.3.cloned.1.call-update
  7.3 0.7 compare_select_fusion
  8.0 0.1 copy.42
  8.1 0.1 reshape.322
  8.2 0.8 broadcast_in_dim_reshape.3
  8.9 0.1 convert_bitcast_fusion
  9.1 0.1 fusion.19
  9.3 23.7 %all-gather = s32[16,4,56]{2,1,0:T(4,128)S(1)} all-gather(s32[1,4,56]{2,1,0:T(4,128)} %bitcast.97), channel_id=1, replica_groups=mesh['aux'=16,'orb'=8] {'aux'}, dimensions={0}, use_global_device_ids=true | all-gather | bytes 15232 | tf_op jit(solution)/shard_map/all_gather | solution.py:63
  33.0 0.1 reshape.307
  33.1 0.1 copy.37
  33.2 0.7 pad_clamp_fusion
  33.9 0.2 fusion.23
  34.1 1.0 iota_compare_fusion
  35.1 0.1 pad_convert_fusion
  35.3 47.4 %all-gather.3.cloned.1.call-done = bf16[32768,128]{1,0:T(8,128)(2,1)} async-done(((bf16[2048,128]{1,0:T(8,128)(2,1)}), bf16[32768,128]{1,0:T(8,128)(2,1)}) %all-gather.3.cloned.1.call-update) | async-done | bytes 8388624 | tf_op jit(solution)/shard_map/all_gather | solution.py:42
  82.7 4.1 %gather_fusion = bf16[128,32,128]{2,1,0:T(8,128)(2,1)S(1)} fusion(bf16[1024,32,128]{2,1,0:T(8,128)(2,1)} %bitcast.96, s32[1024]{0:T(1024)S(1)} %pad_clamp_fusion.1), kind=kCustom, calls=%fused_computation | custom fusion | bytes 2097664 | tf_op jit(solution)/shard_map/gather | solution.py:44
  86.8 14.4 %fusion.59 = bf16[4,8,64,32,128,1]{4,3,2,5,1,0:T(8,128)(2,1)} fusion(bf16[4,8,128,128,1]{3,2,4,1,0:T(8,128)(2,1)S(1)} %bitcast.91, bf16[4,8,64,32,128]{4,3,2,1,0:T(8,128)(2,1)} %param.6), kind=kOutput, calls=%fused_computation.4.clone.clone.clone.2 | convolution fusion | flops 2155872256 | bytes 34603008 | tf_op jit(solution)/shard_map/psaml,pslo->psamo/dot_general | solution.py:45
  101.2 26.7 %fusion.6 = f32[4,8,8,32,32]{3,4,1,2,0:T(8,128)} fusion(bf16[4,8,128,128,1]{3,2,4,1,0:T(8,128)(2,1)S(1)} %bitcast.92, bf16[4,8,64,32,128]{4,3,2,1,0:T(8,128)(2,1)} %param.6, bf16[4,8,64,32,128,1]{4,3,2,5,1,0:T(8,128)(2,1)} %fusion.59), kind=kOutput, calls=%fused_computation.7 | convolution fusion | flops 6450839552 | bytes 35651584 | tf_op jit(solution)/shard_map/psamo,ptano->pstmn/dot_general | solution.py:48
  127.9 5.4 %copy.53 = f32[4,8,8,32,32]{4,3,0,2,1:T(8,128)} copy(f32[4,8,8,32,32]{3,4,1,2,0:T(8,128)} %fusion.6) | data formatting | bytes 2097152 | tf_op jit(solution)/shard_map/reshape | solution.py:49
  133.3 3.8 %reshape.347 = f32[4,64,1024]{2,0,1:T(4,128)S(1)} reshape(f32[4,8,8,32,32]{4,3,0,2,1:T(8,128)} %copy.53) | data formatting | bytes 2097152 | tf_op jit(solution)/shard_map/reshape | solution.py:49
  137.1 2.0 gather_fusion.1
  139.1 1.4 multiply_bitcast_fusion
  140.5 0.5 copy.45
  141.1 0.9 fusion.13
  142.0 2.4 %copy.46 = f32[128,3,1024]{2,1,0:T(4,128)} copy(f32[128,3,1024]{2,0,1:T(8,128)S(1)} %fusion.13) | data formatting | bytes 3145728 | tf_op jit(solution)/shard_map/dot_general | solution.py:60
  144.3 8.9 %all-to-all-start = ((f32[128,3,1024]{2,1,0:T(4,128)}), f32[128,3,1024]{2,1,0:T(4,128)}, u32[]{:S(2)}, u32[]{:S(2)}) async-start(f32[128,3,1024]{2,1,0:T(4,128)} %copy.46), calls=%async_computation | async-start | bytes 4194304 | tf_op jit(solution)/shard_map/all_to_all | solution.py:73
  153.3 47.7 %fusion.32 = s32[16,128,2,128]{1,0,3,2:T(8,128)S(1)} fusion(s32[16,128,2,128]{1,0,3,2:T(8,128)S(1)} %bitcast.89), kind=kOutput, calls=%fused_computation.61 | output fusion | flops 66584576 | bytes 4194304 | tf_op jit(solution)/shard_map/reduce-window
  201.0 0.1 broadcast_add_fusion
  201.2 5.0 %fusion.12 = s32[16,224]{0,1:T(8,128)S(1)} fusion(s32[16,256,128]{2,0,1:T(8,128)S(1)} %bitcast.90, s32[16,224]{0,1:T(8,128)S(1)} %copy.37), kind=kLoop, calls=%fused_computation.12 | loop fusion | flops 2290176 | bytes 1863680 | tf_op jit(solution)/shard_map/reduce_sum | solution.py:26
  206.2 0.1 copy.39
  206.3 0.2 fusion.15
  206.5 0.0 all-to-all-done
  206.5 2.1 bitcast_reduce_fusion
  208.6 1.0 convolution_bitcast_fusion
  (14 shorter events, 0.2 us)
Async XLA Ops:
  6.5 76.1 %all-gather.3.cloned.1.call-start = ((), (), s32[]{:S(2)}) async-start(), calls=%async_computation.1 | async-start | bytes 8912896 | tf_op jit(solution)/shard_map/all_gather | solution.py:42
  144.3 62.1 %all-to-all-start = ((f32[128,3,1024]{2,1,0:T(4,128)}), f32[128,3,1024]{2,1,0:T(4,128)}, u32[]{:S(2)}, u32[]{:S(2)}) async-start(f32[128,3,1024]{2,1,0:T(4,128)} %copy.46), calls=%async_computation | async-start | bytes 4194304 | tf_op jit(solution)/shard_map/all_to_all | solution.py:73
Sparse Core Ops, SparseCore 0:
  9.5 73.1 all-gather.2
where the time goes:
time: 217 us; the launch traced here: 216 us
  other arithmetic  59.5 us (27%)
  waiting for transfers between devices  48.1 us (22%)
  matrix products  43.2 us (20%)
  blocking collectives  23.7 us (11%)
  local copies, waits for them, and re-layouts  19.4 us (9%)
  between operations  13.6 us (6%)
  starting transfers between devices  8.93 us (4%)
    another operation x8, other arithmetic  48.3 us
    all_gather x1, waiting for transfers between devices, body(): every_coeff = lax.all_gather(orbitals, 'aux', axis=0, tiled=True)  47.4 us
    dot_general x1, matrix products, body(): jnp.einsum('psamo,ptano->pstmn', half, half, preferred_element_type=jnp.f...  26.7 us
    all_gather x1, blocking collectives, body(): lax.all_gather(pair_owner, 'aux', axis=0, tiled=True).reshape(aux_count, -1)  23.7 us
    dot_general x1, matrix products, body(): jnp.einsum('psaml,pslo->psamo', three_center, picked, preferred_element_t...  14.4 us
    reshape x2, local copies, waits for them, and re-layouts, body(): blocks = blocks.reshape(local_blocks, slots * slots, block_area)  9.16 us
    all_to_all x1, starting transfers between devices, body(): lax.all_to_all(flat_out, ('aux', 'orb'), split_axis=0, concat_axis=0, til...  8.92 us
    reduce_sum x2, other arithmetic, placement_of(): rank = jnp.sum(before * hits, axis=-1)  5.2 us
  transfers between devices with their start and end apart: 2, of which 1 were waited for; matrix products, arithmetic and copies ran while one was open for 27% of the time, Pallas kernels for 0%

commit v1 on v0

v1 whole, which is shorter than its diff:
```python
import functools

import jax
import jax.numpy as jnp
import numpy as np
from jax import lax
from jax.experimental import pallas as pl
from jax.experimental.pallas import tpu as pltpu
from jax.sharding import PartitionSpec as P

BS = 32
PA = 64
MS = 8
NPS = 4
AUX_DEV = 4
NOCC = 1024
BLK_DEV = 64
OWN_DEV = 16
CAP = 3
FETCH = 16
EP = MS * (MS - 1)
E = AUX_DEV * EP
ENTRIES = AUX_DEV * MS * NPS
OCC = 128
SIDE = 4
AUX = SIDE * SIDE
ORB = 8
DEVS = AUX * ORB
ROW_CAP = SIDE * FETCH
ROWS = 8
CHUNK = 16
LANES = 128
AXES = ("aux", "orb")


def shifted(step, near):
    pairs = []
    for aux in range(AUX):
        x, y = aux % SIDE, aux // SIDE
        for orb in range(ORB):
            if (orb % 2 == 0) == near:
                to = y * SIDE + (x + step) % SIDE
            else:
                to = ((y + step) % SIDE) * SIDE + x
            pairs.append((aux * ORB + orb, to * ORB + orb))
    return pairs


def pack_kernel(req1, req2, req3, own, got1, got2, got3, out1, out2, out3, shards, sems):
    copies = [
        pltpu.make_async_copy(
            src, shards.at[pl.ds(at * BLK_DEV, BLK_DEV)], sems.at[at]
        )
        for at, src in enumerate((own, got1, got2, got3))
    ]
    for copy in copies:
        copy.start()
    for copy in copies:
        copy.wait()
    for req, out in ((req1, out1), (req2, out2), (req3, out3)):

        @pl.loop(0, ROW_CAP, unroll=8)
        def _(r):
            out[r] = shards[req[0, r]]


def pack(reqs, own, got):
    block = jax.ShapeDtypeStruct((ROW_CAP, BS, OCC), jnp.bfloat16)
    return pl.pallas_call(
        pack_kernel,
        out_shape=[block] * 3,
        in_specs=[pl.BlockSpec(memory_space=pltpu.SMEM)] * 3 + [pl.BlockSpec(memory_space=pl.ANY)] * 4,
        out_specs=[pl.BlockSpec(memory_space=pltpu.VMEM)] * 3,
        scratch_shapes=[
            pltpu.VMEM((SIDE * BLK_DEV, BS, OCC), jnp.bfloat16),
            pltpu.SemaphoreType.DMA((4,)),
        ],
        compiler_params=pltpu.CompilerParams(vmem_limit_bytes=32 * 1024 * 1024),
        cost_estimate=pl.CostEstimate(flops=0, bytes_accessed=4 * 1024 * 1024, transcendentals=0),
        name="pack",
    )(*reqs, own, *got)


def main_kernel(
    picks, slots, own, got1, got2, got3, row1, row2, row3, tensor, out,
    blocks, pairs, half, total, staged, sems,
):
    p, c = pl.program_id(0), pl.program_id(1)
    sources = (own, got1, got2, got3, row1, row2, row3)

    @pl.when((p == 0) & (c == 0))
    def _():
        copies = [
            pltpu.make_async_copy(src, blocks.at[pl.ds(at * BLK_DEV, BLK_DEV)], sems.at[at])
            for at, src in enumerate(sources)
        ]
        for copy in copies:
            copy.start()
        staged[...] = jnp.zeros_like(staged)
        pairs[...] = jnp.zeros_like(pairs)
        for copy in copies:
            copy.wait()

    @pl.when(c == 0)
    def _():
        total[...] = jnp.zeros_like(total)
        for s in range(MS):
            side = (s % 2) * OCC
            for k in range(NPS):
                pairs[s // 2, pl.ds(side + k * BS, BS), pl.ds(side, OCC)] = blocks[
                    picks[(p * MS + s) * NPS + k]
                ]

    for pair in range(MS // 2):
        left = jnp.concatenate(
            [tensor[0, 2 * pair + side].reshape(CHUNK * BS, OCC) for side in range(2)], axis=1
        )
        both = jnp.dot(left, pairs[pair], preferred_element_type=jnp.float32).astype(jnp.bfloat16)
        for side in range(2):
            for a in range(CHUNK):
                half[pl.ds((2 * pair + side) * BS, BS), pl.ds(a * OCC, OCC)] = both[
                    a * BS : (a + 1) * BS, side * OCC : (side + 1) * OCC
                ]
    everything = half[...]
    total[...] += lax.dot_general(
        everything, everything, (((1,), (1,)), ((), ())), preferred_element_type=jnp.float32
    )

    @pl.when(c == PA // CHUNK - 1)
    def _():
        factor = np.float32(1.0 / np.sqrt(PA * NOCC))
        e = 0
        for s in range(MS):
            for t in range(MS):
                if s == t:
                    continue
                tile = jnp.concatenate(
                    [
                        total[pl.ds(s * BS + j * ROWS, ROWS), pl.ds(t * BS, BS)]
                        for j in range(BS // ROWS)
                    ],
                    axis=1,
                )
                staged[slots[p * EP + e]] = tile * factor
                e += 1

    @pl.when((p == AUX_DEV - 1) & (c == PA // CHUNK - 1))
    def _():
        out[...] = staged[...].reshape(DEVS * CAP * ROWS, LANES).astype(jnp.bfloat16)


def products(picks, slots, sources, tensor):
    anywhere = pl.BlockSpec(memory_space=pl.ANY)
    flops = AUX_DEV * (MS * PA * BS * OCC * OCC * 4 + 2 * PA * OCC * (MS * BS) ** 2)
    return pl.pallas_call(
        main_kernel,
        out_shape=jax.ShapeDtypeStruct((DEVS * CAP * ROWS, LANES), jnp.bfloat16),
        grid_spec=pltpu.PrefetchScalarGridSpec(
            num_scalar_prefetch=2,
            grid=(AUX_DEV, PA // CHUNK),
            in_specs=[anywhere] * 7
            + [pl.BlockSpec((1, MS, CHUNK, BS, OCC), lambda p, c, *_: (p, 0, c, 0, 0))],
            out_specs=pl.BlockSpec((DEVS * CAP * ROWS, LANES), lambda p, c, *_: (0, 0)),
            scratch_shapes=[
                pltpu.VMEM((7 * BLK_DEV, BS, OCC), jnp.bfloat16),
                pltpu.VMEM((MS // 2, 2 * OCC, 2 * OCC), jnp.bfloat16),
                pltpu.VMEM((MS * BS, CHUNK * OCC), jnp.bfloat16),
                pltpu.VMEM((MS * BS, MS * BS), jnp.float32),
                pltpu.VMEM((DEVS * CAP, ROWS, LANES), jnp.float32),
                pltpu.SemaphoreType.DMA((7,)),
            ],
        ),
        compiler_params=pltpu.CompilerParams(
            dimension_semantics=("arbitrary", "arbitrary"), vmem_limit_bytes=40 * 1024 * 1024
        ),
        cost_estimate=pl.CostEstimate(flops=flops, bytes_accessed=22 * 1024 * 1024, transcendentals=0),
        name="products",
    )(picks, slots, *sources, tensor)


def collect_kernel(where, incoming, out, total):
    total[...] = jnp.zeros_like(total)
    for a in range(AUX):
        rows = incoming[pl.ds(a * ORB * CAP * ROWS, ORB * CAP * ROWS), :].astype(jnp.float32)
        summed = jnp.sum(rows.reshape(ORB, CAP * ROWS, LANES), axis=0)
        for k in range(CAP):
            total[where[a, k]] += summed[k * ROWS : (k + 1) * ROWS, :]
    for r in range(ROWS):
        line = total[:, r, :]
        for j in range(BS // ROWS):
            out[:, pl.ds((j * ROWS + r) * BS, BS)] = line[:, j * BS : (j + 1) * BS]


def collect(where, incoming):
    return pl.pallas_call(
        collect_kernel,
        out_shape=jax.ShapeDtypeStruct((OWN_DEV, BS * BS), jnp.float32),
        in_specs=[pl.BlockSpec(memory_space=pltpu.SMEM), pl.BlockSpec(memory_space=pltpu.VMEM)],
        out_specs=pl.BlockSpec(memory_space=pltpu.VMEM),
        scratch_shapes=[pltpu.VMEM((OWN_DEV, ROWS, LANES), jnp.float32)],
        compiler_params=pltpu.CompilerParams(vmem_limit_bytes=16 * 1024 * 1024),
        name="collect",
    )(where, incoming)


def body(three_center, orbitals, partners, pair_owner):
    aux, orb = lax.axis_index("aux"), lax.axis_index("orb")
    x, y = aux % SIDE, aux // SIDE
    even = orb % 2 == 0
    near, far = jnp.where(even, x, y), jnp.where(even, y, x)
    own = orbitals.reshape(BLK_DEV, BS, OCC)

    got = [lax.ppermute(own, AXES, shifted(-j, True)) for j in (1, 2, 3)]

    wanted = partners.reshape(ENTRIES)
    source = wanted // BLK_DEV
    source_x, source_y = source % SIDE, source // SIDE
    rel_near = (jnp.where(even, source_x, source_y) - near) % SIDE
    rel_far = (jnp.where(even, source_y, source_x) - far) % SIDE
    order = np.arange(ENTRIES)
    earlier = jnp.asarray(order[None, :] < order[:, None])
    rank = jnp.sum((rel_far[None, :] == rel_far[:, None]) & earlier, axis=1, dtype=jnp.int32)
    at_source = rel_near * BLK_DEV + wanted % BLK_DEV
    picks = jnp.where(rel_far == 0, at_source, SIDE * BLK_DEV + (rel_far - 1) * ROW_CAP + rank)

    table = pair_owner.reshape(E)
    lists = []
    for j in (1, 2, 3):
        hits = (rel_far[None, :] == j) & (rank[None, :] == jnp.arange(ROW_CAP, dtype=jnp.int32)[:, None])
        lists.append(jnp.sum(jnp.where(hits, at_source[None, :], 0), axis=1, dtype=jnp.int32))
    requests, tables = [], [table]
    for j in (1, 2, 3):
        sent = jnp.concatenate([lists[j - 1], table, jnp.zeros((384 - ROW_CAP - E,), jnp.int32)])
        there = lax.ppermute(sent.reshape(1, 384), AXES, shifted(j, False))
        requests.append(there[:, :LANES])
        tables.append(there[0, ROW_CAP : ROW_CAP + E])

    row_blocks = pack(requests, own, got)
    rows = [lax.ppermute(row_blocks[j - 1], AXES, shifted(-j, False)) for j in (1, 2, 3)]

    line = jnp.stack(tables)
    grid = [line] + [lax.ppermute(line, AXES, shifted(j, True)) for j in (1, 2, 3)]
    every = jnp.stack(grid)
    mine = every // OWN_DEV == aux * ORB + orb
    ranks = jnp.cumsum(mine.astype(jnp.int32), axis=2) - 1
    local = [
        jnp.sum(jnp.where(mine & (ranks == k), every % OWN_DEV, 0), axis=2, dtype=jnp.int32)
        for k in range(CAP)
    ]
    local = jnp.stack(local, axis=-1)
    steps = np.arange(SIDE)
    local = local[(near - steps) % SIDE][:, (far - steps) % SIDE]
    local = jnp.where(even, local.transpose(1, 0, 2), local).reshape(AUX, CAP)

    owner = table // OWN_DEV
    order = np.arange(E)
    earlier = jnp.asarray(order[None, :] < order[:, None])
    slots = owner * CAP + jnp.sum((owner[None, :] == owner[:, None]) & earlier, axis=1, dtype=jnp.int32)

    outgoing = products(picks, slots, (own, *got, *rows), three_center)
    incoming = lax.all_to_all(outgoing, AXES, split_axis=0, concat_axis=0, tiled=True)
    return collect(local, incoming)


def solution(mesh):
    in_specs = (
        P("aux", None, None, None, None),
        P("aux", "orb"),
        P("aux", None, None),
        P("aux", None),
    )
    out_specs = P(("aux", "orb"), None)
    return jax.shard_map(body, mesh=mesh, in_specs=in_specs, out_specs=out_specs, check_vma=False)
```

time: 217 us -> 95.7 us (0.44)
  other arithmetic: 59.5 us -> 7.6 us
  matrix products: 43.2 us -> 0 us
  Pallas kernels: 0 us -> 30 us
  blocking collectives: 23.7 us -> 0 us
  waiting for transfers between devices: 48.1 us -> 24.7 us
  starting transfers between devices: 8.93 us -> 25.9 us
  between operations: 13.6 us -> 0.19 us
  local copies, waits for them, and re-layouts: 19.4 us -> 6.59 us
    all_gather x1 -> x0, waiting for transfers between devices: 47.4 us -> none  [body(): every_coeff = lax.all_gather(orbitals, 'aux', axis=0, tiled=True)]
    another operation x8 -> x6, other arithmetic: 48.3 us -> 5.02 us
    dot_general x5 -> x0, matrix products: 43.2 us -> none  [the longest x1 26.7 us: body(): jnp.einsum('psamo,ptano->pstmn', half, half, preferred_element_type=jnp.f...]
    pallas_call x0 -> x3, Pallas kernels: none -> 30 us  [the longest x1 26.2 us: products(): pl.pallas_call(main_kernel, out_shape=jax.ShapeDtypeStruct((DEVS * CAP *...]
    all_gather x1 -> x0, blocking collectives: 23.7 us -> none  [body(): lax.all_gather(pair_owner, 'aux', axis=0, tiled=True).reshape(aux_count, -1)]
    ppermute x0 -> x12, starting transfers between devices: none -> 19.1 us  [the longest x3 6.51 us: body(): lax.ppermute(row_blocks[j - 1], AXES, shifted(-j, False))]
    all_to_all x1, waiting for transfers between devices: 0.01 us -> 14.4 us  [body(): lax.all_to_all(outgoing, AXES, split_axis=0, concat_axis=0, tiled=True)]
    ppermute x0 -> x12, waiting for transfers between devices: none -> 10.4 us  [the longest x3 6.36 us: body(): lax.ppermute(line, AXES, shifted(j, True))]
  transfers between devices with their start and end apart: 2 -> 13, of which waited for: 1 -> 6; matrix products, arithmetic and copies ran while one was open for 27% -> 13% of each run, Pallas kernels for 0% -> 0%
where the time goes in v1:
time: 95.7 us; the launch traced here: 95 us
  Pallas kernels  30 us (31%)
  starting transfers between devices  25.9 us (27%)
  waiting for transfers between devices  24.7 us (26%)
  other arithmetic  7.6 us (8%)
  local copies, waits for them, and re-layouts  6.59 us (7%)
    pallas_call x1, Pallas kernels, products(): pl.pallas_call(main_kernel, out_shape=jax.ShapeDtypeStruct((DEVS * CAP *...  26.2 us
    all_to_all x1, waiting for transfers between devices, body(): lax.all_to_all(outgoing, AXES, split_axis=0, concat_axis=0, tiled=True)  14.4 us
    all_to_all x1, starting transfers between devices, body(): lax.all_to_all(outgoing, AXES, split_axis=0, concat_axis=0, tiled=True)  6.73 us
    ppermute x3, starting transfers between devices, body(): lax.ppermute(row_blocks[j - 1], AXES, shifted(-j, False))  6.51 us
    ppermute x3, waiting for transfers between devices, body(): lax.ppermute(line, AXES, shifted(j, True))  6.36 us
    ppermute x3, starting transfers between devices, body(): there = lax.ppermute(sent.reshape(1, 384), AXES, shifted(j, False))  5.91 us
    another operation x4, other arithmetic  4.93 us
    ppermute x3, starting transfers between devices, body(): got = [lax.ppermute(own, AXES, shifted(-j, True)) for j in (1, 2, 3)]  4.53 us
  transfers between devices with their start and end apart: 13, of which 6 were waited for; matrix products, arithmetic and copies ran while one was open for 13% of the time, Pallas kernels for 0%

profile of v1, /device:TPU:0, one launch (start us, length us, event | category | flops | bytes accessed | tf_op | source)
XLA Modules:
  0.0 95.0 jit_solution(13098900953229963168)
XLA Ops:
  0.0 2.8 %collective-permute-start.6 = (bf16[64,32,128]{2,1,0:T(8,128)(2,1)}, bf16[64,32,128]{2,1,0:T(8,128)(2,1)S(1)}, u32[]{:S(2)}, u32[]{:S(2)}) collective-permute-start(bf16[64,32,128]{2,1,0:T(8,128)(2,1)} %bitcast.18), channel_id=1, source_target_pairs={{0,24},{1,97},{2,26},{3,99},{4,28},{5,101},{6,30},{7,103},{8,0},{9... | collective-permute-start | bytes 1572872 | tf_op jit(solution)/shard_map/ppermute | solution.py:213
  2.8 0.8 collective-permute-start.7
  3.6 0.9 collective-permute-start.8
  4.5 0.8 copy.24
  5.3 0.1 reshape.302
  5.5 0.9 convert_reduce_fusion.1
  6.4 0.8 reshape.303
  7.2 0.2 select_reduce_fusion.2
  7.3 0.1 pad_add_fusion.5
  7.4 1.6 %collective-permute-start = (s32[1,384]{1,0:T(1,128)S(1)}, s32[1,384]{1,0:T(1,128)S(1)}, u32[]{:S(2)}, u32[]{:S(2)}) collective-permute-start(s32[1,384]{1,0:T(1,128)S(1)} %reshape.304), channel_id=1, source_target_pairs={{0,32},{1,9},{2,34},{3,11},{4,36},{5,13},{6,38},{7,15},{8,40},{9,1... | collective-permute-start | bytes 4616 | tf_op jit(solution)/shard_map/ppermute | solution.py:234
  9.0 2.9 %collective-permute-start.1 = (s32[1,384]{1,0:T(1,128)S(1)}, s32[1,384]{1,0:T(1,128)S(1)}, u32[]{:S(2)}, u32[]{:S(2)}) collective-permute-start(s32[1,384]{1,0:T(1,128)S(1)} %reshape.305), channel_id=1, source_target_pairs={{0,64},{1,17},{2,66},{3,19},{4,68},{5,21},{6,70},{7,23},{8,72},{9,... | collective-permute-start | bytes 4616 | tf_op jit(solution)/shard_map/ppermute | solution.py:234
  11.9 1.0 %convert_reduce_fusion = s32[224]{0:T(256)S(1)} fusion(pred[224,224]{1,0:T(32,128)(4,1)} %constant.186.clone, s32[224]{0:T(256)S(1)} %and_select_fusion), kind=kLoop, calls=%fused_computation.2 | loop fusion | flops 200480 | bytes 51968 | tf_op jit(solution)/shard_map/reduce_sum | solution.py:258
  13.0 0.0 collective-permute-done
  13.0 1.4 %collective-permute-start.2 = (s32[1,384]{1,0:T(1,128)S(1)}, s32[1,384]{1,0:T(1,128)S(1)}, u32[]{:S(2)}, u32[]{:S(2)}) collective-permute-start(s32[1,384]{1,0:T(1,128)S(1)} %reshape.306), channel_id=1, source_target_pairs={{0,96},{1,25},{2,98},{3,27},{4,100},{5,29},{6,102},{7,31},{8,104},... | collective-permute-start | bytes 4616 | tf_op jit(solution)/shard_map/ppermute | solution.py:234
  14.4 0.8 stack_reshape.3
  15.2 0.1 slice.40
  15.2 0.0 collective-permute-done.1
  15.2 0.1 slice.41
  15.3 1.3 %collective-permute-done.2 = s32[1,384]{1,0:T(1,128)S(1)} collective-permute-done((s32[1,384]{1,0:T(1,128)S(1)}, s32[1,384]{1,0:T(1,128)S(1)}, u32[]{:S(2)}, u32[]{:S(2)}) %collective-permute-start.2) | collective-permute-done | bytes 1568 | tf_op jit(solution)/shard_map/ppermute | solution.py:234
  16.6 0.1 slice.42
  16.7 0.0 collective-permute-done.6.got1
  16.7 0.0 collective-permute-done.7.got2
  16.7 2.7 %collective-permute-done.8.got3 = bf16[64,32,128]{2,1,0:T(8,128)(2,1)S(1)} collective-permute-done((bf16[64,32,128]{2,1,0:T(8,128)(2,1)}, bf16[64,32,128]{2,1,0:T(8,128)(2,1)S(1)}, u32[]{:S(2)}, u32[]{:S(2)}) %collective-permute-start.8) | collective-permute-done | bytes 524320 | tf_op jit(solution)/shard_map/ppermute | solution.py:213
  19.4 0.0 copy-start
  19.4 1.0 %copy-done = bf16[2048,128]{1,0:T(8,128)(2,1)S(1)} copy-done((bf16[2048,128]{1,0:T(8,128)(2,1)S(1)}, bf16[2048,128]{1,0:T(8,128)(2,1)}, u32[]{:S(2)}) %copy-start) | copy-done | bytes 524312
  20.4 2.0 %pack.1 = (bf16[64,32,128]{2,1,0:T(8,128)(2,1)S(1)}, bf16[64,32,128]{2,1,0:T(8,128)(2,1)}, bf16[64,32,128]{2,1,0:T(8,128)(2,1)}) custom-call(s32[1,128]{1,0:T(1,128)S(1)} %slice.46.req1, s32[1,128]{1,0:T(1,128)S(1)} %slice.47.req2, s32[1,128]{1,0:T(1,128)S(1)} %slice.48.req3, bf16[64,32,128]{2,1,0:T(8,128)(2,1)S(1)} %bitcast.21, ...), custom_call_target="tpu_custom_call" | custom-call | bytes 4194304 | tf_op jit(solution)/shard_map/pack/pallas_call | solution.py:69
  22.5 3.3 %collective-permute-start.10 = (bf16[64,32,128]{2,1,0:T(8,128)(2,1)}, bf16[64,32,128]{2,1,0:T(8,128)(2,1)S(1)}, u32[]{:S(2)}, u32[]{:S(2)}) collective-permute-start(bf16[64,32,128]{2,1,0:T(8,128)(2,1)} %get-tuple-element.9), channel_id=1, source_target_pairs={{0,64},{1,17},{2,66},{3,19},{4,68},{5,21},{6,70},{7,23},{8,72},{9,... | collective-permute-start | bytes 1572872 | tf_op jit(solution)/shard_map/ppermute | solution.py:239
  25.8 0.7 collective-permute-start.11
  26.4 2.6 %collective-permute-start.9 = (bf16[64,32,128]{2,1,0:T(8,128)(2,1)S(1)}, bf16[64,32,128]{2,1,0:T(8,128)(2,1)}, u32[]{:S(2)}, u32[]{:S(2)}) collective-permute-start(bf16[64,32,128]{2,1,0:T(8,128)(2,1)S(1)} %get-tuple-element.8), channel_id=1, source_target_pairs={{0,96},{1,25},{2,98},{3,27},{4,100},{5,29},{6,102},{7,31},{8,104},... | collective-permute-start | bytes 1572872 | tf_op jit(solution)/shard_map/ppermute | solution.py:239
  29.0 0.1 collective-permute-start.3
  29.1 2.1 %collective-permute-start.4 = (s32[4,224]{1,0:T(4,128)S(1)}, s32[4,224]{1,0:T(4,128)S(1)}, u32[]{:S(2)}, u32[]{:S(2)}) collective-permute-start(s32[4,224]{1,0:T(4,128)S(1)} %get-tuple-element.24), channel_id=1, source_target_pairs={{0,16},{1,65},{2,18},{3,67},{4,20},{5,69},{6,22},{7,71},{8,24},{9,... | collective-permute-start | bytes 10760 | tf_op jit(solution)/shard_map/ppermute | solution.py:242
  31.2 2.8 %collective-permute-done.3 = s32[4,224]{1,0:T(4,128)S(1)} collective-permute-done((s32[4,224]{1,0:T(4,128)S(1)}, s32[4,224]{1,0:T(4,128)S(1)}, u32[]{:S(2)}, u32[]{:S(2)}) %collective-permute-start.3) | collective-permute-done | bytes 3616 | tf_op jit(solution)/shard_map/ppermute | solution.py:242
  34.0 0.0 collective-permute-start.5
  34.0 0.4 collective-permute-done.4
  34.4 3.2 %collective-permute-done.5 = s32[4,224]{1,0:T(4,128)S(1)} collective-permute-done((s32[4,224]{1,0:T(4,128)S(1)}, s32[4,224]{1,0:T(4,128)S(1)}, u32[]{:S(2)}, u32[]{:S(2)}) %collective-permute-start.5) | collective-permute-done | bytes 3616 | tf_op jit(solution)/shard_map/ppermute | solution.py:242
  37.7 4.8 %reduce-window.6 = s32[4,4,2,128]{3,2,1,0:T(2,128)S(1)} reduce-window(s32[4,4,2,128]{3,2,1,0:T(2,128)S(1)} %reshape.311, s32[]{:T(128)} %constant.169.clone.1), window={size=1x1x1x128 pad=0_0x0_0x0_0x127_0}, to_apply=%region_4.5 | reduce-window | flops 520192 | bytes 32772 | tf_op jit(solution)/shard_map/reduce-window
  42.5 0.1 slice.43
  42.6 0.1 copy.25
  42.7 0.0 collective-permute-done.10.row2
  42.7 0.0 collective-permute-done.11.row3
  42.7 0.0 collective-permute-done.9.row1
  42.8 0.0 copy-start.1
  42.8 1.0 %copy-done.1 = bf16[2048,128]{1,0:T(8,128)(2,1)S(1)} copy-done((bf16[2048,128]{1,0:T(8,128)(2,1)S(1)}, bf16[2048,128]{1,0:T(8,128)(2,1)}, u32[]{:S(2)}) %copy-start.1) | copy-done | bytes 524312
  43.8 26.2 %products.1 = bf16[3072,128]{1,0:T(8,128)(2,1)} custom-call(s32[128]{0:T(128)S(1)} %get-tuple-element.17.picks, s32[224]{0:T(256)S(1)} %multiply_add_fusion.slots, bf16[64,32,128]{2,1,0:T(8,128)(2,1)S(1)} %bitcast.22, bf16[64,32,128]{2,1,0:T(8,128)(2,1)S(1)} %collective-permute-done.6.got1, bf16[64,32,128]{2,1,0:T(8,128)(2,1)S(1)} %collective-permute-done.7.got2, ...), custom_call_target="tpu_custom_call" | custom-call | flops 8589934592 | bytes 23068672 | tf_op jit(solution)/shard_map/products/pallas_call | solution.py:155
  70.0 6.7 %all-to-all-start = ((bf16[128,24,128]{2,1,0:T(8,128)(2,1)}), bf16[128,24,128]{2,1,0:T(8,128)(2,1)S(1)}, u32[]{:S(2)}, u32[]{:S(2)}) async-start(bf16[128,24,128]{2,1,0:T(8,128)(2,1)} %bitcast.11), calls=%async_computation | async-start | bytes 1572864 | tf_op jit(solution)/shard_map/all_to_all | solution.py:261
  76.8 0.1 copy.26
  76.9 0.1 broadcast_add_fusion
  77.0 0.3 select_reduce_fusion.5
  77.3 0.1 copy.27
  77.4 0.1 copy.28
  77.5 0.1 copy.29
  77.7 0.1 pad_add_fusion.1
  77.7 0.6 gather_fusion
  78.3 0.6 gather_fusion.1
  78.9 14.4 %all-to-all-done = bf16[128,24,128]{2,1,0:T(8,128)(2,1)S(1)} async-done(((bf16[128,24,128]{2,1,0:T(8,128)(2,1)}), bf16[128,24,128]{2,1,0:T(8,128)(2,1)S(1)}, u32[]{:S(2)}, u32[]{:S(2)}) %all-to-all-start) | async-done | bytes 786464 | tf_op jit(solution)/shard_map/all_to_all | solution.py:261
  93.3 1.7 %collect.1 = f32[16,1024]{1,0:T(8,128)} custom-call(s32[16,3]{1,0:T(8,128)S(1)} %bitcast.23, bf16[3072,128]{1,0:T(8,128)(2,1)S(1)} %bitcast.17), custom_call_target="tpu_custom_call" | custom-call | tf_op jit(solution)/shard_map/collect/pallas_call | solution.py:195
  (25 shorter events, 0.2 us)
Async XLA Ops:
  0.0 16.7 %collective-permute-start.6 = (bf16[64,32,128]{2,1,0:T(8,128)(2,1)}, bf16[64,32,128]{2,1,0:T(8,128)(2,1)S(1)}, u32[]{:S(2)}, u32[]{:S(2)}) collective-permute-start(bf16[64,32,128]{2,1,0:T(8,128)(2,1)} %bitcast.18), channel_id=1, source_target_pairs={{0,24},{1,97},{2,26},{3,99},{4,28},{5,101},{6,30},{7,103},{8,0},{9... | collective-permute-start | bytes 1572872 | tf_op jit(solution)/shard_map/ppermute | solution.py:213
  2.8 13.9 %collective-permute-start.7 = (bf16[64,32,128]{2,1,0:T(8,128)(2,1)}, bf16[64,32,128]{2,1,0:T(8,128)(2,1)S(1)}, u32[]{:S(2)}, u32[]{:S(2)}) collective-permute-start(bf16[64,32,128]{2,1,0:T(8,128)(2,1)} %bitcast.19), channel_id=1, source_target_pairs={{0,16},{1,65},{2,18},{3,67},{4,20},{5,69},{6,22},{7,71},{8,24},{9,... | collective-permute-start | bytes 1572872 | tf_op jit(solution)/shard_map/ppermute | solution.py:213
  3.6 15.7 %collective-permute-start.8 = (bf16[64,32,128]{2,1,0:T(8,128)(2,1)}, bf16[64,32,128]{2,1,0:T(8,128)(2,1)S(1)}, u32[]{:S(2)}, u32[]{:S(2)}) collective-permute-start(bf16[64,32,128]{2,1,0:T(8,128)(2,1)} %bitcast.20), channel_id=1, source_target_pairs={{0,8},{1,33},{2,10},{3,35},{4,12},{5,37},{6,14},{7,39},{8,16},{9,4... | collective-permute-start | bytes 1572872 | tf_op jit(solution)/shard_map/ppermute | solution.py:213
  7.4 5.6 %collective-permute-start = (s32[1,384]{1,0:T(1,128)S(1)}, s32[1,384]{1,0:T(1,128)S(1)}, u32[]{:S(2)}, u32[]{:S(2)}) collective-permute-start(s32[1,384]{1,0:T(1,128)S(1)} %reshape.304), channel_id=1, source_target_pairs={{0,32},{1,9},{2,34},{3,11},{4,36},{5,13},{6,38},{7,15},{8,40},{9,1... | collective-permute-start | bytes 4616 | tf_op jit(solution)/shard_map/ppermute | solution.py:234
  9.0 6.2 %collective-permute-start.1 = (s32[1,384]{1,0:T(1,128)S(1)}, s32[1,384]{1,0:T(1,128)S(1)}, u32[]{:S(2)}, u32[]{:S(2)}) collective-permute-start(s32[1,384]{1,0:T(1,128)S(1)} %reshape.305), channel_id=1, source_target_pairs={{0,64},{1,17},{2,66},{3,19},{4,68},{5,21},{6,70},{7,23},{8,72},{9,... | collective-permute-start | bytes 4616 | tf_op jit(solution)/shard_map/ppermute | solution.py:234
  13.0 3.6 %collective-permute-start.2 = (s32[1,384]{1,0:T(1,128)S(1)}, s32[1,384]{1,0:T(1,128)S(1)}, u32[]{:S(2)}, u32[]{:S(2)}) collective-permute-start(s32[1,384]{1,0:T(1,128)S(1)} %reshape.306), channel_id=1, source_target_pairs={{0,96},{1,25},{2,98},{3,27},{4,100},{5,29},{6,102},{7,31},{8,104},... | collective-permute-start | bytes 4616 | tf_op jit(solution)/shard_map/ppermute | solution.py:234
  19.4 1.0 %copy-start = (bf16[2048,128]{1,0:T(8,128)(2,1)S(1)}, bf16[2048,128]{1,0:T(8,128)(2,1)}, u32[]{:S(2)}) copy-start(bf16[2048,128]{1,0:T(8,128)(2,1)} %param.8) | copy-start | bytes 1572868
  22.5 20.2 %collective-permute-start.10 = (bf16[64,32,128]{2,1,0:T(8,128)(2,1)}, bf16[64,32,128]{2,1,0:T(8,128)(2,1)S(1)}, u32[]{:S(2)}, u32[]{:S(2)}) collective-permute-start(bf16[64,32,128]{2,1,0:T(8,128)(2,1)} %get-tuple-element.9), channel_id=1, source_target_pairs={{0,64},{1,17},{2,66},{3,19},{4,68},{5,21},{6,70},{7,23},{8,72},{9,... | collective-permute-start | bytes 1572872 | tf_op jit(solution)/shard_map/ppermute | solution.py:239
  25.8 17.0 %collective-permute-start.11 = (bf16[64,32,128]{2,1,0:T(8,128)(2,1)}, bf16[64,32,128]{2,1,0:T(8,128)(2,1)S(1)}, u32[]{:S(2)}, u32[]{:S(2)}) collective-permute-start(bf16[64,32,128]{2,1,0:T(8,128)(2,1)} %get-tuple-element.10), channel_id=1, source_target_pairs={{0,32},{1,9},{2,34},{3,11},{4,36},{5,13},{6,38},{7,15},{8,40},{9,1... | collective-permute-start | bytes 1572872 | tf_op jit(solution)/shard_map/ppermute | solution.py:239
  26.4 16.3 %collective-permute-start.9 = (bf16[64,32,128]{2,1,0:T(8,128)(2,1)S(1)}, bf16[64,32,128]{2,1,0:T(8,128)(2,1)}, u32[]{:S(2)}, u32[]{:S(2)}) collective-permute-start(bf16[64,32,128]{2,1,0:T(8,128)(2,1)S(1)} %get-tuple-element.8), channel_id=1, source_target_pairs={{0,96},{1,25},{2,98},{3,27},{4,100},{5,29},{6,102},{7,31},{8,104},... | collective-permute-start | bytes 1572872 | tf_op jit(solution)/shard_map/ppermute | solution.py:239
  29.0 5.0 %collective-permute-start.3 = (s32[4,224]{1,0:T(4,128)S(1)}, s32[4,224]{1,0:T(4,128)S(1)}, u32[]{:S(2)}, u32[]{:S(2)}) collective-permute-start(s32[4,224]{1,0:T(4,128)S(1)} %get-tuple-element.24), channel_id=1, source_target_pairs={{0,8},{1,33},{2,10},{3,35},{4,12},{5,37},{6,14},{7,39},{8,16},{9,4... | collective-permute-start | bytes 10760 | tf_op jit(solution)/shard_map/ppermute | solution.py:242
  29.1 5.3 %collective-permute-start.4 = (s32[4,224]{1,0:T(4,128)S(1)}, s32[4,224]{1,0:T(4,128)S(1)}, u32[]{:S(2)}, u32[]{:S(2)}) collective-permute-start(s32[4,224]{1,0:T(4,128)S(1)} %get-tuple-element.24), channel_id=1, source_target_pairs={{0,16},{1,65},{2,18},{3,67},{4,20},{5,69},{6,22},{7,71},{8,24},{9,... | collective-permute-start | bytes 10760 | tf_op jit(solution)/shard_map/ppermute | solution.py:242
  34.0 3.6 %collective-permute-start.5 = (s32[4,224]{1,0:T(4,128)S(1)}, s32[4,224]{1,0:T(4,128)S(1)}, u32[]{:S(2)}, u32[]{:S(2)}) collective-permute-start(s32[4,224]{1,0:T(4,128)S(1)} %get-tuple-element.24), channel_id=1, source_target_pairs={{0,24},{1,97},{2,26},{3,99},{4,28},{5,101},{6,30},{7,103},{8,0},{9... | collective-permute-start | bytes 10760 | tf_op jit(solution)/shard_map/ppermute | solution.py:242
  42.8 1.0 %copy-start.1 = (bf16[2048,128]{1,0:T(8,128)(2,1)S(1)}, bf16[2048,128]{1,0:T(8,128)(2,1)}, u32[]{:S(2)}) copy-start(bf16[2048,128]{1,0:T(8,128)(2,1)} %param.8) | copy-start | bytes 1572868
  70.0 23.2 %all-to-all-start = ((bf16[128,24,128]{2,1,0:T(8,128)(2,1)}), bf16[128,24,128]{2,1,0:T(8,128)(2,1)S(1)}, u32[]{:S(2)}, u32[]{:S(2)}) async-start(bf16[128,24,128]{2,1,0:T(8,128)(2,1)} %bitcast.11), calls=%async_computation | async-start | bytes 1572864 | tf_op jit(solution)/shard_map/all_to_all | solution.py:261

commit v2 on v0

v2 whole, which is shorter than its diff:
```python
import functools

import jax
import jax.numpy as jnp
import numpy as np
from jax import lax
from jax.experimental import pallas as pl
from jax.experimental.pallas import tpu as pltpu
from jax.sharding import PartitionSpec as P

BS = 32
PA = 64
MS = 8
NPS = 4
AUX_DEV = 4
NOCC = 1024
BLK_DEV = 64
OWN_DEV = 16
CAP = 3
FETCH = 16
EP = MS * (MS - 1)
E = AUX_DEV * EP
ENTRIES = AUX_DEV * MS * NPS
OCC = 128
SIDE = 4
AUX = SIDE * SIDE
ORB = 8
DEVS = AUX * ORB
ROW_CAP = SIDE * FETCH
EARLY = 32
LATE = ROW_CAP - EARLY
ROWS = 8
CHUNK = 8
LANES = 128
AXES = ("aux", "orb")


def shifted(step, near):
    pairs = []
    for aux in range(AUX):
        x, y = aux % SIDE, aux // SIDE
        for orb in range(ORB):
            if (orb % 2 == 0) == near:
                to = y * SIDE + (x + step) % SIDE
            else:
                to = ((y + step) % SIDE) * SIDE + x
            pairs.append((aux * ORB + orb, to * ORB + orb))
    return pairs


def in_vmem(array):
    return pltpu.with_memory_space_constraint(array, pltpu.VMEM)


def in_hbm(array):
    return pltpu.with_memory_space_constraint(array, pltpu.HBM)


VMEM = pl.BlockSpec(memory_space=pltpu.VMEM)
SMEM = pl.BlockSpec(memory_space=pltpu.SMEM)
HBM = pl.BlockSpec(memory_space=pltpu.HBM)
MIB = 1024 * 1024
LIST_ROW = AUX_DEV
BLOCKS = ROW_CAP + 3 * ROW_CAP
SOON = ROW_CAP + 3 * EARLY


def cost(flops, moved):
    return pl.CostEstimate(flops=flops, bytes_accessed=moved, transcendentals=0)


def columns(row):
    return jnp.broadcast_to(row, (LANES, LANES)).T


def plan_kernel(place, partners, owners, sent0, sent1, sent2, sent3, picks, slots, count):
    near, far, even = place[0], place[1], place[2]
    table = jnp.full((ROWS, LANES), -1, jnp.int32)
    for sent in (sent0, sent1, sent2, sent3):
        sent[...] = table
        sent[pl.ds(0, AUX_DEV), pl.ds(0, EP)] = owners[...]

    named = partners[...].reshape(AUX_DEV * MS, NPS)
    at = lax.broadcasted_iota(jnp.int32, (AUX_DEV * MS, LANES), 0) * NPS
    lane = lax.broadcasted_iota(jnp.int32, (AUX_DEV * MS, LANES), 1)
    spread = jnp.zeros((AUX_DEV * MS, LANES), jnp.int32)
    for k in range(NPS):
        spread += jnp.where(lane == at + k, named[:, k : k + 1], 0)
    wanted = jnp.sum(spread, axis=0, keepdims=True)

    down = lax.broadcasted_iota(jnp.int32, (LANES, LANES), 0)
    across = lax.broadcasted_iota(jnp.int32, (LANES, LANES), 1)
    earlier = down < across
    source, local = wanted >> 6, wanted & 63
    source_x, source_y = source & 3, source >> 2
    rel_near = (source_y + even * (source_x - source_y) - near) & 3
    rel_far = (source_x + even * (source_y - source_x) - far) & 3
    same = (columns(rel_far) == rel_far) & earlier
    rank = jnp.sum(same.astype(jnp.int32), axis=0, keepdims=True)
    packed = columns((rel_far * ROW_CAP + rank) * 256 + rel_near * BLK_DEV + local)
    key, value = packed >> 8, packed & 255
    for both, sends in enumerate(((sent0, sent1), (sent2, sent3))):
        line = jnp.sum(jnp.where(key == across + both * LANES, value, 0), axis=0, keepdims=True)
        for sent in sends:
            sent[pl.ds(LIST_ROW, 1), :] = line

    there = rel_far - 1
    remote = jnp.where(
        rank < EARLY, ROW_CAP + there * EARLY + rank, SOON + there * LATE + rank - EARLY
    )
    pick = jnp.where(rel_far == 0, rank, remote)
    picks[...] = pick
    missing = jnp.where(pick >= SOON, across[:1], LANES)
    count[...] = jnp.broadcast_to(jnp.min(missing, axis=1, keepdims=True) >> 5, (1, LANES))

    owner = sent0[...] >> 4
    stood = []
    for p in range(AUX_DEV):
        row = owner[p : p + 1]
        column = columns(row)
        hits = ((column == row) & earlier).astype(jnp.int32)
        for before in stood:
            hits += (before == row).astype(jnp.int32)
        slots[pl.ds(p, 1), :] = row * CAP + jnp.sum(hits, axis=0, keepdims=True)
        stood.append(column)


def plan(place, partners, owners):
    tile = jax.ShapeDtypeStruct((ROWS, LANES), jnp.int32)
    line = jax.ShapeDtypeStruct((1, LANES), jnp.int32)
    return pl.pallas_call(
        plan_kernel,
        out_shape=[tile] * 4 + [line, tile, line],
        in_specs=[SMEM] + [VMEM] * 2,
        out_specs=[VMEM] * 7,
        compiler_params=pltpu.CompilerParams(vmem_limit_bytes=2 * MIB),
        cost_estimate=cost(0, 64 * 1024),
        name="plan",
    )(place, partners, owners)


STAGED = (DEVS * CAP + 1, ROWS, LANES)
PAIRS = (2, MS // 2, 2 * OCC, 2 * OCC)


def stage_kernel(tensor, own, picks, slots, count, tensor_out, own_out, staged, pairs, sems):
    del picks, slots, count
    copies = [
        pltpu.make_async_copy(own, own_out, sems.at[0]),
        pltpu.make_async_copy(tensor, tensor_out, sems.at[1]),
    ]
    for copy in copies:
        copy.start()
    staged[...] = jnp.zeros_like(staged)
    pairs[...] = jnp.zeros_like(pairs)
    for copy in copies:
        copy.wait()


def stage(tensor, own, *lists):
    return pl.pallas_call(
        stage_kernel,
        out_shape=[
            pltpu.VMEM(tensor.shape, tensor.dtype),
            pltpu.VMEM(own.shape, own.dtype),
            pltpu.VMEM(STAGED, jnp.float32),
            pltpu.VMEM(PAIRS, jnp.bfloat16),
        ],
        in_specs=[HBM] * 2 + [SMEM] * 3,
        out_specs=[VMEM] * 4,
        scratch_shapes=[pltpu.SemaphoreType.DMA((2,))],
        compiler_params=pltpu.CompilerParams(vmem_limit_bytes=MIB),
        cost_estimate=cost(0, 18 * MIB),
        name="stage",
    )(in_hbm(tensor), in_hbm(own), *lists)


def pack_early_kernel(
    req1, req2, req3, own, got1, got2, got3, out1, out2, out3, shards
):
    for at, src in enumerate((own, got1, got2, got3)):
        shards[pl.ds(at * BLK_DEV, BLK_DEV)] = src[...]
    for j, (req, out) in enumerate(((req1, out1), (req2, out2), (req3, out3))):

        @pl.loop(0, EARLY, unroll=8)
        def _(r):
            out[r] = shards[req[LIST_ROW, (j + 1) % 2 * ROW_CAP + r]]


def block_array(rows):
    return pltpu.VMEM((rows, BS, OCC), jnp.bfloat16)


def pack_early(received, own, got):
    return pl.pallas_call(
        pack_early_kernel,
        out_shape=[block_array(EARLY)] * 3 + [block_array(SIDE * BLK_DEV)],
        in_specs=[SMEM] * 3 + [VMEM] * 4,
        out_specs=[VMEM] * 4,
        compiler_params=pltpu.CompilerParams(vmem_limit_bytes=2 * MIB),
        cost_estimate=cost(0, 4 * MIB),
        name="pack_early",
    )(*received, own, *[in_vmem(g) for g in got])


def pack_late_kernel(
    req0, req1, req2, req3, shards, mine, tab1, tab2, tab3, out0, out1, out2, out3, tables
):
    for at, src in enumerate((mine, tab1, tab2, tab3)):
        tables[at] = src[...]
    for j, (req, out) in enumerate(((req1, out1), (req2, out2), (req3, out3))):

        @pl.loop(0, LATE, unroll=8)
        def _(r):
            out[r] = shards[req[LIST_ROW, (j + 1) % 2 * ROW_CAP + EARLY + r]]

    @pl.loop(0, ROW_CAP, unroll=8)
    def _(r):
        out0[r] = shards[req0[LIST_ROW, r]]


def pack_late(mine, received, shards):
    return pl.pallas_call(
        pack_late_kernel,
        out_shape=[block_array(ROW_CAP)]
        + [block_array(LATE)] * 3
        + [pltpu.VMEM((SIDE, ROWS, LANES), jnp.int32)],
        in_specs=[SMEM] * 4 + [VMEM] * 5,
        out_specs=[VMEM] * 5,
        compiler_params=pltpu.CompilerParams(vmem_limit_bytes=2 * MIB),
        cost_estimate=cost(0, 2 * MIB),
        name="pack_late",
    )(mine, *received, shards, mine, *received)


def run_blocks(low, high, picks, slots, tensor, staged, pairs, blocks, total, half):
    def fill(p):
        for s in range(MS):
            side = (s % 2) * OCC
            for k in range(NPS):
                pairs[p % 2, s // 2, pl.ds(side + k * BS, BS), pl.ds(side, OCC)] = blocks[
                    picks[0, (p * MS + s) * NPS + k]
                ]

    def first(p, c):
        for pair in range(MS // 2):
            left = jnp.concatenate(
                [
                    tensor[p, 2 * pair + side, pl.ds(c * CHUNK, CHUNK)].reshape(CHUNK * BS, OCC)
                    for side in range(2)
                ],
                axis=1,
            )
            both = jnp.dot(left, pairs[p % 2, pair], preferred_element_type=jnp.float32)
            both = both.astype(jnp.bfloat16)
            for side in range(2):
                for a in range(CHUNK):
                    half[c % 2, pl.ds((2 * pair + side) * BS, BS), pl.ds(a * OCC, OCC)] = both[
                        a * BS : (a + 1) * BS, side * OCC : (side + 1) * OCC
                    ]

    def second(p, c):
        slab = half[c % 2]
        product = lax.dot_general(
            slab, slab, (((1,), (1,)), ((), ())), preferred_element_type=jnp.float32
        )
        if c == 0:
            total[p % 2] = product
        else:
            total[p % 2] += product

    @pl.when(low < high)
    def _():
        fill(low)

    last = PA // CHUNK

    @pl.loop(low, high)
    def _(p):
        first(p, 0)
        for c in range(last):
            if c + 1 < last:
                first(p, c + 1)
            second(p, c)
            if c == 0:
                put(jnp.maximum(p - 1, 0), p > 0, slots, total, staged)
            if c == 1:
                fill(jnp.minimum(p + 1, high - 1))


def put(p, valid, slots, total, staged):
    factor = np.float32(1.0 / np.sqrt(PA * NOCC))
    e = 0
    for s in range(MS):
        for t in range(MS):
            if s == t:
                continue
            tile = jnp.concatenate(
                [
                    total[p % 2, pl.ds(s * BS + j * ROWS, ROWS), pl.ds(t * BS, BS)]
                    for j in range(BS // ROWS)
                ],
                axis=1,
            )
            staged[jnp.where(valid, slots[p, e], DEVS * CAP)] = tile * factor
            e += 1


def early_kernel(
    count, picks, slots, row0, row1, row2, row3, tensor, staged0, pairs0,
    staged, pairs, blocks, total, half,
):
    del staged0, pairs0
    blocks[pl.ds(0, ROW_CAP)] = row0[...]
    for at, src in enumerate((row1, row2, row3)):
        blocks[pl.ds(ROW_CAP + at * EARLY, EARLY)] = src[...]
    run_blocks(0, count[0, 0], picks, slots, tensor, staged, pairs, blocks, total, half)


def late_kernel(
    count, picks, slots, late1, late2, late3, tensor, staged0, pairs0, blocks0, total0,
    staged, pairs, blocks, total, out, half,
):
    del staged0, pairs0, blocks0, total0
    for at, src in enumerate((late1, late2, late3)):
        blocks[pl.ds(SOON + at * LATE, LATE)] = src[...]
    run_blocks(count[0, 0], AUX_DEV, picks, slots, tensor, staged, pairs, blocks, total, half)
    put(AUX_DEV - 1, True, slots, total, staged)
    done = staged[pl.ds(0, DEVS * CAP)]
    out[...] = done.reshape(DEVS * CAP * ROWS, LANES).astype(jnp.bfloat16)


STATE = [
    pltpu.VMEM(STAGED, jnp.float32),
    pltpu.VMEM(PAIRS, jnp.bfloat16),
    pltpu.VMEM((BLOCKS, BS, OCC), jnp.bfloat16),
    pltpu.VMEM((2, MS * BS, MS * BS), jnp.float32),
]
HALF = pltpu.VMEM((2, MS * BS, CHUNK * OCC), jnp.bfloat16)
FLOPS = 2 * (MS * PA * BS * OCC * OCC * 4 + 2 * PA * OCC * (MS * BS) ** 2)


def early_products(count, picks, slots, rows, tensor, staged, pairs):
    return pl.pallas_call(
        early_kernel,
        out_shape=STATE,
        in_specs=[SMEM] * 3 + [VMEM] * 7,
        out_specs=[VMEM] * 4,
        input_output_aliases={8: 0, 9: 1},
        scratch_shapes=[HALF],
        compiler_params=pltpu.CompilerParams(vmem_limit_bytes=8 * MIB),
        cost_estimate=cost(FLOPS, 8 * MIB),
        name="early_products",
    )(count, picks, slots, *[in_vmem(r) for r in rows], tensor, staged, pairs)


def late_products(count, picks, slots, late, tensor, state):
    return pl.pallas_call(
        late_kernel,
        out_shape=STATE + [jax.ShapeDtypeStruct((DEVS * CAP * ROWS, LANES), jnp.bfloat16)],
        in_specs=[SMEM] * 3 + [VMEM] * 8,
        out_specs=[VMEM] * 5,
        input_output_aliases={7: 0, 8: 1, 9: 2, 10: 3},
        scratch_shapes=[HALF],
        compiler_params=pltpu.CompilerParams(vmem_limit_bytes=8 * MIB),
        cost_estimate=cost(FLOPS, 8 * MIB),
        name="late_products",
    )(count, picks, slots, *[in_vmem(r) for r in late], tensor, *state)[4]


def locate_kernel(place, tables0, tables1, tables2, tables3, where):
    none = 1 << 20
    lane = lax.broadcasted_iota(jnp.int32, (AUX, LANES), 1)
    left = []
    for p in range(AUX_DEV):
        row = jnp.concatenate(
            [tables[:, p, :] for tables in (tables0, tables1, tables2, tables3)], axis=0
        )
        mark = (p * LANES + lane) * OWN_DEV + (row & (OWN_DEV - 1))
        left.append(jnp.where((row >> 4) == place[3], mark, none))
    found = jnp.zeros((AUX, LANES), jnp.int32)
    for k in range(CAP):
        least = jnp.minimum(jnp.minimum(left[0], left[1]), jnp.minimum(left[2], left[3]))
        least = jnp.min(least, axis=1, keepdims=True)
        found = jnp.where(lane == k, least & (OWN_DEV - 1), found)
        left = [jnp.where(v > least, v, none) for v in left]
    where[...] = found


def locate(place, every):
    return pl.pallas_call(
        locate_kernel,
        out_shape=jax.ShapeDtypeStruct((AUX, LANES), jnp.int32),
        in_specs=[SMEM] + [VMEM] * 4,
        out_specs=VMEM,
        compiler_params=pltpu.CompilerParams(vmem_limit_bytes=2 * MIB),
        cost_estimate=cost(0, 64 * 1024),
        name="locate",
    )(place, *every)


def collect_kernel(place, where, incoming, out, total):
    total[...] = jnp.zeros_like(total)
    for a in range(AUX):
        x, y = a % SIDE, a // SIDE
        even = place[2] == 1
        i = (place[0] - jnp.where(even, x, y)) & 3
        j = (place[1] - jnp.where(even, y, x)) & 3
        rows = incoming[pl.ds(a * ORB * CAP * ROWS, ORB * CAP * ROWS), :].astype(jnp.float32)
        summed = jnp.sum(rows.reshape(ORB, CAP * ROWS, LANES), axis=0)
        for k in range(CAP):
            total[where[i * SIDE + j, k]] += summed[k * ROWS : (k + 1) * ROWS, :]
    for r in range(ROWS):
        line = total[:, r, :]
        for j in range(BS // ROWS):
            out[:, pl.ds((j * ROWS + r) * BS, BS)] = line[:, j * BS : (j + 1) * BS]


def collect(place, where, incoming):
    return pl.pallas_call(
        collect_kernel,
        out_shape=jax.ShapeDtypeStruct((OWN_DEV, BS * BS), jnp.float32),
        in_specs=[SMEM, SMEM, VMEM],
        out_specs=VMEM,
        scratch_shapes=[pltpu.VMEM((OWN_DEV, ROWS, LANES), jnp.float32)],
        compiler_params=pltpu.CompilerParams(vmem_limit_bytes=16 * MIB),
        name="collect",
    )(place, where, incoming)


def body(three_center, orbitals, partners, pair_owner):
    aux, orb = lax.axis_index("aux"), lax.axis_index("orb")
    x, y = aux % SIDE, aux // SIDE
    even = orb % 2 == 0
    near, far = jnp.where(even, x, y), jnp.where(even, y, x)
    own = orbitals.reshape(BLK_DEV, BS, OCC)

    got = [lax.ppermute(own, AXES, shifted(-j, True)) for j in (1, 2, 3)]

    place = jnp.stack([near, far, even.astype(jnp.int32), aux * ORB + orb]).astype(jnp.int32)
    mine, *sent, picks, slots, count = plan(place, partners, pair_owner)
    received = [lax.ppermute(sent[j - 1], AXES, shifted(j, False)) for j in (1, 2, 3)]

    tensor, own, staged, pairs = stage(three_center, own, picks, slots, count)
    *early, shards = pack_early(received, own, got)
    early = [lax.ppermute(early[j - 1], AXES, shifted(-j, False)) for j in (1, 2, 3)]
    row0, *late, tables = pack_late(mine, received, shards)
    late = [lax.ppermute(late[j - 1], AXES, shifted(-j, False)) for j in (1, 2, 3)]
    every = [tables] + [lax.ppermute(tables, AXES, shifted(j, True)) for j in (1, 2, 3)]

    state = early_products(count, picks, slots, (row0, *early), tensor, staged, pairs)
    outgoing = late_products(count, picks, slots, late, tensor, state)
    incoming = lax.all_to_all(outgoing, AXES, split_axis=0, concat_axis=0, tiled=True)

    return collect(place, locate(place, every), incoming)


def solution(mesh):
    in_specs = (
        P("aux", None, None, None, None),
        P("aux", "orb"),
        P("aux", None, None),
        P("aux", None),
    )
    out_specs = P(("aux", "orb"), None)
    return jax.shard_map(body, mesh=mesh, in_specs=in_specs, out_specs=out_specs, check_vma=False)
```

time: 217 us -> 78.1 us (0.36)
  other arithmetic: 59.5 us -> 0.08 us
  matrix products: 43.2 us -> 0 us
  waiting for transfers between devices: 48.1 us -> 15.7 us
  Pallas kernels: 0 us -> 26.8 us
  starting transfers between devices: 8.93 us -> 33.4 us
  blocking collectives: 23.7 us -> 0 us
  local copies, waits for them, and re-layouts: 19.4 us -> 1.47 us
  between operations: 13.6 us -> 0.12 us
    another operation x8 -> x1, other arithmetic: 48.3 us -> 0.08 us  [body(): jnp.stack([near, far, even.astype(jnp.int32), aux * ORB + orb])]
    all_gather x1 -> x0, waiting for transfers between devices: 47.4 us -> none  [body(): every_coeff = lax.all_gather(orbitals, 'aux', axis=0, tiled=True)]
    dot_general x5 -> x0, matrix products: 43.2 us -> none  [the longest x1 26.7 us: body(): jnp.einsum('psamo,ptano->pstmn', half, half, preferred_element_type=jnp.f...]
    pallas_call x0 -> x8, Pallas kernels: none -> 26.8 us  [the longest x1 9.22 us: early_products(): pl.pallas_call(early_kernel, out_shape=STATE, in_specs=[SMEM] * 3 + [VMEM...]
    ppermute x0 -> x15, starting transfers between devices: none -> 24.1 us  [the longest x3 6.05 us: body(): lax.ppermute(sent[j - 1], AXES, shifted(j, False))]
    all_gather x1 -> x0, blocking collectives: 23.7 us -> none  [body(): lax.all_gather(pair_owner, 'aux', axis=0, tiled=True).reshape(aux_count, -1)]
    ppermute x0 -> x15, waiting for transfers between devices: none -> 11.7 us  [the longest x3 7.45 us: body(): lax.ppermute(tables, AXES, shifted(j, True))]
    reshape x3 -> x0, local copies, waits for them, and re-layouts: 9.24 us -> none  [the longest x2 9.16 us: body(): blocks = blocks.reshape(local_blocks, slots * slots, block_area)]
  transfers between devices with their start and end apart: 2 -> 16, of which waited for: 1 -> 6; matrix products, arithmetic and copies ran while one was open for 27% -> 1% of each run, Pallas kernels for 0% -> 25%
where the time goes in v2:
time: 78.1 us; the launch traced here: 77.6 us
  starting transfers between devices  33.4 us (43%)
  Pallas kernels  26.8 us (34%)
  waiting for transfers between devices  15.7 us (20%)
  local copies, waits for them, and re-layouts  1.47 us (2%)
    all_to_all x1, starting transfers between devices, body(): lax.all_to_all(outgoing, AXES, split_axis=0, concat_axis=0, tiled=True)  9.37 us
    pallas_call x1, Pallas kernels, early_products(): pl.pallas_call(early_kernel, out_shape=STATE, in_specs=[SMEM] * 3 + [VMEM...  9.22 us
    ppermute x3, waiting for transfers between devices, body(): lax.ppermute(tables, AXES, shifted(j, True))  7.45 us
    pallas_call x1, Pallas kernels, stage(): pl.pallas_call(stage_kernel, out_shape=[pltpu.VMEM(tensor.shape, tensor.d...  6.58 us
    ppermute x3, starting transfers between devices, body(): lax.ppermute(sent[j - 1], AXES, shifted(j, False))  6.05 us
    ppermute x3, starting transfers between devices, body(): got = [lax.ppermute(own, AXES, shifted(-j, True)) for j in (1, 2, 3)]  5.74 us
    pallas_call x1, Pallas kernels, late_products(): pl.pallas_call(late_kernel, out_shape=STATE + [jax.ShapeDtypeStruct((DEVS...  4.76 us
    ppermute x3, starting transfers between devices, body(): lax.ppermute(late[j - 1], AXES, shifted(-j, False))  4.68 us
  transfers between devices with their start and end apart: 16, of which 6 were waited for; matrix products, arithmetic and copies ran while one was open for 1% of the time, Pallas kernels for 25%

profile of v2, /device:TPU:0, one launch (start us, length us, event | category | flops | bytes accessed | tf_op | source)
XLA Modules:
  0.0 77.6 jit_solution(135833481706834800)
XLA Ops:
  0.0 1.6 %collective-permute-start.5 = (bf16[64,32,128]{2,1,0:T(8,128)(2,1)}, bf16[64,32,128]{2,1,0:T(8,128)(2,1)S(1)}, u32[]{:S(2)}, u32[]{:S(2)}) collective-permute-start(bf16[64,32,128]{2,1,0:T(8,128)(2,1)} %bitcast.8), channel_id=1, source_target_pairs={{0,8},{1,33},{2,10},{3,35},{4,12},{5,37},{6,14},{7,39},{8,16},{9,4... | collective-permute-start | bytes 1572872 | tf_op jit(solution)/shard_map/ppermute | solution.py:438
  1.6 2.7 %collective-permute-start.4 = (bf16[64,32,128]{2,1,0:T(8,128)(2,1)}, bf16[64,32,128]{2,1,0:T(8,128)(2,1)S(1)}, u32[]{:S(2)}, u32[]{:S(2)}) collective-permute-start(bf16[64,32,128]{2,1,0:T(8,128)(2,1)} %bitcast.9), channel_id=1, source_target_pairs={{0,16},{1,65},{2,18},{3,67},{4,20},{5,69},{6,22},{7,71},{8,24},{9,... | collective-permute-start | bytes 1572872 | tf_op jit(solution)/shard_map/ppermute | solution.py:438
  4.3 1.4 %collective-permute-start.3 = (bf16[64,32,128]{2,1,0:T(8,128)(2,1)}, bf16[64,32,128]{2,1,0:T(8,128)(2,1)S(1)}, u32[]{:S(2)}, u32[]{:S(2)}) collective-permute-start(bf16[64,32,128]{2,1,0:T(8,128)(2,1)} %bitcast.10), channel_id=1, source_target_pairs={{0,24},{1,97},{2,26},{3,99},{4,28},{5,101},{6,30},{7,103},{8,0},{9... | collective-permute-start | bytes 1572872 | tf_op jit(solution)/shard_map/ppermute | solution.py:438
  5.7 0.8 %copy.11.partners = s32[4,8,4]{2,1,0:T(8,128)S(1)} copy(s32[4,8,4]{1,2,0:T(4,128)} %param.6) | data formatting | bytes 1024 | tf_op args[2]
  6.5 0.1 pad_add_fusion.place
  6.6 0.0 copy-start
  6.6 0.7 copy-done
  7.3 1.1 %plan.1 = (s32[8,128]{1,0:T(8,128)S(1)}, s32[8,128]{1,0:T(8,128)S(1)}, s32[8,128]{1,0:T(8,128)S(1)}, s32[8,128]{1,0:T(8,128)S(1)}, s32[1,128]{1,0:T(1,128)S(1)},...) custom-call(s32[4]{0:T(128)S(1)} %pad_add_fusion.place, s32[4,8,4]{2,1,0:T(8,128)S(1)} %copy.11.partners, s32[4,56]{1,0:T(4,128)S(1)} %copy-done), custom_call_target="tpu_custom_call" | custom-call | bytes 65536 | tf_op jit(solution)/shard_map/plan/pallas_call | solution.py:131
  8.3 1.6 %collective-permute-start = (s32[8,128]{1,0:T(8,128)S(1)}, s32[8,128]{1,0:T(8,128)S(1)}, u32[]{:S(2)}, u32[]{:S(2)}) collective-permute-start(s32[8,128]{1,0:T(8,128)S(1)} %get-tuple-element.31), channel_id=1, source_target_pairs={{0,32},{1,9},{2,34},{3,11},{4,36},{5,13},{6,38},{7,15},{8,40},{9,1... | collective-permute-start | bytes 12296 | tf_op jit(solution)/shard_map/ppermute | solution.py:442
  10.0 2.9 %collective-permute-start.1 = (s32[8,128]{1,0:T(8,128)S(1)}, s32[8,128]{1,0:T(8,128)S(1)}, u32[]{:S(2)}, u32[]{:S(2)}) collective-permute-start(s32[8,128]{1,0:T(8,128)S(1)} %get-tuple-element.32), channel_id=1, source_target_pairs={{0,64},{1,17},{2,66},{3,19},{4,68},{5,21},{6,70},{7,23},{8,72},{9,... | collective-permute-start | bytes 12296 | tf_op jit(solution)/shard_map/ppermute | solution.py:442
  12.9 0.7 collective-permute-done.req1.tab1
  13.6 1.5 %collective-permute-start.2 = (s32[8,128]{1,0:T(8,128)S(1)}, s32[8,128]{1,0:T(8,128)S(1)}, u32[]{:S(2)}, u32[]{:S(2)}) collective-permute-start(s32[8,128]{1,0:T(8,128)S(1)} %get-tuple-element.33), channel_id=1, source_target_pairs={{0,96},{1,25},{2,98},{3,27},{4,100},{5,29},{6,102},{7,31},{8,104},... | collective-permute-start | bytes 12296 | tf_op jit(solution)/shard_map/ppermute | solution.py:442
  15.1 6.6 %stage.1 = (bf16[4,8,64,32,128]{4,3,2,1,0:T(8,128)(2,1)S(1)}, bf16[64,32,128]{2,1,0:T(8,128)(2,1)S(1)}, f32[385,8,128]{2,1,0:T(8,128)S(1)}, bf16[2,4,256,256]{3,2,1,0:T(8,128)(2,1)S(1)}) custom-call(bf16[4,8,64,32,128]{4,3,2,1,0:T(8,128)(2,1)} %tensor.1, bf16[64,32,128]{2,1,0:T(8,128)(2,1)} %bitcast.11, s32[1,128]{1,0:T(1,128)S(1)} %get-tuple-element.34.picks, ...), custom_call_target="tpu_custom_call" | custom-call | bytes 18874368 | tf_op jit(solution)/shard_map/stage/pallas_call | solution.py:161
  21.7 0.0 collective-permute-done.1.req2.tab2
  21.7 0.0 collective-permute-done.2.req3.tab3
  21.8 0.0 collective-permute-done.5.got3
  21.8 0.0 collective-permute-done.4.got2
  21.8 0.0 collective-permute-done.3.got1
  21.8 1.2 %pack_early.1 = (bf16[32,32,128]{2,1,0:T(8,128)(2,1)S(1)}, bf16[32,32,128]{2,1,0:T(8,128)(2,1)S(1)}, bf16[32,32,128]{2,1,0:T(8,128)(2,1)S(1)}, bf16[256,32,128]{2,1,0:T(8,128)(2,1)S(1)}) custom-call(s32[8,128]{1,0:T(8,128)S(1)} %collective-permute-done.req1.tab1, s32[8,128]{1,0:T(8,128)S(1)} %collective-permute-done.1.req2.tab2, ...), custom_call_target="tpu_custom_call" | custom-call | bytes 4194304 | tf_op jit(solution)/shard_map/pack_early/pallas_call | solution.py:195
  23.0 2.7 %collective-permute-start.12 = (bf16[32,32,128]{2,1,0:T(8,128)(2,1)S(1)}, bf16[32,32,128]{2,1,0:T(8,128)(2,1)S(1)}, u32[]{:S(2)}, u32[]{:S(2)}) collective-permute-start(bf16[32,32,128]{2,1,0:T(8,128)(2,1)S(1)} %get-tuple-element.45), channel_id=1, source_target_pairs={{0,96},{1,25},{2,98},{3,27},{4,100},{5,29},{6,102},{7,31},{8,104},... | collective-permute-start | bytes 786440 | tf_op jit(solution)/shard_map/ppermute | solution.py:446
  25.6 0.0 collective-permute-start.13
  25.7 0.9 %collective-permute-start.14 = (bf16[32,32,128]{2,1,0:T(8,128)(2,1)S(1)}, bf16[32,32,128]{2,1,0:T(8,128)(2,1)S(1)}, u32[]{:S(2)}, u32[]{:S(2)}) collective-permute-start(bf16[32,32,128]{2,1,0:T(8,128)(2,1)S(1)} %get-tuple-element.47), channel_id=1, source_target_pairs={{0,32},{1,9},{2,34},{3,11},{4,36},{5,13},{6,38},{7,15},{8,40},{9,1... | collective-permute-start | bytes 786440 | tf_op jit(solution)/shard_map/ppermute | solution.py:446
  26.6 1.3 %pack_late.1 = (bf16[64,32,128]{2,1,0:T(8,128)(2,1)S(1)}, bf16[32,32,128]{2,1,0:T(8,128)(2,1)S(1)}, bf16[32,32,128]{2,1,0:T(8,128)(2,1)S(1)}, bf16[32,32,128]{2,1,0:T(8,128)(2,1)S(1)}, s32[4,8,128]{2,1,0:T(8,128)S(1)}) custom-call(s32[8,128]{1,0:T(8,128)S(1)} %get-tuple-element.30.req0.mine, s32[8,128]{1,0:T(8,128)S(1)} %collective-permute-done.req1.tab1, ...), custom_call_target="tpu_custom_call" | custom-call | bytes 2097152 | tf_op jit(solution)/shard_map/pack_late/pallas_call | solution.py:223
  27.9 2.4 %collective-permute-start.9 = (bf16[32,32,128]{2,1,0:T(8,128)(2,1)S(1)}, bf16[32,32,128]{2,1,0:T(8,128)(2,1)S(1)}, u32[]{:S(2)}, u32[]{:S(2)}) collective-permute-start(bf16[32,32,128]{2,1,0:T(8,128)(2,1)S(1)} %get-tuple-element.40), channel_id=1, source_target_pairs={{0,96},{1,25},{2,98},{3,27},{4,100},{5,29},{6,102},{7,31},{8,104},... | collective-permute-start | bytes 786440 | tf_op jit(solution)/shard_map/ppermute | solution.py:448
  30.3 2.3 %collective-permute-start.10 = (bf16[32,32,128]{2,1,0:T(8,128)(2,1)S(1)}, bf16[32,32,128]{2,1,0:T(8,128)(2,1)S(1)}, u32[]{:S(2)}, u32[]{:S(2)}) collective-permute-start(bf16[32,32,128]{2,1,0:T(8,128)(2,1)S(1)} %get-tuple-element.41), channel_id=1, source_target_pairs={{0,64},{1,17},{2,66},{3,19},{4,68},{5,21},{6,70},{7,23},{8,72},{9,... | collective-permute-start | bytes 786440 | tf_op jit(solution)/shard_map/ppermute | solution.py:448
  32.6 0.0 collective-permute-done.12.row1
  32.6 0.0 collective-permute-start.11
  32.6 1.0 %collective-permute-done.13.row2 = bf16[32,32,128]{2,1,0:T(8,128)(2,1)S(1)} collective-permute-done((bf16[32,32,128]{2,1,0:T(8,128)(2,1)S(1)}, bf16[32,32,128]{2,1,0:T(8,128)(2,1)S(1)}, u32[]{:S(2)}, u32[]{:S(2)}) %collective-permute-start.13) | collective-permute-done | bytes 262176 | tf_op jit(solution)/shard_map/ppermute | solution.py:446
  33.6 2.4 %collective-permute-done.14.row3 = bf16[32,32,128]{2,1,0:T(8,128)(2,1)S(1)} collective-permute-done((bf16[32,32,128]{2,1,0:T(8,128)(2,1)S(1)}, bf16[32,32,128]{2,1,0:T(8,128)(2,1)S(1)}, u32[]{:S(2)}, u32[]{:S(2)}) %collective-permute-start.14) | collective-permute-done | bytes 262176 | tf_op jit(solution)/shard_map/ppermute | solution.py:446
  36.0 9.2 %early_products.1 = (f32[385,8,128]{2,1,0:T(8,128)S(1)}, bf16[2,4,256,256]{3,2,1,0:T(8,128)(2,1)S(1)}, bf16[256,32,128]{2,1,0:T(8,128)(2,1)S(1)}, f32[2,256,256]{2,1,0:T(8,128)S(1)}) custom-call(s32[1,128]{1,0:T(1,128)S(1)} %get-tuple-element.36.count, s32[1,128]{1,0:T(1,128)S(1)} %get-tuple-element.34.picks, ...), custom_call_target="tpu_custom_call", output_to_operand_aliasing={{0}: (8, {}), {1}: (9, {})} | custom-call | flops 4294967296 | bytes 8388608 | tf_op jit(solution)/shard_map/early_products/pallas_call | solution.py:344
  45.3 0.0 collective-permute-done.9.late1
  45.3 0.0 collective-permute-done.10.late2
  45.3 0.0 collective-permute-done.11.late3
  45.3 4.8 %late_products.1 = (f32[385,8,128]{2,1,0:T(8,128)S(1)}, bf16[2,4,256,256]{3,2,1,0:T(8,128)(2,1)S(1)}, bf16[256,32,128]{2,1,0:T(8,128)(2,1)S(1)}, f32[2,256,256]{2,1,0:T(8,128)S(1)}, bf16[3072,128]{1,0:T(8,128)(2,1)}) custom-call(s32[1,128]{1,0:T(1,128)S(1)} %get-tuple-element.36.count, ...), custom_call_target="tpu_custom_call", output_to_operand_aliasing={{0}: (7, {}), {1}: (8, {}), {2}: (9, {}), {3}: (10, {})} | custom-call | flops 4294967296 | bytes 8388608 | tf_op jit(solution)/shard_map/late_products/pallas_call | solution.py:358
  50.1 9.4 %all-to-all-start = ((bf16[128,24,128]{2,1,0:T(8,128)(2,1)}), bf16[128,24,128]{2,1,0:T(8,128)(2,1)S(1)}, u32[]{:S(2)}, u32[]{:S(2)}) async-start(bf16[128,24,128]{2,1,0:T(8,128)(2,1)} %bitcast.5), calls=%async_computation | async-start | bytes 1572864 | tf_op jit(solution)/shard_map/all_to_all | solution.py:453
  59.5 2.2 %collective-permute-start.8 = (s32[4,8,128]{2,1,0:T(8,128)S(1)}, s32[4,8,128]{2,1,0:T(8,128)S(1)}, u32[]{:S(2)}, u32[]{:S(2)}) collective-permute-start(s32[4,8,128]{2,1,0:T(8,128)S(1)} %get-tuple-element.39.tables0), channel_id=1, source_target_pairs={{0,24},{1,97},{2,26},{3,99},{4,28},{5,101},{6,30},{7,103},{8,0},{9... | collective-permute-start | bytes 49160 | tf_op jit(solution)/shard_map/ppermute | solution.py:449
  61.7 0.9 %collective-permute-start.7 = (s32[4,8,128]{2,1,0:T(8,128)S(1)}, s32[4,8,128]{2,1,0:T(8,128)S(1)}, u32[]{:S(2)}, u32[]{:S(2)}) collective-permute-start(s32[4,8,128]{2,1,0:T(8,128)S(1)} %get-tuple-element.39.tables0), channel_id=1, source_target_pairs={{0,16},{1,65},{2,18},{3,67},{4,20},{5,69},{6,22},{7,71},{8,24},{9,... | collective-permute-start | bytes 49160 | tf_op jit(solution)/shard_map/ppermute | solution.py:449
  62.6 0.9 %collective-permute-start.6 = (s32[4,8,128]{2,1,0:T(8,128)S(1)}, s32[4,8,128]{2,1,0:T(8,128)S(1)}, u32[]{:S(2)}, u32[]{:S(2)}) collective-permute-start(s32[4,8,128]{2,1,0:T(8,128)S(1)} %get-tuple-element.39.tables0), channel_id=1, source_target_pairs={{0,8},{1,33},{2,10},{3,35},{4,12},{5,37},{6,14},{7,39},{8,16},{9,4... | collective-permute-start | bytes 49160 | tf_op jit(solution)/shard_map/ppermute | solution.py:449
  63.4 5.9 %collective-permute-done.8.tables3 = s32[4,8,128]{2,1,0:T(8,128)S(1)} collective-permute-done((s32[4,8,128]{2,1,0:T(8,128)S(1)}, s32[4,8,128]{2,1,0:T(8,128)S(1)}, u32[]{:S(2)}, u32[]{:S(2)}) %collective-permute-start.8) | collective-permute-done | bytes 16416 | tf_op jit(solution)/shard_map/ppermute | solution.py:449
  69.3 1.5 %collective-permute-done.7.tables2 = s32[4,8,128]{2,1,0:T(8,128)S(1)} collective-permute-done((s32[4,8,128]{2,1,0:T(8,128)S(1)}, s32[4,8,128]{2,1,0:T(8,128)S(1)}, u32[]{:S(2)}, u32[]{:S(2)}) %collective-permute-start.7) | collective-permute-done | bytes 16416 | tf_op jit(solution)/shard_map/ppermute | solution.py:449
  70.9 0.0 collective-permute-done.6.tables1
  70.9 1.0 %locate.1.where = s32[16,128]{1,0:T(8,128)S(1)} custom-call(s32[4]{0:T(128)S(1)} %pad_add_fusion.place, s32[4,8,128]{2,1,0:T(8,128)S(1)} %get-tuple-element.39.tables0, s32[4,8,128]{2,1,0:T(8,128)S(1)} %collective-permute-done.6.tables1, s32[4,8,128]{2,1,0:T(8,128)S(1)} %collective-permute-done.7.tables2, s32[4,8,128]{2,1,0:T(8,128)S(1)} %collective-permute-done.8.tables3), custom_call_target="tpu_custom_call" | custom-call | bytes 65536 | tf_op jit(solution)/shard_map/locate/pallas_call | solution.py:391
  71.9 4.1 %all-to-all-done = bf16[128,24,128]{2,1,0:T(8,128)(2,1)S(1)} async-done(((bf16[128,24,128]{2,1,0:T(8,128)(2,1)}), bf16[128,24,128]{2,1,0:T(8,128)(2,1)S(1)}, u32[]{:S(2)}, u32[]{:S(2)}) %all-to-all-start) | async-done | bytes 786464 | tf_op jit(solution)/shard_map/all_to_all | solution.py:453
  76.0 1.7 %collect.1 = f32[16,1024]{1,0:T(8,128)} custom-call(s32[4]{0:T(128)S(1)} %pad_add_fusion.place, s32[16,128]{1,0:T(8,128)S(1)} %locate.1.where, bf16[3072,128]{1,0:T(8,128)(2,1)S(1)} %bitcast.7), custom_call_target="tpu_custom_call" | custom-call | tf_op jit(solution)/shard_map/collect/pallas_call | solution.py:420
Async XLA Ops:
  0.0 21.8 %collective-permute-start.5 = (bf16[64,32,128]{2,1,0:T(8,128)(2,1)}, bf16[64,32,128]{2,1,0:T(8,128)(2,1)S(1)}, u32[]{:S(2)}, u32[]{:S(2)}) collective-permute-start(bf16[64,32,128]{2,1,0:T(8,128)(2,1)} %bitcast.8), channel_id=1, source_target_pairs={{0,8},{1,33},{2,10},{3,35},{4,12},{5,37},{6,14},{7,39},{8,16},{9,4... | collective-permute-start | bytes 1572872 | tf_op jit(solution)/shard_map/ppermute | solution.py:438
  1.6 20.2 %collective-permute-start.4 = (bf16[64,32,128]{2,1,0:T(8,128)(2,1)}, bf16[64,32,128]{2,1,0:T(8,128)(2,1)S(1)}, u32[]{:S(2)}, u32[]{:S(2)}) collective-permute-start(bf16[64,32,128]{2,1,0:T(8,128)(2,1)} %bitcast.9), channel_id=1, source_target_pairs={{0,16},{1,65},{2,18},{3,67},{4,20},{5,69},{6,22},{7,71},{8,24},{9,... | collective-permute-start | bytes 1572872 | tf_op jit(solution)/shard_map/ppermute | solution.py:438
  4.3 17.5 %collective-permute-start.3 = (bf16[64,32,128]{2,1,0:T(8,128)(2,1)}, bf16[64,32,128]{2,1,0:T(8,128)(2,1)S(1)}, u32[]{:S(2)}, u32[]{:S(2)}) collective-permute-start(bf16[64,32,128]{2,1,0:T(8,128)(2,1)} %bitcast.10), channel_id=1, source_target_pairs={{0,24},{1,97},{2,26},{3,99},{4,28},{5,101},{6,30},{7,103},{8,0},{9... | collective-permute-start | bytes 1572872 | tf_op jit(solution)/shard_map/ppermute | solution.py:438
  6.6 0.7 copy-start
  8.3 5.3 %collective-permute-start = (s32[8,128]{1,0:T(8,128)S(1)}, s32[8,128]{1,0:T(8,128)S(1)}, u32[]{:S(2)}, u32[]{:S(2)}) collective-permute-start(s32[8,128]{1,0:T(8,128)S(1)} %get-tuple-element.31), channel_id=1, source_target_pairs={{0,32},{1,9},{2,34},{3,11},{4,36},{5,13},{6,38},{7,15},{8,40},{9,1... | collective-permute-start | bytes 12296 | tf_op jit(solution)/shard_map/ppermute | solution.py:442
  10.0 11.7 %collective-permute-start.1 = (s32[8,128]{1,0:T(8,128)S(1)}, s32[8,128]{1,0:T(8,128)S(1)}, u32[]{:S(2)}, u32[]{:S(2)}) collective-permute-start(s32[8,128]{1,0:T(8,128)S(1)} %get-tuple-element.32), channel_id=1, source_target_pairs={{0,64},{1,17},{2,66},{3,19},{4,68},{5,21},{6,70},{7,23},{8,72},{9,... | collective-permute-start | bytes 12296 | tf_op jit(solution)/shard_map/ppermute | solution.py:442
  13.6 8.1 %collective-permute-start.2 = (s32[8,128]{1,0:T(8,128)S(1)}, s32[8,128]{1,0:T(8,128)S(1)}, u32[]{:S(2)}, u32[]{:S(2)}) collective-permute-start(s32[8,128]{1,0:T(8,128)S(1)} %get-tuple-element.33), channel_id=1, source_target_pairs={{0,96},{1,25},{2,98},{3,27},{4,100},{5,29},{6,102},{7,31},{8,104},... | collective-permute-start | bytes 12296 | tf_op jit(solution)/shard_map/ppermute | solution.py:442
  23.0 9.6 %collective-permute-start.12 = (bf16[32,32,128]{2,1,0:T(8,128)(2,1)S(1)}, bf16[32,32,128]{2,1,0:T(8,128)(2,1)S(1)}, u32[]{:S(2)}, u32[]{:S(2)}) collective-permute-start(bf16[32,32,128]{2,1,0:T(8,128)(2,1)S(1)} %get-tuple-element.45), channel_id=1, source_target_pairs={{0,96},{1,25},{2,98},{3,27},{4,100},{5,29},{6,102},{7,31},{8,104},... | collective-permute-start | bytes 786440 | tf_op jit(solution)/shard_map/ppermute | solution.py:446
  25.6 8.0 %collective-permute-start.13 = (bf16[32,32,128]{2,1,0:T(8,128)(2,1)S(1)}, bf16[32,32,128]{2,1,0:T(8,128)(2,1)S(1)}, u32[]{:S(2)}, u32[]{:S(2)}) collective-permute-start(bf16[32,32,128]{2,1,0:T(8,128)(2,1)S(1)} %get-tuple-element.46), channel_id=1, source_target_pairs={{0,64},{1,17},{2,66},{3,19},{4,68},{5,21},{6,70},{7,23},{8,72},{9,... | collective-permute-start | bytes 786440 | tf_op jit(solution)/shard_map/ppermute | solution.py:446
  25.7 10.4 %collective-permute-start.14 = (bf16[32,32,128]{2,1,0:T(8,128)(2,1)S(1)}, bf16[32,32,128]{2,1,0:T(8,128)(2,1)S(1)}, u32[]{:S(2)}, u32[]{:S(2)}) collective-permute-start(bf16[32,32,128]{2,1,0:T(8,128)(2,1)S(1)} %get-tuple-element.47), channel_id=1, source_target_pairs={{0,32},{1,9},{2,34},{3,11},{4,36},{5,13},{6,38},{7,15},{8,40},{9,1... | collective-permute-start | bytes 786440 | tf_op jit(solution)/shard_map/ppermute | solution.py:446
  27.9 17.4 %collective-permute-start.9 = (bf16[32,32,128]{2,1,0:T(8,128)(2,1)S(1)}, bf16[32,32,128]{2,1,0:T(8,128)(2,1)S(1)}, u32[]{:S(2)}, u32[]{:S(2)}) collective-permute-start(bf16[32,32,128]{2,1,0:T(8,128)(2,1)S(1)} %get-tuple-element.40), channel_id=1, source_target_pairs={{0,96},{1,25},{2,98},{3,27},{4,100},{5,29},{6,102},{7,31},{8,104},... | collective-permute-start | bytes 786440 | tf_op jit(solution)/shard_map/ppermute | solution.py:448
  30.3 15.0 %collective-permute-start.10 = (bf16[32,32,128]{2,1,0:T(8,128)(2,1)S(1)}, bf16[32,32,128]{2,1,0:T(8,128)(2,1)S(1)}, u32[]{:S(2)}, u32[]{:S(2)}) collective-permute-start(bf16[32,32,128]{2,1,0:T(8,128)(2,1)S(1)} %get-tuple-element.41), channel_id=1, source_target_pairs={{0,64},{1,17},{2,66},{3,19},{4,68},{5,21},{6,70},{7,23},{8,72},{9,... | collective-permute-start | bytes 786440 | tf_op jit(solution)/shard_map/ppermute | solution.py:448
  32.6 12.7 %collective-permute-start.11 = (bf16[32,32,128]{2,1,0:T(8,128)(2,1)S(1)}, bf16[32,32,128]{2,1,0:T(8,128)(2,1)S(1)}, u32[]{:S(2)}, u32[]{:S(2)}) collective-permute-start(bf16[32,32,128]{2,1,0:T(8,128)(2,1)S(1)} %get-tuple-element.42), channel_id=1, source_target_pairs={{0,32},{1,9},{2,34},{3,11},{4,36},{5,13},{6,38},{7,15},{8,40},{9,1... | collective-permute-start | bytes 786440 | tf_op jit(solution)/shard_map/ppermute | solution.py:448
  50.1 25.9 %all-to-all-start = ((bf16[128,24,128]{2,1,0:T(8,128)(2,1)}), bf16[128,24,128]{2,1,0:T(8,128)(2,1)S(1)}, u32[]{:S(2)}, u32[]{:S(2)}) async-start(bf16[128,24,128]{2,1,0:T(8,128)(2,1)} %bitcast.5), calls=%async_computation | async-start | bytes 1572864 | tf_op jit(solution)/shard_map/all_to_all | solution.py:453
  59.5 9.9 %collective-permute-start.8 = (s32[4,8,128]{2,1,0:T(8,128)S(1)}, s32[4,8,128]{2,1,0:T(8,128)S(1)}, u32[]{:S(2)}, u32[]{:S(2)}) collective-permute-start(s32[4,8,128]{2,1,0:T(8,128)S(1)} %get-tuple-element.39.tables0), channel_id=1, source_target_pairs={{0,24},{1,97},{2,26},{3,99},{4,28},{5,101},{6,30},{7,103},{8,0},{9... | collective-permute-start | bytes 49160 | tf_op jit(solution)/shard_map/ppermute | solution.py:449
  61.7 9.2 %collective-permute-start.7 = (s32[4,8,128]{2,1,0:T(8,128)S(1)}, s32[4,8,128]{2,1,0:T(8,128)S(1)}, u32[]{:S(2)}, u32[]{:S(2)}) collective-permute-start(s32[4,8,128]{2,1,0:T(8,128)S(1)} %get-tuple-element.39.tables0), channel_id=1, source_target_pairs={{0,16},{1,65},{2,18},{3,67},{4,20},{5,69},{6,22},{7,71},{8,24},{9,... | collective-permute-start | bytes 49160 | tf_op jit(solution)/shard_map/ppermute | solution.py:449
  62.6 8.3 %collective-permute-start.6 = (s32[4,8,128]{2,1,0:T(8,128)S(1)}, s32[4,8,128]{2,1,0:T(8,128)S(1)}, u32[]{:S(2)}, u32[]{:S(2)}) collective-permute-start(s32[4,8,128]{2,1,0:T(8,128)S(1)} %get-tuple-element.39.tables0), channel_id=1, source_target_pairs={{0,8},{1,33},{2,10},{3,35},{4,12},{5,37},{6,14},{7,39},{8,16},{9,4... | collective-permute-start | bytes 49160 | tf_op jit(solution)/shard_map/ppermute | solution.py:449

commit v3 on v2

--- a/solution.py
+++ b/solution.py
@@ -143,11 +143,11 @@
 PAIRS = (2, MS // 2, 2 * OCC, 2 * OCC)
 
 
-def stage_kernel(tensor, own, picks, slots, count, tensor_out, own_out, staged, pairs, sems):
+def stage_kernel(tensor, own, picks, slots, count, held, own_out, staged, pairs, sems):
     del picks, slots, count
     copies = [
         pltpu.make_async_copy(own, own_out, sems.at[0]),
-        pltpu.make_async_copy(tensor, tensor_out, sems.at[1]),
+        pltpu.make_async_copy(tensor.at[0], held.at[0], sems.at[1]),
     ]
     for copy in copies:
         copy.start()
@@ -170,7 +170,7 @@
         out_specs=[VMEM] * 4,
         scratch_shapes=[pltpu.SemaphoreType.DMA((2,))],
         compiler_params=pltpu.CompilerParams(vmem_limit_bytes=MIB),
-        cost_estimate=cost(0, 18 * MIB),
+        cost_estimate=cost(0, 5 * MIB),
         name="stage",
     )(in_hbm(tensor), in_hbm(own), *lists)
 
@@ -224,7 +224,9 @@
         pack_late_kernel,
         out_shape=[block_array(ROW_CAP)]
         + [block_array(LATE)] * 3
-        + [pltpu.VMEM((SIDE, ROWS, LANES), jnp.int32)],
+        + [
+            pltpu.VMEM((SIDE, ROWS, LANES), jnp.int32),
+        ],
         in_specs=[SMEM] * 4 + [VMEM] * 5,
         out_specs=[VMEM] * 5,
         compiler_params=pltpu.CompilerParams(vmem_limit_bytes=2 * MIB),
@@ -233,7 +235,7 @@
     )(mine, *received, shards, mine, *received)
 
 
-def run_blocks(low, high, picks, slots, tensor, staged, pairs, blocks, total, half):
+def run_blocks(low, high, picks, slots, tensor, staged, pairs, blocks, total, half, ready):
     def fill(p):
         for s in range(MS):
             side = (s % 2) * OCC
@@ -277,6 +279,7 @@
 
     @pl.loop(low, high)
     def _(p):
+        ready(p)
         first(p, 0)
         for c in range(last):
             if c + 1 < last:
@@ -307,24 +310,43 @@
 
 
 def early_kernel(
-    count, picks, slots, row0, row1, row2, row3, tensor, staged0, pairs0,
-    staged, pairs, blocks, total, half,
+    count, picks, slots, row0, row1, row2, row3, tensor, staged0, pairs0, held0,
+    staged, pairs, held, blocks, total, half, sems,
 ):
-    del staged0, pairs0
+    del staged0, pairs0, held0
+
+    def rest(p):
+        return pltpu.make_async_copy(tensor.at[p], held.at[p], sems.at[p])
+
+    for p in range(1, AUX_DEV):
+        rest(p).start()
     blocks[pl.ds(0, ROW_CAP)] = row0[...]
     for at, src in enumerate((row1, row2, row3)):
         blocks[pl.ds(ROW_CAP + at * EARLY, EARLY)] = src[...]
-    run_blocks(0, count[0, 0], picks, slots, tensor, staged, pairs, blocks, total, half)
+
+    def ready(p):
+        @pl.when(p > 0)
+        def _():
+            rest(p).wait()
+
+    run_blocks(0, count[0, 0], picks, slots, held, staged, pairs, blocks, total, half, ready)
+    for p in range(1, AUX_DEV):
+
+        @pl.when(p >= count[0, 0])
+        def _():
+            rest(p).wait()
 
 
 def late_kernel(
-    count, picks, slots, late1, late2, late3, tensor, staged0, pairs0, blocks0, total0,
-    staged, pairs, blocks, total, out, half,
+    count, picks, slots, late1, late2, late3, staged0, pairs0, held0, blocks0, total0,
+    staged, pairs, held, blocks, total, out, half,
 ):
-    del staged0, pairs0, blocks0, total0
+    del staged0, pairs0, held0, blocks0, total0
     for at, src in enumerate((late1, late2, late3)):
         blocks[pl.ds(SOON + at * LATE, LATE)] = src[...]
-    run_blocks(count[0, 0], AUX_DEV, picks, slots, tensor, staged, pairs, blocks, total, half)
+    run_blocks(
+        count[0, 0], AUX_DEV, picks, slots, held, staged, pairs, blocks, total, half, lambda p: None
+    )
     put(AUX_DEV - 1, True, slots, total, staged)
     done = staged[pl.ds(0, DEVS * CAP)]
     out[...] = done.reshape(DEVS * CAP * ROWS, LANES).astype(jnp.bfloat16)
@@ -333,6 +355,7 @@
 STATE = [
     pltpu.VMEM(STAGED, jnp.float32),
     pltpu.VMEM(PAIRS, jnp.bfloat16),
+    pltpu.VMEM((AUX_DEV, MS, PA, BS, OCC), jnp.bfloat16),
     pltpu.VMEM((BLOCKS, BS, OCC), jnp.bfloat16),
     pltpu.VMEM((2, MS * BS, MS * BS), jnp.float32),
 ]
@@ -340,32 +363,32 @@
 FLOPS = 2 * (MS * PA * BS * OCC * OCC * 4 + 2 * PA * OCC * (MS * BS) ** 2)
 
 
-def early_products(count, picks, slots, rows, tensor, staged, pairs):
+def early_products(count, picks, slots, rows, tensor, staged, pairs, held):
     return pl.pallas_call(
         early_kernel,
         out_shape=STATE,
-        in_specs=[SMEM] * 3 + [VMEM] * 7,
-        out_specs=[VMEM] * 4,
-        input_output_aliases={8: 0, 9: 1},
-        scratch_shapes=[HALF],
+        in_specs=[SMEM] * 3 + [VMEM] * 4 + [HBM] + [VMEM] * 3,
+        out_specs=[VMEM] * 5,
+        input_output_aliases={8: 0, 9: 1, 10: 2},
+        scratch_shapes=[HALF, pltpu.SemaphoreType.DMA((AUX_DEV,))],
         compiler_params=pltpu.CompilerParams(vmem_limit_bytes=8 * MIB),
         cost_estimate=cost(FLOPS, 8 * MIB),
         name="early_products",
-    )(count, picks, slots, *[in_vmem(r) for r in rows], tensor, staged, pairs)
-
-
-def late_products(count, picks, slots, late, tensor, state):
+    )(count, picks, slots, *[in_vmem(r) for r in rows], in_hbm(tensor), staged, pairs, held)
+
+
+def late_products(count, picks, slots, late, state):
     return pl.pallas_call(
         late_kernel,
         out_shape=STATE + [jax.ShapeDtypeStruct((DEVS * CAP * ROWS, LANES), jnp.bfloat16)],
         in_specs=[SMEM] * 3 + [VMEM] * 8,
-        out_specs=[VMEM] * 5,
-        input_output_aliases={7: 0, 8: 1, 9: 2, 10: 3},
+        out_specs=[VMEM] * 6,
+        input_output_aliases={6: 0, 7: 1, 8: 2, 9: 3, 10: 4},
         scratch_shapes=[HALF],
         compiler_params=pltpu.CompilerParams(vmem_limit_bytes=8 * MIB),
         cost_estimate=cost(FLOPS, 8 * MIB),
         name="late_products",
-    )(count, picks, slots, *[in_vmem(r) for r in late], tensor, *state)[4]
+    )(count, picks, slots, *[in_vmem(r) for r in late], *state)[5]
 
 
 def locate_kernel(place, tables0, tables1, tables2, tables3, where):
@@ -441,15 +464,17 @@
     mine, *sent, picks, slots, count = plan(place, partners, pair_owner)
     received = [lax.ppermute(sent[j - 1], AXES, shifted(j, False)) for j in (1, 2, 3)]
 
-    tensor, own, staged, pairs = stage(three_center, own, picks, slots, count)
-    *early, shards = pack_early(received, own, got)
+    held, here, staged, pairs = stage(three_center, own, picks, slots, count)
+    *early, shards = pack_early(received, here, got)
     early = [lax.ppermute(early[j - 1], AXES, shifted(-j, False)) for j in (1, 2, 3)]
     row0, *late, tables = pack_late(mine, received, shards)
     late = [lax.ppermute(late[j - 1], AXES, shifted(-j, False)) for j in (1, 2, 3)]
     every = [tables] + [lax.ppermute(tables, AXES, shifted(j, True)) for j in (1, 2, 3)]
 
-    state = early_products(count, picks, slots, (row0, *early), tensor, staged, pairs)
-    outgoing = late_products(count, picks, slots, late, tensor, state)
+    state = early_products(
+        count, picks, slots, (row0, *early), three_center, staged, pairs, held
+    )
+    outgoing = late_products(count, picks, slots, late, state)
     incoming = lax.all_to_all(outgoing, AXES, split_axis=0, concat_axis=0, tiled=True)
 
     return collect(place, locate(place, every), incoming)

time: 78.1 us -> 74.5 us (0.954)
  Pallas kernels: 26.8 us -> 23.2 us
    pallas_call x1, Pallas kernels: 6.58 us -> 2.98 us  [stage(): pl.pallas_call(stage_kernel, out_shape=[pltpu.VMEM(tensor.shape, tensor.d...]
  transfers between devices with their start and end apart: 16 -> 16, of which waited for: 6 -> 6; matrix products, arithmetic and copies ran while one was open for 1% -> 1% of each run, Pallas kernels for 25% -> 21%
where the time goes in v3:
time: 74.5 us; the launch traced here: 74 us
  starting transfers between devices  33.2 us (45%)
  Pallas kernels  23.2 us (31%)
  waiting for transfers between devices  15.9 us (21%)
  local copies, waits for them, and re-layouts  1.47 us (2%)
    pallas_call x1, Pallas kernels, early_products(): pl.pallas_call(early_kernel, out_shape=STATE, in_specs=[SMEM] * 3 + [VMEM...  9.2 us
    all_to_all x1, starting transfers between devices, body(): lax.all_to_all(outgoing, AXES, split_axis=0, concat_axis=0, tiled=True)  9.16 us
    ppermute x3, waiting for transfers between devices, body(): lax.ppermute(tables, AXES, shifted(j, True))  7.45 us
    ppermute x3, starting transfers between devices, body(): lax.ppermute(sent[j - 1], AXES, shifted(j, False))  6.05 us
    ppermute x3, starting transfers between devices, body(): got = [lax.ppermute(own, AXES, shifted(-j, True)) for j in (1, 2, 3)]  5.74 us
    pallas_call x1, Pallas kernels, late_products(): pl.pallas_call(late_kernel, out_shape=STATE + [jax.ShapeDtypeStruct((DEVS...  4.77 us
    ppermute x3, starting transfers between devices, body(): lax.ppermute(late[j - 1], AXES, shifted(-j, False))  4.19 us
    ppermute x3, starting transfers between devices, body(): lax.ppermute(early[j - 1], AXES, shifted(-j, False))  4.12 us
  transfers between devices with their start and end apart: 16, of which 6 were waited for; matrix products, arithmetic and copies ran while one was open for 1% of the time, Pallas kernels for 21%

profile of v3, /device:TPU:0, one launch (start us, length us, event | category | flops | bytes accessed | tf_op | source)
XLA Modules:
  0.0 74.0 jit_solution(6157460161061812530)
XLA Ops:
  0.0 1.6 %collective-permute-start.5 = (bf16[64,32,128]{2,1,0:T(8,128)(2,1)}, bf16[64,32,128]{2,1,0:T(8,128)(2,1)S(1)}, u32[]{:S(2)}, u32[]{:S(2)}) collective-permute-start(bf16[64,32,128]{2,1,0:T(8,128)(2,1)} %bitcast.8), channel_id=1, source_target_pairs={{0,8},{1,33},{2,10},{3,35},{4,12},{5,37},{6,14},{7,39},{8,16},{9,4... | collective-permute-start | bytes 1572872 | tf_op jit(solution)/shard_map/ppermute | solution.py:461
  1.6 2.7 %collective-permute-start.4 = (bf16[64,32,128]{2,1,0:T(8,128)(2,1)}, bf16[64,32,128]{2,1,0:T(8,128)(2,1)S(1)}, u32[]{:S(2)}, u32[]{:S(2)}) collective-permute-start(bf16[64,32,128]{2,1,0:T(8,128)(2,1)} %bitcast.9), channel_id=1, source_target_pairs={{0,16},{1,65},{2,18},{3,67},{4,20},{5,69},{6,22},{7,71},{8,24},{9,... | collective-permute-start | bytes 1572872 | tf_op jit(solution)/shard_map/ppermute | solution.py:461
  4.3 1.4 %collective-permute-start.3 = (bf16[64,32,128]{2,1,0:T(8,128)(2,1)}, bf16[64,32,128]{2,1,0:T(8,128)(2,1)S(1)}, u32[]{:S(2)}, u32[]{:S(2)}) collective-permute-start(bf16[64,32,128]{2,1,0:T(8,128)(2,1)} %bitcast.10), channel_id=1, source_target_pairs={{0,24},{1,97},{2,26},{3,99},{4,28},{5,101},{6,30},{7,103},{8,0},{9... | collective-permute-start | bytes 1572872 | tf_op jit(solution)/shard_map/ppermute | solution.py:461
  5.7 0.8 %copy.13.partners = s32[4,8,4]{2,1,0:T(8,128)S(1)} copy(s32[4,8,4]{1,2,0:T(4,128)} %param.6) | data formatting | bytes 1024 | tf_op args[2]
  6.5 0.1 pad_add_fusion.place
  6.6 0.0 copy-start
  6.6 0.7 copy-done
  7.3 1.1 %plan.1 = (s32[8,128]{1,0:T(8,128)S(1)}, s32[8,128]{1,0:T(8,128)S(1)}, s32[8,128]{1,0:T(8,128)S(1)}, s32[8,128]{1,0:T(8,128)S(1)}, s32[1,128]{1,0:T(1,128)S(1)},...) custom-call(s32[4]{0:T(128)S(1)} %pad_add_fusion.place, s32[4,8,4]{2,1,0:T(8,128)S(1)} %copy.13.partners, s32[4,56]{1,0:T(4,128)S(1)} %copy-done), custom_call_target="tpu_custom_call" | custom-call | bytes 65536 | tf_op jit(solution)/shard_map/plan/pallas_call | solution.py:131
  8.3 1.6 %collective-permute-start = (s32[8,128]{1,0:T(8,128)S(1)}, s32[8,128]{1,0:T(8,128)S(1)}, u32[]{:S(2)}, u32[]{:S(2)}) collective-permute-start(s32[8,128]{1,0:T(8,128)S(1)} %get-tuple-element.32), channel_id=1, source_target_pairs={{0,32},{1,9},{2,34},{3,11},{4,36},{5,13},{6,38},{7,15},{8,40},{9,1... | collective-permute-start | bytes 12296 | tf_op jit(solution)/shard_map/ppermute | solution.py:465
  10.0 2.9 %collective-permute-start.1 = (s32[8,128]{1,0:T(8,128)S(1)}, s32[8,128]{1,0:T(8,128)S(1)}, u32[]{:S(2)}, u32[]{:S(2)}) collective-permute-start(s32[8,128]{1,0:T(8,128)S(1)} %get-tuple-element.33), channel_id=1, source_target_pairs={{0,64},{1,17},{2,66},{3,19},{4,68},{5,21},{6,70},{7,23},{8,72},{9,... | collective-permute-start | bytes 12296 | tf_op jit(solution)/shard_map/ppermute | solution.py:465
  12.9 0.7 %collective-permute-done.req1.tab1 = s32[8,128]{1,0:T(8,128)S(1)} collective-permute-done((s32[8,128]{1,0:T(8,128)S(1)}, s32[8,128]{1,0:T(8,128)S(1)}, u32[]{:S(2)}, u32[]{:S(2)}) %collective-permute-start) | collective-permute-done | bytes 4128 | tf_op jit(solution)/shard_map/ppermute | solution.py:465
  13.6 1.5 %collective-permute-start.2 = (s32[8,128]{1,0:T(8,128)S(1)}, s32[8,128]{1,0:T(8,128)S(1)}, u32[]{:S(2)}, u32[]{:S(2)}) collective-permute-start(s32[8,128]{1,0:T(8,128)S(1)} %get-tuple-element.34), channel_id=1, source_target_pairs={{0,96},{1,25},{2,98},{3,27},{4,100},{5,29},{6,102},{7,31},{8,104},... | collective-permute-start | bytes 12296 | tf_op jit(solution)/shard_map/ppermute | solution.py:465
  15.1 3.0 %stage.1 = (bf16[4,8,64,32,128]{4,3,2,1,0:T(8,128)(2,1)S(1)}, bf16[64,32,128]{2,1,0:T(8,128)(2,1)S(1)}, f32[385,8,128]{2,1,0:T(8,128)S(1)}, bf16[2,4,256,256]{3,2,1,0:T(8,128)(2,1)S(1)}) custom-call(bf16[4,8,64,32,128]{4,3,2,1,0:T(8,128)(2,1)} %tensor.3, bf16[64,32,128]{2,1,0:T(8,128)(2,1)} %bitcast.11, s32[1,128]{1,0:T(1,128)S(1)} %get-tuple-element.35.picks, ...), custom_call_target="tpu_custom_call" | custom-call | bytes 5242880 | tf_op jit(solution)/shard_map/stage/pallas_call | solution.py:161
  18.1 0.0 collective-permute-done.1.req2.tab2
  18.1 0.0 collective-permute-done.2.req3.tab3
  18.2 0.0 collective-permute-done.5.got3
  18.2 0.0 collective-permute-done.4.got2
  18.2 0.0 collective-permute-done.3.got1
  18.2 1.2 %pack_early.1 = (bf16[32,32,128]{2,1,0:T(8,128)(2,1)S(1)}, bf16[32,32,128]{2,1,0:T(8,128)(2,1)S(1)}, bf16[32,32,128]{2,1,0:T(8,128)(2,1)S(1)}, bf16[256,32,128]{2,1,0:T(8,128)(2,1)S(1)}) custom-call(s32[8,128]{1,0:T(8,128)S(1)} %collective-permute-done.req1.tab1, s32[8,128]{1,0:T(8,128)S(1)} %collective-permute-done.1.req2.tab2, ...), custom_call_target="tpu_custom_call" | custom-call | bytes 4194304 | tf_op jit(solution)/shard_map/pack_early/pallas_call | solution.py:195
  19.4 2.7 %collective-permute-start.12 = (bf16[32,32,128]{2,1,0:T(8,128)(2,1)S(1)}, bf16[32,32,128]{2,1,0:T(8,128)(2,1)S(1)}, u32[]{:S(2)}, u32[]{:S(2)}) collective-permute-start(bf16[32,32,128]{2,1,0:T(8,128)(2,1)S(1)} %get-tuple-element.45), channel_id=1, source_target_pairs={{0,96},{1,25},{2,98},{3,27},{4,100},{5,29},{6,102},{7,31},{8,104},... | collective-permute-start | bytes 786440 | tf_op jit(solution)/shard_map/ppermute | solution.py:469
  22.1 0.2 collective-permute-start.13
  22.3 1.2 %collective-permute-start.14 = (bf16[32,32,128]{2,1,0:T(8,128)(2,1)S(1)}, bf16[32,32,128]{2,1,0:T(8,128)(2,1)S(1)}, u32[]{:S(2)}, u32[]{:S(2)}) collective-permute-start(bf16[32,32,128]{2,1,0:T(8,128)(2,1)S(1)} %get-tuple-element.47), channel_id=1, source_target_pairs={{0,32},{1,9},{2,34},{3,11},{4,36},{5,13},{6,38},{7,15},{8,40},{9,1... | collective-permute-start | bytes 786440 | tf_op jit(solution)/shard_map/ppermute | solution.py:469
  23.5 1.3 %pack_late.1 = (bf16[64,32,128]{2,1,0:T(8,128)(2,1)S(1)}, bf16[32,32,128]{2,1,0:T(8,128)(2,1)S(1)}, bf16[32,32,128]{2,1,0:T(8,128)(2,1)S(1)}, bf16[32,32,128]{2,1,0:T(8,128)(2,1)S(1)}, s32[4,8,128]{2,1,0:T(8,128)S(1)}) custom-call(s32[8,128]{1,0:T(8,128)S(1)} %get-tuple-element.31.req0.mine, s32[8,128]{1,0:T(8,128)S(1)} %collective-permute-done.req1.tab1, ...), custom_call_target="tpu_custom_call" | custom-call | bytes 2097152 | tf_op jit(solution)/shard_map/pack_late/pallas_call | solution.py:223
  24.8 2.1 %collective-permute-start.9 = (bf16[32,32,128]{2,1,0:T(8,128)(2,1)S(1)}, bf16[32,32,128]{2,1,0:T(8,128)(2,1)S(1)}, u32[]{:S(2)}, u32[]{:S(2)}) collective-permute-start(bf16[32,32,128]{2,1,0:T(8,128)(2,1)S(1)} %get-tuple-element.41), channel_id=1, source_target_pairs={{0,96},{1,25},{2,98},{3,27},{4,100},{5,29},{6,102},{7,31},{8,104},... | collective-permute-start | bytes 786440 | tf_op jit(solution)/shard_map/ppermute | solution.py:471
  26.9 2.1 %collective-permute-start.10 = (bf16[32,32,128]{2,1,0:T(8,128)(2,1)S(1)}, bf16[32,32,128]{2,1,0:T(8,128)(2,1)S(1)}, u32[]{:S(2)}, u32[]{:S(2)}) collective-permute-start(bf16[32,32,128]{2,1,0:T(8,128)(2,1)S(1)} %get-tuple-element.42), channel_id=1, source_target_pairs={{0,64},{1,17},{2,66},{3,19},{4,68},{5,21},{6,70},{7,23},{8,72},{9,... | collective-permute-start | bytes 786440 | tf_op jit(solution)/shard_map/ppermute | solution.py:471
  29.0 0.0 collective-permute-done.12.row1
  29.0 0.0 collective-permute-start.11
  29.0 1.0 %collective-permute-done.13.row2 = bf16[32,32,128]{2,1,0:T(8,128)(2,1)S(1)} collective-permute-done((bf16[32,32,128]{2,1,0:T(8,128)(2,1)S(1)}, bf16[32,32,128]{2,1,0:T(8,128)(2,1)S(1)}, u32[]{:S(2)}, u32[]{:S(2)}) %collective-permute-start.13) | collective-permute-done | bytes 262176 | tf_op jit(solution)/shard_map/ppermute | solution.py:469
  30.0 2.6 %collective-permute-done.14.row3 = bf16[32,32,128]{2,1,0:T(8,128)(2,1)S(1)} collective-permute-done((bf16[32,32,128]{2,1,0:T(8,128)(2,1)S(1)}, bf16[32,32,128]{2,1,0:T(8,128)(2,1)S(1)}, u32[]{:S(2)}, u32[]{:S(2)}) %collective-permute-start.14) | collective-permute-done | bytes 262176 | tf_op jit(solution)/shard_map/ppermute | solution.py:469
  32.7 9.2 %early_products.1 = (f32[385,8,128]{2,1,0:T(8,128)S(1)}, bf16[2,4,256,256]{3,2,1,0:T(8,128)(2,1)S(1)}, bf16[4,8,64,32,128]{4,3,2,1,0:T(8,128)(2,1)S(1)}, bf16[25...) custom-call(s32[1,128]{1,0:T(1,128)S(1)} %get-tuple-element.37.count, ...), custom_call_target="tpu_custom_call", output_to_operand_aliasing={{0}: (8, {}), {1}: (9, {}), {2}: (10, {})} | custom-call | flops 4294967296 | bytes 8388608 | tf_op jit(solution)/shard_map/early_products/pallas_call | solution.py:367
  41.9 0.0 collective-permute-done.9.late1
  41.9 0.0 collective-permute-done.10.late2
  41.9 0.0 collective-permute-done.11.late3
  41.9 4.8 %late_products.1 = (f32[385,8,128]{2,1,0:T(8,128)S(1)}, bf16[2,4,256,256]{3,2,1,0:T(8,128)(2,1)S(1)}, bf16[4,8,64,32,128]{4,3,2,1,0:T(8,128)(2,1)S(1)}, bf16[256...) custom-call(s32[1,128]{1,0:T(1,128)S(1)} %get-tuple-element.37.count, ...), custom_call_target="tpu_custom_call", output_to_operand_aliasing={{0}: (6, {}), {1}: (7, {}), {2}: (8, {}), {3}: (9, {}), {4}... | custom-call | flops 4294967296 | bytes 8388608 | tf_op jit(solution)/shard_map/late_products/pallas_call | solution.py:381
  46.7 9.2 %all-to-all-start = ((bf16[128,24,128]{2,1,0:T(8,128)(2,1)}), bf16[128,24,128]{2,1,0:T(8,128)(2,1)S(1)}, u32[]{:S(2)}, u32[]{:S(2)}) async-start(bf16[128,24,128]{2,1,0:T(8,128)(2,1)} %bitcast.5), calls=%async_computation | async-start | bytes 1572864 | tf_op jit(solution)/shard_map/all_to_all | solution.py:478
  55.8 2.2 %collective-permute-start.8 = (s32[4,8,128]{2,1,0:T(8,128)S(1)}, s32[4,8,128]{2,1,0:T(8,128)S(1)}, u32[]{:S(2)}, u32[]{:S(2)}) collective-permute-start(s32[4,8,128]{2,1,0:T(8,128)S(1)} %get-tuple-element.40.tables0), channel_id=1, source_target_pairs={{0,24},{1,97},{2,26},{3,99},{4,28},{5,101},{6,30},{7,103},{8,0},{9... | collective-permute-start | bytes 49160 | tf_op jit(solution)/shard_map/ppermute | solution.py:472
  58.1 0.9 %collective-permute-start.7 = (s32[4,8,128]{2,1,0:T(8,128)S(1)}, s32[4,8,128]{2,1,0:T(8,128)S(1)}, u32[]{:S(2)}, u32[]{:S(2)}) collective-permute-start(s32[4,8,128]{2,1,0:T(8,128)S(1)} %get-tuple-element.40.tables0), channel_id=1, source_target_pairs={{0,16},{1,65},{2,18},{3,67},{4,20},{5,69},{6,22},{7,71},{8,24},{9,... | collective-permute-start | bytes 49160 | tf_op jit(solution)/shard_map/ppermute | solution.py:472
  58.9 0.9 %collective-permute-start.6 = (s32[4,8,128]{2,1,0:T(8,128)S(1)}, s32[4,8,128]{2,1,0:T(8,128)S(1)}, u32[]{:S(2)}, u32[]{:S(2)}) collective-permute-start(s32[4,8,128]{2,1,0:T(8,128)S(1)} %get-tuple-element.40.tables0), channel_id=1, source_target_pairs={{0,8},{1,33},{2,10},{3,35},{4,12},{5,37},{6,14},{7,39},{8,16},{9,4... | collective-permute-start | bytes 49160 | tf_op jit(solution)/shard_map/ppermute | solution.py:472
  59.8 5.9 %collective-permute-done.8.tables3 = s32[4,8,128]{2,1,0:T(8,128)S(1)} collective-permute-done((s32[4,8,128]{2,1,0:T(8,128)S(1)}, s32[4,8,128]{2,1,0:T(8,128)S(1)}, u32[]{:S(2)}, u32[]{:S(2)}) %collective-permute-start.8) | collective-permute-done | bytes 16416 | tf_op jit(solution)/shard_map/ppermute | solution.py:472
  65.7 1.5 %collective-permute-done.7.tables2 = s32[4,8,128]{2,1,0:T(8,128)S(1)} collective-permute-done((s32[4,8,128]{2,1,0:T(8,128)S(1)}, s32[4,8,128]{2,1,0:T(8,128)S(1)}, u32[]{:S(2)}, u32[]{:S(2)}) %collective-permute-start.7) | collective-permute-done | bytes 16416 | tf_op jit(solution)/shard_map/ppermute | solution.py:472
  67.2 0.0 collective-permute-done.6.tables1
  67.2 1.0 %locate.1.where = s32[16,128]{1,0:T(8,128)S(1)} custom-call(s32[4]{0:T(128)S(1)} %pad_add_fusion.place, s32[4,8,128]{2,1,0:T(8,128)S(1)} %get-tuple-element.40.tables0, s32[4,8,128]{2,1,0:T(8,128)S(1)} %collective-permute-done.6.tables1, s32[4,8,128]{2,1,0:T(8,128)S(1)} %collective-permute-done.7.tables2, s32[4,8,128]{2,1,0:T(8,128)S(1)} %collective-permute-done.8.tables3), custom_call_target="tpu_custom_call" | custom-call | bytes 65536 | tf_op jit(solution)/shard_map/locate/pallas_call | solution.py:414
  68.3 4.1 %all-to-all-done = bf16[128,24,128]{2,1,0:T(8,128)(2,1)S(1)} async-done(((bf16[128,24,128]{2,1,0:T(8,128)(2,1)}), bf16[128,24,128]{2,1,0:T(8,128)(2,1)S(1)}, u32[]{:S(2)}, u32[]{:S(2)}) %all-to-all-start) | async-done | bytes 786464 | tf_op jit(solution)/shard_map/all_to_all | solution.py:478
  72.3 1.7 %collect.1 = f32[16,1024]{1,0:T(8,128)} custom-call(s32[4]{0:T(128)S(1)} %pad_add_fusion.place, s32[16,128]{1,0:T(8,128)S(1)} %locate.1.where, bf16[3072,128]{1,0:T(8,128)(2,1)S(1)} %bitcast.7), custom_call_target="tpu_custom_call" | custom-call | tf_op jit(solution)/shard_map/collect/pallas_call | solution.py:443
Async XLA Ops:
  0.0 18.2 %collective-permute-start.5 = (bf16[64,32,128]{2,1,0:T(8,128)(2,1)}, bf16[64,32,128]{2,1,0:T(8,128)(2,1)S(1)}, u32[]{:S(2)}, u32[]{:S(2)}) collective-permute-start(bf16[64,32,128]{2,1,0:T(8,128)(2,1)} %bitcast.8), channel_id=1, source_target_pairs={{0,8},{1,33},{2,10},{3,35},{4,12},{5,37},{6,14},{7,39},{8,16},{9,4... | collective-permute-start | bytes 1572872 | tf_op jit(solution)/shard_map/ppermute | solution.py:461
  1.6 16.6 %collective-permute-start.4 = (bf16[64,32,128]{2,1,0:T(8,128)(2,1)}, bf16[64,32,128]{2,1,0:T(8,128)(2,1)S(1)}, u32[]{:S(2)}, u32[]{:S(2)}) collective-permute-start(bf16[64,32,128]{2,1,0:T(8,128)(2,1)} %bitcast.9), channel_id=1, source_target_pairs={{0,16},{1,65},{2,18},{3,67},{4,20},{5,69},{6,22},{7,71},{8,24},{9,... | collective-permute-start | bytes 1572872 | tf_op jit(solution)/shard_map/ppermute | solution.py:461
  4.3 13.9 %collective-permute-start.3 = (bf16[64,32,128]{2,1,0:T(8,128)(2,1)}, bf16[64,32,128]{2,1,0:T(8,128)(2,1)S(1)}, u32[]{:S(2)}, u32[]{:S(2)}) collective-permute-start(bf16[64,32,128]{2,1,0:T(8,128)(2,1)} %bitcast.10), channel_id=1, source_target_pairs={{0,24},{1,97},{2,26},{3,99},{4,28},{5,101},{6,30},{7,103},{8,0},{9... | collective-permute-start | bytes 1572872 | tf_op jit(solution)/shard_map/ppermute | solution.py:461
  6.6 0.7 copy-start
  8.3 5.3 %collective-permute-start = (s32[8,128]{1,0:T(8,128)S(1)}, s32[8,128]{1,0:T(8,128)S(1)}, u32[]{:S(2)}, u32[]{:S(2)}) collective-permute-start(s32[8,128]{1,0:T(8,128)S(1)} %get-tuple-element.32), channel_id=1, source_target_pairs={{0,32},{1,9},{2,34},{3,11},{4,36},{5,13},{6,38},{7,15},{8,40},{9,1... | collective-permute-start | bytes 12296 | tf_op jit(solution)/shard_map/ppermute | solution.py:465
  10.0 8.1 %collective-permute-start.1 = (s32[8,128]{1,0:T(8,128)S(1)}, s32[8,128]{1,0:T(8,128)S(1)}, u32[]{:S(2)}, u32[]{:S(2)}) collective-permute-start(s32[8,128]{1,0:T(8,128)S(1)} %get-tuple-element.33), channel_id=1, source_target_pairs={{0,64},{1,17},{2,66},{3,19},{4,68},{5,21},{6,70},{7,23},{8,72},{9,... | collective-permute-start | bytes 12296 | tf_op jit(solution)/shard_map/ppermute | solution.py:465
  13.6 4.5 %collective-permute-start.2 = (s32[8,128]{1,0:T(8,128)S(1)}, s32[8,128]{1,0:T(8,128)S(1)}, u32[]{:S(2)}, u32[]{:S(2)}) collective-permute-start(s32[8,128]{1,0:T(8,128)S(1)} %get-tuple-element.34), channel_id=1, source_target_pairs={{0,96},{1,25},{2,98},{3,27},{4,100},{5,29},{6,102},{7,31},{8,104},... | collective-permute-start | bytes 12296 | tf_op jit(solution)/shard_map/ppermute | solution.py:465
  19.4 9.6 %collective-permute-start.12 = (bf16[32,32,128]{2,1,0:T(8,128)(2,1)S(1)}, bf16[32,32,128]{2,1,0:T(8,128)(2,1)S(1)}, u32[]{:S(2)}, u32[]{:S(2)}) collective-permute-start(bf16[32,32,128]{2,1,0:T(8,128)(2,1)S(1)} %get-tuple-element.45), channel_id=1, source_target_pairs={{0,96},{1,25},{2,98},{3,27},{4,100},{5,29},{6,102},{7,31},{8,104},... | collective-permute-start | bytes 786440 | tf_op jit(solution)/shard_map/ppermute | solution.py:469
  22.1 8.0 %collective-permute-start.13 = (bf16[32,32,128]{2,1,0:T(8,128)(2,1)S(1)}, bf16[32,32,128]{2,1,0:T(8,128)(2,1)S(1)}, u32[]{:S(2)}, u32[]{:S(2)}) collective-permute-start(bf16[32,32,128]{2,1,0:T(8,128)(2,1)S(1)} %get-tuple-element.46), channel_id=1, source_target_pairs={{0,64},{1,17},{2,66},{3,19},{4,68},{5,21},{6,70},{7,23},{8,72},{9,... | collective-permute-start | bytes 786440 | tf_op jit(solution)/shard_map/ppermute | solution.py:469
  22.3 10.4 %collective-permute-start.14 = (bf16[32,32,128]{2,1,0:T(8,128)(2,1)S(1)}, bf16[32,32,128]{2,1,0:T(8,128)(2,1)S(1)}, u32[]{:S(2)}, u32[]{:S(2)}) collective-permute-start(bf16[32,32,128]{2,1,0:T(8,128)(2,1)S(1)} %get-tuple-element.47), channel_id=1, source_target_pairs={{0,32},{1,9},{2,34},{3,11},{4,36},{5,13},{6,38},{7,15},{8,40},{9,1... | collective-permute-start | bytes 786440 | tf_op jit(solution)/shard_map/ppermute | solution.py:469
  24.8 17.1 %collective-permute-start.9 = (bf16[32,32,128]{2,1,0:T(8,128)(2,1)S(1)}, bf16[32,32,128]{2,1,0:T(8,128)(2,1)S(1)}, u32[]{:S(2)}, u32[]{:S(2)}) collective-permute-start(bf16[32,32,128]{2,1,0:T(8,128)(2,1)S(1)} %get-tuple-element.41), channel_id=1, source_target_pairs={{0,96},{1,25},{2,98},{3,27},{4,100},{5,29},{6,102},{7,31},{8,104},... | collective-permute-start | bytes 786440 | tf_op jit(solution)/shard_map/ppermute | solution.py:471
  26.9 15.0 %collective-permute-start.10 = (bf16[32,32,128]{2,1,0:T(8,128)(2,1)S(1)}, bf16[32,32,128]{2,1,0:T(8,128)(2,1)S(1)}, u32[]{:S(2)}, u32[]{:S(2)}) collective-permute-start(bf16[32,32,128]{2,1,0:T(8,128)(2,1)S(1)} %get-tuple-element.42), channel_id=1, source_target_pairs={{0,64},{1,17},{2,66},{3,19},{4,68},{5,21},{6,70},{7,23},{8,72},{9,... | collective-permute-start | bytes 786440 | tf_op jit(solution)/shard_map/ppermute | solution.py:471
  29.0 12.9 %collective-permute-start.11 = (bf16[32,32,128]{2,1,0:T(8,128)(2,1)S(1)}, bf16[32,32,128]{2,1,0:T(8,128)(2,1)S(1)}, u32[]{:S(2)}, u32[]{:S(2)}) collective-permute-start(bf16[32,32,128]{2,1,0:T(8,128)(2,1)S(1)} %get-tuple-element.43), channel_id=1, source_target_pairs={{0,32},{1,9},{2,34},{3,11},{4,36},{5,13},{6,38},{7,15},{8,40},{9,1... | collective-permute-start | bytes 786440 | tf_op jit(solution)/shard_map/ppermute | solution.py:471
  46.7 25.7 %all-to-all-start = ((bf16[128,24,128]{2,1,0:T(8,128)(2,1)}), bf16[128,24,128]{2,1,0:T(8,128)(2,1)S(1)}, u32[]{:S(2)}, u32[]{:S(2)}) async-start(bf16[128,24,128]{2,1,0:T(8,128)(2,1)} %bitcast.5), calls=%async_computation | async-start | bytes 1572864 | tf_op jit(solution)/shard_map/all_to_all | solution.py:478
  55.8 9.9 %collective-permute-start.8 = (s32[4,8,128]{2,1,0:T(8,128)S(1)}, s32[4,8,128]{2,1,0:T(8,128)S(1)}, u32[]{:S(2)}, u32[]{:S(2)}) collective-permute-start(s32[4,8,128]{2,1,0:T(8,128)S(1)} %get-tuple-element.40.tables0), channel_id=1, source_target_pairs={{0,24},{1,97},{2,26},{3,99},{4,28},{5,101},{6,30},{7,103},{8,0},{9... | collective-permute-start | bytes 49160 | tf_op jit(solution)/shard_map/ppermute | solution.py:472
  58.1 9.2 %collective-permute-start.7 = (s32[4,8,128]{2,1,0:T(8,128)S(1)}, s32[4,8,128]{2,1,0:T(8,128)S(1)}, u32[]{:S(2)}, u32[]{:S(2)}) collective-permute-start(s32[4,8,128]{2,1,0:T(8,128)S(1)} %get-tuple-element.40.tables0), channel_id=1, source_target_pairs={{0,16},{1,65},{2,18},{3,67},{4,20},{5,69},{6,22},{7,71},{8,24},{9,... | collective-permute-start | bytes 49160 | tf_op jit(solution)/shard_map/ppermute | solution.py:472
  58.9 8.3 %collective-permute-start.6 = (s32[4,8,128]{2,1,0:T(8,128)S(1)}, s32[4,8,128]{2,1,0:T(8,128)S(1)}, u32[]{:S(2)}, u32[]{:S(2)}) collective-permute-start(s32[4,8,128]{2,1,0:T(8,128)S(1)} %get-tuple-element.40.tables0), channel_id=1, source_target_pairs={{0,8},{1,33},{2,10},{3,35},{4,12},{5,37},{6,14},{7,39},{8,16},{9,4... | collective-permute-start | bytes 49160 | tf_op jit(solution)/shard_map/ppermute | solution.py:472

commit v4 on v3

--- a/solution.py
+++ b/solution.py
@@ -61,6 +61,7 @@
 HBM = pl.BlockSpec(memory_space=pltpu.HBM)
 MIB = 1024 * 1024
 LIST_ROW = AUX_DEV
+SIDE_SLOTS = DEVS * CAP // 2
 BLOCKS = ROW_CAP + 3 * ROW_CAP
 SOON = ROW_CAP + 3 * EARLY
 
@@ -121,7 +122,8 @@
         hits = ((column == row) & earlier).astype(jnp.int32)
         for before in stood:
             hits += (before == row).astype(jnp.int32)
-        slots[pl.ds(p, 1), :] = row * CAP + jnp.sum(hits, axis=0, keepdims=True)
+        at = (row & 1) * SIDE_SLOTS + (row >> 1) * CAP
+        slots[pl.ds(p, 1), :] = at + jnp.sum(hits, axis=0, keepdims=True)
         stood.append(column)
 
 
@@ -338,7 +340,7 @@
 
 
 def late_kernel(
-    count, picks, slots, late1, late2, late3, staged0, pairs0, held0, blocks0, total0,
+    place, count, picks, slots, late1, late2, late3, staged0, pairs0, held0, blocks0, total0,
     staged, pairs, held, blocks, total, out, half,
 ):
     del staged0, pairs0, held0, blocks0, total0
@@ -348,8 +350,25 @@
         count[0, 0], AUX_DEV, picks, slots, held, staged, pairs, blocks, total, half, lambda p: None
     )
     put(AUX_DEV - 1, True, slots, total, staged)
-    done = staged[pl.ds(0, DEVS * CAP)]
-    out[...] = done.reshape(DEVS * CAP * ROWS, LANES).astype(jnp.bfloat16)
+    done = staged[pl.ds(place[2] * SIDE_SLOTS, SIDE_SLOTS)]
+    out[...] = done.reshape(SIDE_SLOTS * ROWS, LANES).astype(jnp.bfloat16)
+
+
+def join_kernel(place, staged, came, out):
+    kept = staged[pl.ds((1 - place[2]) * SIDE_SLOTS, SIDE_SLOTS)].reshape(SIDE_SLOTS * ROWS, LANES)
+    out[...] = (kept + came[...].astype(jnp.float32)).astype(jnp.bfloat16)
+
+
+def join(place, staged, came):
+    return pl.pallas_call(
+        join_kernel,
+        out_shape=jax.ShapeDtypeStruct(came.shape, came.dtype),
+        in_specs=[SMEM] + [VMEM] * 2,
+        out_specs=VMEM,
+        compiler_params=pltpu.CompilerParams(vmem_limit_bytes=4 * MIB),
+        cost_estimate=cost(0, 2 * MIB),
+        name="join",
+    )(place, staged, in_vmem(came))
 
 
 STATE = [
@@ -377,18 +396,18 @@
     )(count, picks, slots, *[in_vmem(r) for r in rows], in_hbm(tensor), staged, pairs, held)
 
 
-def late_products(count, picks, slots, late, state):
+def late_products(place, count, picks, slots, late, state):
     return pl.pallas_call(
         late_kernel,
-        out_shape=STATE + [jax.ShapeDtypeStruct((DEVS * CAP * ROWS, LANES), jnp.bfloat16)],
-        in_specs=[SMEM] * 3 + [VMEM] * 8,
+        out_shape=STATE + [jax.ShapeDtypeStruct((SIDE_SLOTS * ROWS, LANES), jnp.bfloat16)],
+        in_specs=[SMEM] * 4 + [VMEM] * 8,
         out_specs=[VMEM] * 6,
-        input_output_aliases={6: 0, 7: 1, 8: 2, 9: 3, 10: 4},
+        input_output_aliases={7: 0, 8: 1, 9: 2, 10: 3, 11: 4},
         scratch_shapes=[HALF],
         compiler_params=pltpu.CompilerParams(vmem_limit_bytes=8 * MIB),
         cost_estimate=cost(FLOPS, 8 * MIB),
         name="late_products",
-    )(count, picks, slots, *[in_vmem(r) for r in late], *state)[5]
+    )(place, count, picks, slots, *[in_vmem(r) for r in late], *state)
 
 
 def locate_kernel(place, tables0, tables1, tables2, tables3, where):
@@ -429,8 +448,8 @@
         even = place[2] == 1
         i = (place[0] - jnp.where(even, x, y)) & 3
         j = (place[1] - jnp.where(even, y, x)) & 3
-        rows = incoming[pl.ds(a * ORB * CAP * ROWS, ORB * CAP * ROWS), :].astype(jnp.float32)
-        summed = jnp.sum(rows.reshape(ORB, CAP * ROWS, LANES), axis=0)
+        rows = incoming[pl.ds(a * SIDE * CAP * ROWS, SIDE * CAP * ROWS), :].astype(jnp.float32)
+        summed = jnp.sum(rows.reshape(SIDE, CAP * ROWS, LANES), axis=0)
         for k in range(CAP):
             total[where[i * SIDE + j, k]] += summed[k * ROWS : (k + 1) * ROWS, :]
     for r in range(ROWS):
@@ -474,8 +493,13 @@
     state = early_products(
         count, picks, slots, (row0, *early), three_center, staged, pairs, held
     )
-    outgoing = late_products(count, picks, slots, late, state)
-    incoming = lax.all_to_all(outgoing, AXES, split_axis=0, concat_axis=0, tiled=True)
+    state = late_products(place, count, picks, slots, late, state)
+    swap = [(device, device ^ 1) for device in range(DEVS)]
+    outgoing = join(place, state[0], lax.ppermute(state[5], AXES, swap))
+    cores = [list(range(core, DEVS, 2)) for core in range(2)]
+    incoming = lax.all_to_all(
+        outgoing, AXES, split_axis=0, concat_axis=0, axis_index_groups=cores, tiled=True
+    )
 
     return collect(place, locate(place, every), incoming)
 

time: 74.5 us -> 72.6 us (0.974)
  waiting for transfers between devices: 15.9 us -> 12.7 us
  starting transfers between devices: 33.2 us -> 34.3 us
    ppermute x3, waiting for transfers between devices: 7.45 us -> 4.09 us  [body(): lax.ppermute(tables, AXES, shifted(j, True))]
    ppermute x0 -> x1, waiting for transfers between devices: none -> 1.71 us  [body(): outgoing = join(place, state[0], lax.ppermute(state[5], AXES, swap))]
    all_to_all x1, waiting for transfers between devices: 4.05 us -> 2.51 us  [body(): lax.all_to_all(outgoing, AXES, split_axis=0, concat_axis=0, axis_index_gr...]
    pallas_call x1 -> x2, Pallas kernels: 4.77 us -> 5.22 us  [the longest x1 3.85 us: late_products(): pl.pallas_call(late_kernel, out_shape=STATE + [jax.ShapeDtypeStruct((SIDE...]
  transfers between devices with their start and end apart: 16 -> 17, of which waited for: 6 -> 8; matrix products, arithmetic and copies ran while one was open for 1% -> 1% of each run, Pallas kernels for 21% -> 22%
where the time goes in v4:
time: 72.6 us; the launch traced here: 72.3 us
  starting transfers between devices  34.3 us (47%)
  Pallas kernels  23.6 us (33%)
  waiting for transfers between devices  12.7 us (17%)
  local copies, waits for them, and re-layouts  1.47 us (2%)
    all_to_all x1, starting transfers between devices, body(): lax.all_to_all(outgoing, AXES, split_axis=0, concat_axis=0, axis_index_gr...  9.52 us
    pallas_call x1, Pallas kernels, early_products(): pl.pallas_call(early_kernel, out_shape=STATE, in_specs=[SMEM] * 3 + [VMEM...  9.2 us
    ppermute x3, starting transfers between devices, body(): lax.ppermute(sent[j - 1], AXES, shifted(j, False))  6.05 us
    ppermute x3, starting transfers between devices, body(): got = [lax.ppermute(own, AXES, shifted(-j, True)) for j in (1, 2, 3)]  5.74 us
    ppermute x3, starting transfers between devices, body(): lax.ppermute(tables, AXES, shifted(j, True))  4.57 us
    ppermute x3, starting transfers between devices, body(): lax.ppermute(late[j - 1], AXES, shifted(-j, False))  4.19 us
    ppermute x3, starting transfers between devices, body(): lax.ppermute(early[j - 1], AXES, shifted(-j, False))  4.12 us
    ppermute x3, waiting for transfers between devices, body(): lax.ppermute(tables, AXES, shifted(j, True))  4.09 us
  transfers between devices with their start and end apart: 17, of which 8 were waited for; matrix products, arithmetic and copies ran while one was open for 1% of the time, Pallas kernels for 22%

profile of v4, /device:TPU:0, one launch (start us, length us, event | category | flops | bytes accessed | tf_op | source)
XLA Modules:
  0.0 72.3 jit_solution(11483004062466636682)
XLA Ops:
  0.0 1.6 %collective-permute-start.5 = (bf16[64,32,128]{2,1,0:T(8,128)(2,1)}, bf16[64,32,128]{2,1,0:T(8,128)(2,1)S(1)}, u32[]{:S(2)}, u32[]{:S(2)}) collective-permute-start(bf16[64,32,128]{2,1,0:T(8,128)(2,1)} %bitcast.8), channel_id=1, source_target_pairs={{0,8},{1,33},{2,10},{3,35},{4,12},{5,37},{6,14},{7,39},{8,16},{9,4... | collective-permute-start | bytes 1572872 | tf_op jit(solution)/shard_map/ppermute | solution.py:480
  1.6 2.7 %collective-permute-start.4 = (bf16[64,32,128]{2,1,0:T(8,128)(2,1)}, bf16[64,32,128]{2,1,0:T(8,128)(2,1)S(1)}, u32[]{:S(2)}, u32[]{:S(2)}) collective-permute-start(bf16[64,32,128]{2,1,0:T(8,128)(2,1)} %bitcast.9), channel_id=1, source_target_pairs={{0,16},{1,65},{2,18},{3,67},{4,20},{5,69},{6,22},{7,71},{8,24},{9,... | collective-permute-start | bytes 1572872 | tf_op jit(solution)/shard_map/ppermute | solution.py:480
  4.3 1.4 %collective-permute-start.3 = (bf16[64,32,128]{2,1,0:T(8,128)(2,1)}, bf16[64,32,128]{2,1,0:T(8,128)(2,1)S(1)}, u32[]{:S(2)}, u32[]{:S(2)}) collective-permute-start(bf16[64,32,128]{2,1,0:T(8,128)(2,1)} %bitcast.10), channel_id=1, source_target_pairs={{0,24},{1,97},{2,26},{3,99},{4,28},{5,101},{6,30},{7,103},{8,0},{9... | collective-permute-start | bytes 1572872 | tf_op jit(solution)/shard_map/ppermute | solution.py:480
  5.7 0.8 %copy.13.partners = s32[4,8,4]{2,1,0:T(8,128)S(1)} copy(s32[4,8,4]{1,2,0:T(4,128)} %param.6) | data formatting | bytes 1024 | tf_op args[2]
  6.5 0.1 pad_add_fusion.place
  6.6 0.0 copy-start
  6.6 0.7 copy-done
  7.3 1.1 %plan.1 = (s32[8,128]{1,0:T(8,128)S(1)}, s32[8,128]{1,0:T(8,128)S(1)}, s32[8,128]{1,0:T(8,128)S(1)}, s32[8,128]{1,0:T(8,128)S(1)}, s32[1,128]{1,0:T(1,128)S(1)},...) custom-call(s32[4]{0:T(128)S(1)} %pad_add_fusion.place, s32[4,8,4]{2,1,0:T(8,128)S(1)} %copy.13.partners, s32[4,56]{1,0:T(4,128)S(1)} %copy-done), custom_call_target="tpu_custom_call" | custom-call | bytes 65536 | tf_op jit(solution)/shard_map/plan/pallas_call | solution.py:133
  8.3 1.6 %collective-permute-start = (s32[8,128]{1,0:T(8,128)S(1)}, s32[8,128]{1,0:T(8,128)S(1)}, u32[]{:S(2)}, u32[]{:S(2)}) collective-permute-start(s32[8,128]{1,0:T(8,128)S(1)} %get-tuple-element.33), channel_id=1, source_target_pairs={{0,32},{1,9},{2,34},{3,11},{4,36},{5,13},{6,38},{7,15},{8,40},{9,1... | collective-permute-start | bytes 12296 | tf_op jit(solution)/shard_map/ppermute | solution.py:484
  10.0 2.9 %collective-permute-start.1 = (s32[8,128]{1,0:T(8,128)S(1)}, s32[8,128]{1,0:T(8,128)S(1)}, u32[]{:S(2)}, u32[]{:S(2)}) collective-permute-start(s32[8,128]{1,0:T(8,128)S(1)} %get-tuple-element.34), channel_id=1, source_target_pairs={{0,64},{1,17},{2,66},{3,19},{4,68},{5,21},{6,70},{7,23},{8,72},{9,... | collective-permute-start | bytes 12296 | tf_op jit(solution)/shard_map/ppermute | solution.py:484
  12.9 0.7 %collective-permute-done.req1.tab1 = s32[8,128]{1,0:T(8,128)S(1)} collective-permute-done((s32[8,128]{1,0:T(8,128)S(1)}, s32[8,128]{1,0:T(8,128)S(1)}, u32[]{:S(2)}, u32[]{:S(2)}) %collective-permute-start) | collective-permute-done | bytes 4128 | tf_op jit(solution)/shard_map/ppermute | solution.py:484
  13.6 1.5 %collective-permute-start.2 = (s32[8,128]{1,0:T(8,128)S(1)}, s32[8,128]{1,0:T(8,128)S(1)}, u32[]{:S(2)}, u32[]{:S(2)}) collective-permute-start(s32[8,128]{1,0:T(8,128)S(1)} %get-tuple-element.35), channel_id=1, source_target_pairs={{0,96},{1,25},{2,98},{3,27},{4,100},{5,29},{6,102},{7,31},{8,104},... | collective-permute-start | bytes 12296 | tf_op jit(solution)/shard_map/ppermute | solution.py:484
  15.1 3.0 %stage.1 = (bf16[4,8,64,32,128]{4,3,2,1,0:T(8,128)(2,1)S(1)}, bf16[64,32,128]{2,1,0:T(8,128)(2,1)S(1)}, f32[385,8,128]{2,1,0:T(8,128)S(1)}, bf16[2,4,256,256]{3,2,1,0:T(8,128)(2,1)S(1)}) custom-call(bf16[4,8,64,32,128]{4,3,2,1,0:T(8,128)(2,1)} %tensor.3, bf16[64,32,128]{2,1,0:T(8,128)(2,1)} %bitcast.11, s32[1,128]{1,0:T(1,128)S(1)} %get-tuple-element.36.picks, ...), custom_call_target="tpu_custom_call" | custom-call | bytes 5242880 | tf_op jit(solution)/shard_map/stage/pallas_call | solution.py:163
  18.1 0.0 collective-permute-done.1.req2.tab2
  18.1 0.0 collective-permute-done.2.req3.tab3
  18.2 0.0 collective-permute-done.5.got3
  18.2 0.0 collective-permute-done.4.got2
  18.2 0.0 collective-permute-done.3.got1
  18.2 1.2 %pack_early.1 = (bf16[32,32,128]{2,1,0:T(8,128)(2,1)S(1)}, bf16[32,32,128]{2,1,0:T(8,128)(2,1)S(1)}, bf16[32,32,128]{2,1,0:T(8,128)(2,1)S(1)}, bf16[256,32,128]{2,1,0:T(8,128)(2,1)S(1)}) custom-call(s32[8,128]{1,0:T(8,128)S(1)} %collective-permute-done.req1.tab1, s32[8,128]{1,0:T(8,128)S(1)} %collective-permute-done.1.req2.tab2, ...), custom_call_target="tpu_custom_call" | custom-call | bytes 4194304 | tf_op jit(solution)/shard_map/pack_early/pallas_call | solution.py:197
  19.4 2.7 %collective-permute-start.12 = (bf16[32,32,128]{2,1,0:T(8,128)(2,1)S(1)}, bf16[32,32,128]{2,1,0:T(8,128)(2,1)S(1)}, u32[]{:S(2)}, u32[]{:S(2)}) collective-permute-start(bf16[32,32,128]{2,1,0:T(8,128)(2,1)S(1)} %get-tuple-element.46), channel_id=1, source_target_pairs={{0,96},{1,25},{2,98},{3,27},{4,100},{5,29},{6,102},{7,31},{8,104},... | collective-permute-start | bytes 786440 | tf_op jit(solution)/shard_map/ppermute | solution.py:488
  22.1 0.2 collective-permute-start.13
  22.3 1.2 %collective-permute-start.14 = (bf16[32,32,128]{2,1,0:T(8,128)(2,1)S(1)}, bf16[32,32,128]{2,1,0:T(8,128)(2,1)S(1)}, u32[]{:S(2)}, u32[]{:S(2)}) collective-permute-start(bf16[32,32,128]{2,1,0:T(8,128)(2,1)S(1)} %get-tuple-element.48), channel_id=1, source_target_pairs={{0,32},{1,9},{2,34},{3,11},{4,36},{5,13},{6,38},{7,15},{8,40},{9,1... | collective-permute-start | bytes 786440 | tf_op jit(solution)/shard_map/ppermute | solution.py:488
  23.5 1.3 %pack_late.1 = (bf16[64,32,128]{2,1,0:T(8,128)(2,1)S(1)}, bf16[32,32,128]{2,1,0:T(8,128)(2,1)S(1)}, bf16[32,32,128]{2,1,0:T(8,128)(2,1)S(1)}, bf16[32,32,128]{2,1,0:T(8,128)(2,1)S(1)}, s32[4,8,128]{2,1,0:T(8,128)S(1)}) custom-call(s32[8,128]{1,0:T(8,128)S(1)} %get-tuple-element.32.req0.mine, s32[8,128]{1,0:T(8,128)S(1)} %collective-permute-done.req1.tab1, ...), custom_call_target="tpu_custom_call" | custom-call | bytes 2097152 | tf_op jit(solution)/shard_map/pack_late/pallas_call | solution.py:225
  24.8 2.1 %collective-permute-start.9 = (bf16[32,32,128]{2,1,0:T(8,128)(2,1)S(1)}, bf16[32,32,128]{2,1,0:T(8,128)(2,1)S(1)}, u32[]{:S(2)}, u32[]{:S(2)}) collective-permute-start(bf16[32,32,128]{2,1,0:T(8,128)(2,1)S(1)} %get-tuple-element.42), channel_id=1, source_target_pairs={{0,96},{1,25},{2,98},{3,27},{4,100},{5,29},{6,102},{7,31},{8,104},... | collective-permute-start | bytes 786440 | tf_op jit(solution)/shard_map/ppermute | solution.py:490
  26.9 2.1 %collective-permute-start.10 = (bf16[32,32,128]{2,1,0:T(8,128)(2,1)S(1)}, bf16[32,32,128]{2,1,0:T(8,128)(2,1)S(1)}, u32[]{:S(2)}, u32[]{:S(2)}) collective-permute-start(bf16[32,32,128]{2,1,0:T(8,128)(2,1)S(1)} %get-tuple-element.43), channel_id=1, source_target_pairs={{0,64},{1,17},{2,66},{3,19},{4,68},{5,21},{6,70},{7,23},{8,72},{9,... | collective-permute-start | bytes 786440 | tf_op jit(solution)/shard_map/ppermute | solution.py:490
  29.0 0.0 collective-permute-done.12.row1
  29.0 0.0 collective-permute-start.11
  29.0 1.0 %collective-permute-done.13.row2 = bf16[32,32,128]{2,1,0:T(8,128)(2,1)S(1)} collective-permute-done((bf16[32,32,128]{2,1,0:T(8,128)(2,1)S(1)}, bf16[32,32,128]{2,1,0:T(8,128)(2,1)S(1)}, u32[]{:S(2)}, u32[]{:S(2)}) %collective-permute-start.13) | collective-permute-done | bytes 262176 | tf_op jit(solution)/shard_map/ppermute | solution.py:488
  30.0 2.6 %collective-permute-done.14.row3 = bf16[32,32,128]{2,1,0:T(8,128)(2,1)S(1)} collective-permute-done((bf16[32,32,128]{2,1,0:T(8,128)(2,1)S(1)}, bf16[32,32,128]{2,1,0:T(8,128)(2,1)S(1)}, u32[]{:S(2)}, u32[]{:S(2)}) %collective-permute-start.14) | collective-permute-done | bytes 262176 | tf_op jit(solution)/shard_map/ppermute | solution.py:488
  32.7 9.2 %early_products.1 = (f32[385,8,128]{2,1,0:T(8,128)S(1)}, bf16[2,4,256,256]{3,2,1,0:T(8,128)(2,1)S(1)}, bf16[4,8,64,32,128]{4,3,2,1,0:T(8,128)(2,1)S(1)}, bf16[25...) custom-call(s32[1,128]{1,0:T(1,128)S(1)} %get-tuple-element.38.count, ...), custom_call_target="tpu_custom_call", output_to_operand_aliasing={{0}: (8, {}), {1}: (9, {}), {2}: (10, {})} | custom-call | flops 4294967296 | bytes 8388608 | tf_op jit(solution)/shard_map/early_products/pallas_call | solution.py:386
  41.9 0.0 collective-permute-done.9.late1
  41.9 0.0 collective-permute-done.10.late2
  41.9 0.0 collective-permute-done.11.late3
  41.9 3.9 %late_products.1 = (f32[385,8,128]{2,1,0:T(8,128)S(1)}, bf16[2,4,256,256]{3,2,1,0:T(8,128)(2,1)S(1)}, bf16[4,8,64,32,128]{4,3,2,1,0:T(8,128)(2,1)S(1)}, bf16[256...) custom-call(s32[4]{0:T(128)S(1)} %pad_add_fusion.place, ...), custom_call_target="tpu_custom_call", output_to_operand_aliasing={{0}: (7, {}), {1}: (8, {}), {2}: (9, {}), {3}: (10, {}), {4... | custom-call | flops 4294967296 | bytes 8388608 | tf_op jit(solution)/shard_map/late_products/pallas_call | solution.py:400
  45.8 0.1 collective-permute-start.15
  45.9 1.7 %collective-permute-done.15.came = bf16[1536,128]{1,0:T(8,128)(2,1)S(1)} collective-permute-done((bf16[1536,128]{1,0:T(8,128)(2,1)S(1)}, bf16[1536,128]{1,0:T(8,128)(2,1)S(1)}, u32[]{:S(2)}, u32[]{:S(2)}) %collective-permute-start.15) | collective-permute-done | bytes 393248 | tf_op jit(solution)/shard_map/ppermute | solution.py:498
  47.6 1.4 %join.1 = bf16[1536,128]{1,0:T(8,128)(2,1)} custom-call(s32[4]{0:T(128)S(1)} %pad_add_fusion.place, f32[385,8,128]{2,1,0:T(8,128)S(1)} %get-tuple-element.57.staged, bf16[1536,128]{1,0:T(8,128)(2,1)S(1)} %collective-permute-done.15.came), custom_call_target="tpu_custom_call" | custom-call | bytes 2097152 | tf_op jit(solution)/shard_map/join/pallas_call | solution.py:363
  48.9 9.5 %all-to-all-start = ((bf16[64,24,128]{2,1,0:T(8,128)(2,1)}), bf16[64,24,128]{2,1,0:T(8,128)(2,1)S(1)}, u32[]{:S(2)}, u32[]{:S(2)}) async-start(bf16[64,24,128]{2,1,0:T(8,128)(2,1)} %bitcast.5), calls=%async_computation | async-start | bytes 786432 | tf_op jit(solution)/shard_map/all_to_all | solution.py:500
  58.5 2.9 %collective-permute-start.8 = (s32[4,8,128]{2,1,0:T(8,128)S(1)}, s32[4,8,128]{2,1,0:T(8,128)S(1)}, u32[]{:S(2)}, u32[]{:S(2)}) collective-permute-start(s32[4,8,128]{2,1,0:T(8,128)S(1)} %get-tuple-element.41.tables0), channel_id=1, source_target_pairs={{0,24},{1,97},{2,26},{3,99},{4,28},{5,101},{6,30},{7,103},{8,0},{9... | collective-permute-start | bytes 49160 | tf_op jit(solution)/shard_map/ppermute | solution.py:491
  61.3 0.9 %collective-permute-start.7 = (s32[4,8,128]{2,1,0:T(8,128)S(1)}, s32[4,8,128]{2,1,0:T(8,128)S(1)}, u32[]{:S(2)}, u32[]{:S(2)}) collective-permute-start(s32[4,8,128]{2,1,0:T(8,128)S(1)} %get-tuple-element.41.tables0), channel_id=1, source_target_pairs={{0,16},{1,65},{2,18},{3,67},{4,20},{5,69},{6,22},{7,71},{8,24},{9,... | collective-permute-start | bytes 49160 | tf_op jit(solution)/shard_map/ppermute | solution.py:491
  62.2 0.9 %collective-permute-start.6 = (s32[4,8,128]{2,1,0:T(8,128)S(1)}, s32[4,8,128]{2,1,0:T(8,128)S(1)}, u32[]{:S(2)}, u32[]{:S(2)}) collective-permute-start(s32[4,8,128]{2,1,0:T(8,128)S(1)} %get-tuple-element.41.tables0), channel_id=1, source_target_pairs={{0,8},{1,33},{2,10},{3,35},{4,12},{5,37},{6,14},{7,39},{8,16},{9,4... | collective-permute-start | bytes 49160 | tf_op jit(solution)/shard_map/ppermute | solution.py:491
  63.0 1.7 %collective-permute-done.8.tables3 = s32[4,8,128]{2,1,0:T(8,128)S(1)} collective-permute-done((s32[4,8,128]{2,1,0:T(8,128)S(1)}, s32[4,8,128]{2,1,0:T(8,128)S(1)}, u32[]{:S(2)}, u32[]{:S(2)}) %collective-permute-start.8) | collective-permute-done | bytes 16416 | tf_op jit(solution)/shard_map/ppermute | solution.py:491
  64.7 1.9 %collective-permute-done.7.tables2 = s32[4,8,128]{2,1,0:T(8,128)S(1)} collective-permute-done((s32[4,8,128]{2,1,0:T(8,128)S(1)}, s32[4,8,128]{2,1,0:T(8,128)S(1)}, u32[]{:S(2)}, u32[]{:S(2)}) %collective-permute-start.7) | collective-permute-done | bytes 16416 | tf_op jit(solution)/shard_map/ppermute | solution.py:491
  66.6 0.6 collective-permute-done.6.tables1
  67.1 1.0 %locate.1.where = s32[16,128]{1,0:T(8,128)S(1)} custom-call(s32[4]{0:T(128)S(1)} %pad_add_fusion.place, s32[4,8,128]{2,1,0:T(8,128)S(1)} %get-tuple-element.41.tables0, s32[4,8,128]{2,1,0:T(8,128)S(1)} %collective-permute-done.6.tables1, s32[4,8,128]{2,1,0:T(8,128)S(1)} %collective-permute-done.7.tables2, s32[4,8,128]{2,1,0:T(8,128)S(1)} %collective-permute-done.8.tables3), custom_call_target="tpu_custom_call" | custom-call | bytes 65536 | tf_op jit(solution)/shard_map/locate/pallas_call | solution.py:433
  68.2 2.5 %all-to-all-done = bf16[64,24,128]{2,1,0:T(8,128)(2,1)S(1)} async-done(((bf16[64,24,128]{2,1,0:T(8,128)(2,1)}), bf16[64,24,128]{2,1,0:T(8,128)(2,1)S(1)}, u32[]{:S(2)}, u32[]{:S(2)}) %all-to-all-start) | async-done | bytes 393248 | tf_op jit(solution)/shard_map/all_to_all | solution.py:500
  70.7 1.7 %collect.1 = f32[16,1024]{1,0:T(8,128)} custom-call(s32[4]{0:T(128)S(1)} %pad_add_fusion.place, s32[16,128]{1,0:T(8,128)S(1)} %locate.1.where, bf16[1536,128]{1,0:T(8,128)(2,1)S(1)} %bitcast.7), custom_call_target="tpu_custom_call" | custom-call | tf_op jit(solution)/shard_map/collect/pallas_call | solution.py:462
Async XLA Ops:
  0.0 18.2 %collective-permute-start.5 = (bf16[64,32,128]{2,1,0:T(8,128)(2,1)}, bf16[64,32,128]{2,1,0:T(8,128)(2,1)S(1)}, u32[]{:S(2)}, u32[]{:S(2)}) collective-permute-start(bf16[64,32,128]{2,1,0:T(8,128)(2,1)} %bitcast.8), channel_id=1, source_target_pairs={{0,8},{1,33},{2,10},{3,35},{4,12},{5,37},{6,14},{7,39},{8,16},{9,4... | collective-permute-start | bytes 1572872 | tf_op jit(solution)/shard_map/ppermute | solution.py:480
  1.6 16.6 %collective-permute-start.4 = (bf16[64,32,128]{2,1,0:T(8,128)(2,1)}, bf16[64,32,128]{2,1,0:T(8,128)(2,1)S(1)}, u32[]{:S(2)}, u32[]{:S(2)}) collective-permute-start(bf16[64,32,128]{2,1,0:T(8,128)(2,1)} %bitcast.9), channel_id=1, source_target_pairs={{0,16},{1,65},{2,18},{3,67},{4,20},{5,69},{6,22},{7,71},{8,24},{9,... | collective-permute-start | bytes 1572872 | tf_op jit(solution)/shard_map/ppermute | solution.py:480
  4.3 13.9 %collective-permute-start.3 = (bf16[64,32,128]{2,1,0:T(8,128)(2,1)}, bf16[64,32,128]{2,1,0:T(8,128)(2,1)S(1)}, u32[]{:S(2)}, u32[]{:S(2)}) collective-permute-start(bf16[64,32,128]{2,1,0:T(8,128)(2,1)} %bitcast.10), channel_id=1, source_target_pairs={{0,24},{1,97},{2,26},{3,99},{4,28},{5,101},{6,30},{7,103},{8,0},{9... | collective-permute-start | bytes 1572872 | tf_op jit(solution)/shard_map/ppermute | solution.py:480
  6.6 0.7 copy-start
  8.3 5.3 %collective-permute-start = (s32[8,128]{1,0:T(8,128)S(1)}, s32[8,128]{1,0:T(8,128)S(1)}, u32[]{:S(2)}, u32[]{:S(2)}) collective-permute-start(s32[8,128]{1,0:T(8,128)S(1)} %get-tuple-element.33), channel_id=1, source_target_pairs={{0,32},{1,9},{2,34},{3,11},{4,36},{5,13},{6,38},{7,15},{8,40},{9,1... | collective-permute-start | bytes 12296 | tf_op jit(solution)/shard_map/ppermute | solution.py:484
  10.0 8.1 %collective-permute-start.1 = (s32[8,128]{1,0:T(8,128)S(1)}, s32[8,128]{1,0:T(8,128)S(1)}, u32[]{:S(2)}, u32[]{:S(2)}) collective-permute-start(s32[8,128]{1,0:T(8,128)S(1)} %get-tuple-element.34), channel_id=1, source_target_pairs={{0,64},{1,17},{2,66},{3,19},{4,68},{5,21},{6,70},{7,23},{8,72},{9,... | collective-permute-start | bytes 12296 | tf_op jit(solution)/shard_map/ppermute | solution.py:484
  13.6 4.5 %collective-permute-start.2 = (s32[8,128]{1,0:T(8,128)S(1)}, s32[8,128]{1,0:T(8,128)S(1)}, u32[]{:S(2)}, u32[]{:S(2)}) collective-permute-start(s32[8,128]{1,0:T(8,128)S(1)} %get-tuple-element.35), channel_id=1, source_target_pairs={{0,96},{1,25},{2,98},{3,27},{4,100},{5,29},{6,102},{7,31},{8,104},... | collective-permute-start | bytes 12296 | tf_op jit(solution)/shard_map/ppermute | solution.py:484
  19.4 9.6 %collective-permute-start.12 = (bf16[32,32,128]{2,1,0:T(8,128)(2,1)S(1)}, bf16[32,32,128]{2,1,0:T(8,128)(2,1)S(1)}, u32[]{:S(2)}, u32[]{:S(2)}) collective-permute-start(bf16[32,32,128]{2,1,0:T(8,128)(2,1)S(1)} %get-tuple-element.46), channel_id=1, source_target_pairs={{0,96},{1,25},{2,98},{3,27},{4,100},{5,29},{6,102},{7,31},{8,104},... | collective-permute-start | bytes 786440 | tf_op jit(solution)/shard_map/ppermute | solution.py:488
  22.1 8.0 %collective-permute-start.13 = (bf16[32,32,128]{2,1,0:T(8,128)(2,1)S(1)}, bf16[32,32,128]{2,1,0:T(8,128)(2,1)S(1)}, u32[]{:S(2)}, u32[]{:S(2)}) collective-permute-start(bf16[32,32,128]{2,1,0:T(8,128)(2,1)S(1)} %get-tuple-element.47), channel_id=1, source_target_pairs={{0,64},{1,17},{2,66},{3,19},{4,68},{5,21},{6,70},{7,23},{8,72},{9,... | collective-permute-start | bytes 786440 | tf_op jit(solution)/shard_map/ppermute | solution.py:488
  22.3 10.4 %collective-permute-start.14 = (bf16[32,32,128]{2,1,0:T(8,128)(2,1)S(1)}, bf16[32,32,128]{2,1,0:T(8,128)(2,1)S(1)}, u32[]{:S(2)}, u32[]{:S(2)}) collective-permute-start(bf16[32,32,128]{2,1,0:T(8,128)(2,1)S(1)} %get-tuple-element.48), channel_id=1, source_target_pairs={{0,32},{1,9},{2,34},{3,11},{4,36},{5,13},{6,38},{7,15},{8,40},{9,1... | collective-permute-start | bytes 786440 | tf_op jit(solution)/shard_map/ppermute | solution.py:488
  24.8 17.1 %collective-permute-start.9 = (bf16[32,32,128]{2,1,0:T(8,128)(2,1)S(1)}, bf16[32,32,128]{2,1,0:T(8,128)(2,1)S(1)}, u32[]{:S(2)}, u32[]{:S(2)}) collective-permute-start(bf16[32,32,128]{2,1,0:T(8,128)(2,1)S(1)} %get-tuple-element.42), channel_id=1, source_target_pairs={{0,96},{1,25},{2,98},{3,27},{4,100},{5,29},{6,102},{7,31},{8,104},... | collective-permute-start | bytes 786440 | tf_op jit(solution)/shard_map/ppermute | solution.py:490
  26.9 15.0 %collective-permute-start.10 = (bf16[32,32,128]{2,1,0:T(8,128)(2,1)S(1)}, bf16[32,32,128]{2,1,0:T(8,128)(2,1)S(1)}, u32[]{:S(2)}, u32[]{:S(2)}) collective-permute-start(bf16[32,32,128]{2,1,0:T(8,128)(2,1)S(1)} %get-tuple-element.43), channel_id=1, source_target_pairs={{0,64},{1,17},{2,66},{3,19},{4,68},{5,21},{6,70},{7,23},{8,72},{9,... | collective-permute-start | bytes 786440 | tf_op jit(solution)/shard_map/ppermute | solution.py:490
  29.0 12.9 %collective-permute-start.11 = (bf16[32,32,128]{2,1,0:T(8,128)(2,1)S(1)}, bf16[32,32,128]{2,1,0:T(8,128)(2,1)S(1)}, u32[]{:S(2)}, u32[]{:S(2)}) collective-permute-start(bf16[32,32,128]{2,1,0:T(8,128)(2,1)S(1)} %get-tuple-element.44), channel_id=1, source_target_pairs={{0,32},{1,9},{2,34},{3,11},{4,36},{5,13},{6,38},{7,15},{8,40},{9,1... | collective-permute-start | bytes 786440 | tf_op jit(solution)/shard_map/ppermute | solution.py:490
  45.8 1.8 %collective-permute-start.15 = (bf16[1536,128]{1,0:T(8,128)(2,1)S(1)}, bf16[1536,128]{1,0:T(8,128)(2,1)S(1)}, u32[]{:S(2)}, u32[]{:S(2)}) collective-permute-start(bf16[1536,128]{1,0:T(8,128)(2,1)S(1)} %get-tuple-element.58), channel_id=1, source_target_pairs={{0,1},{1,0},{2,3},{3,2},{4,5},{5,4},{6,7},{7,6},{8,9},{9,8},{10,11... | collective-permute-start | bytes 1179656 | tf_op jit(solution)/shard_map/ppermute | solution.py:498
  48.9 21.7 %all-to-all-start = ((bf16[64,24,128]{2,1,0:T(8,128)(2,1)}), bf16[64,24,128]{2,1,0:T(8,128)(2,1)S(1)}, u32[]{:S(2)}, u32[]{:S(2)}) async-start(bf16[64,24,128]{2,1,0:T(8,128)(2,1)} %bitcast.5), calls=%async_computation | async-start | bytes 786432 | tf_op jit(solution)/shard_map/all_to_all | solution.py:500
  58.5 6.2 %collective-permute-start.8 = (s32[4,8,128]{2,1,0:T(8,128)S(1)}, s32[4,8,128]{2,1,0:T(8,128)S(1)}, u32[]{:S(2)}, u32[]{:S(2)}) collective-permute-start(s32[4,8,128]{2,1,0:T(8,128)S(1)} %get-tuple-element.41.tables0), channel_id=1, source_target_pairs={{0,24},{1,97},{2,26},{3,99},{4,28},{5,101},{6,30},{7,103},{8,0},{9... | collective-permute-start | bytes 49160 | tf_op jit(solution)/shard_map/ppermute | solution.py:491
  61.3 5.2 %collective-permute-start.7 = (s32[4,8,128]{2,1,0:T(8,128)S(1)}, s32[4,8,128]{2,1,0:T(8,128)S(1)}, u32[]{:S(2)}, u32[]{:S(2)}) collective-permute-start(s32[4,8,128]{2,1,0:T(8,128)S(1)} %get-tuple-element.41.tables0), channel_id=1, source_target_pairs={{0,16},{1,65},{2,18},{3,67},{4,20},{5,69},{6,22},{7,71},{8,24},{9,... | collective-permute-start | bytes 49160 | tf_op jit(solution)/shard_map/ppermute | solution.py:491
  62.2 4.9 %collective-permute-start.6 = (s32[4,8,128]{2,1,0:T(8,128)S(1)}, s32[4,8,128]{2,1,0:T(8,128)S(1)}, u32[]{:S(2)}, u32[]{:S(2)}) collective-permute-start(s32[4,8,128]{2,1,0:T(8,128)S(1)} %get-tuple-element.41.tables0), channel_id=1, source_target_pairs={{0,8},{1,33},{2,10},{3,35},{4,12},{5,37},{6,14},{7,39},{8,16},{9,4... | collective-permute-start | bytes 49160 | tf_op jit(solution)/shard_map/ppermute | solution.py:491

commit v5 on v4

--- a/solution.py
+++ b/solution.py
@@ -61,6 +61,7 @@
 HBM = pl.BlockSpec(memory_space=pltpu.HBM)
 MIB = 1024 * 1024
 LIST_ROW = AUX_DEV
+PICKS, COUNT, EVEN = 4, 5, 6
 SIDE_SLOTS = DEVS * CAP // 2
 BLOCKS = ROW_CAP + 3 * ROW_CAP
 SOON = ROW_CAP + 3 * EARLY
@@ -74,7 +75,7 @@
     return jnp.broadcast_to(row, (LANES, LANES)).T
 
 
-def plan_kernel(place, partners, owners, sent0, sent1, sent2, sent3, picks, slots, count):
+def plan_kernel(place, partners, owners, sent0, sent1, sent2, sent3, lists):
     near, far, even = place[0], place[1], place[2]
     table = jnp.full((ROWS, LANES), -1, jnp.int32)
     for sent in (sent0, sent1, sent2, sent3):
@@ -110,9 +111,11 @@
         rank < EARLY, ROW_CAP + there * EARLY + rank, SOON + there * LATE + rank - EARLY
     )
     pick = jnp.where(rel_far == 0, rank, remote)
-    picks[...] = pick
+    lists[pl.ds(PICKS, 1), :] = pick
     missing = jnp.where(pick >= SOON, across[:1], LANES)
-    count[...] = jnp.broadcast_to(jnp.min(missing, axis=1, keepdims=True) >> 5, (1, LANES))
+    count = jnp.min(missing, axis=1, keepdims=True) >> 5
+    lists[pl.ds(COUNT, 1), :] = jnp.broadcast_to(count, (1, LANES))
+    lists[pl.ds(EVEN, 2), :] = jnp.broadcast_to(even, (2, LANES))
 
     owner = sent0[...] >> 4
     stood = []
@@ -123,18 +126,17 @@
         for before in stood:
             hits += (before == row).astype(jnp.int32)
         at = (row & 1) * SIDE_SLOTS + (row >> 1) * CAP
-        slots[pl.ds(p, 1), :] = at + jnp.sum(hits, axis=0, keepdims=True)
+        lists[pl.ds(p, 1), :] = at + jnp.sum(hits, axis=0, keepdims=True)
         stood.append(column)
 
 
 def plan(place, partners, owners):
     tile = jax.ShapeDtypeStruct((ROWS, LANES), jnp.int32)
-    line = jax.ShapeDtypeStruct((1, LANES), jnp.int32)
     return pl.pallas_call(
         plan_kernel,
-        out_shape=[tile] * 4 + [line, tile, line],
+        out_shape=[tile] * 5,
         in_specs=[SMEM] + [VMEM] * 2,
-        out_specs=[VMEM] * 7,
+        out_specs=[VMEM] * 5,
         compiler_params=pltpu.CompilerParams(vmem_limit_bytes=2 * MIB),
         cost_estimate=cost(0, 64 * 1024),
         name="plan",
@@ -145,8 +147,8 @@
 PAIRS = (2, MS // 2, 2 * OCC, 2 * OCC)
 
 
-def stage_kernel(tensor, own, picks, slots, count, held, own_out, staged, pairs, sems):
-    del picks, slots, count
+def stage_kernel(tensor, own, lists, held, own_out, staged, pairs, sems):
+    del lists
     copies = [
         pltpu.make_async_copy(own, own_out, sems.at[0]),
         pltpu.make_async_copy(tensor.at[0], held.at[0], sems.at[1]),
@@ -159,7 +161,7 @@
         copy.wait()
 
 
-def stage(tensor, own, *lists):
+def stage(tensor, own, lists):
     return pl.pallas_call(
         stage_kernel,
         out_shape=[
@@ -168,13 +170,13 @@
             pltpu.VMEM(STAGED, jnp.float32),
             pltpu.VMEM(PAIRS, jnp.bfloat16),
         ],
-        in_specs=[HBM] * 2 + [SMEM] * 3,
+        in_specs=[HBM] * 2 + [SMEM],
         out_specs=[VMEM] * 4,
         scratch_shapes=[pltpu.SemaphoreType.DMA((2,))],
         compiler_params=pltpu.CompilerParams(vmem_limit_bytes=MIB),
         cost_estimate=cost(0, 5 * MIB),
         name="stage",
-    )(in_hbm(tensor), in_hbm(own), *lists)
+    )(in_hbm(tensor), in_hbm(own), lists)
 
 
 def pack_early_kernel(
@@ -237,13 +239,13 @@
     )(mine, *received, shards, mine, *received)
 
 
-def run_blocks(low, high, picks, slots, tensor, staged, pairs, blocks, total, half, ready):
+def run_blocks(low, high, lists, tensor, staged, pairs, blocks, total, half, ready):
     def fill(p):
         for s in range(MS):
             side = (s % 2) * OCC
             for k in range(NPS):
                 pairs[p % 2, s // 2, pl.ds(side + k * BS, BS), pl.ds(side, OCC)] = blocks[
-                    picks[0, (p * MS + s) * NPS + k]
+                    lists[PICKS, (p * MS + s) * NPS + k]
                 ]
 
     def first(p, c):
@@ -288,12 +290,12 @@
                 first(p, c + 1)
             second(p, c)
             if c == 0:
-                put(jnp.maximum(p - 1, 0), p > 0, slots, total, staged)
+                put(jnp.maximum(p - 1, 0), p > 0, lists, total, staged)
             if c == 1:
                 fill(jnp.minimum(p + 1, high - 1))
 
 
-def put(p, valid, slots, total, staged):
+def put(p, valid, lists, total, staged):
     factor = np.float32(1.0 / np.sqrt(PA * NOCC))
     e = 0
     for s in range(MS):
@@ -307,12 +309,12 @@
                 ],
                 axis=1,
             )
-            staged[jnp.where(valid, slots[p, e], DEVS * CAP)] = tile * factor
+            staged[jnp.where(valid, lists[p, e], DEVS * CAP)] = tile * factor
             e += 1
 
 
 def early_kernel(
-    count, picks, slots, row0, row1, row2, row3, tensor, staged0, pairs0, held0,
+    lists, row0, row1, row2, row3, tensor, staged0, pairs0, held0,
     staged, pairs, held, blocks, total, half, sems,
 ):
     del staged0, pairs0, held0
@@ -331,35 +333,35 @@
         def _():
             rest(p).wait()
 
-    run_blocks(0, count[0, 0], picks, slots, held, staged, pairs, blocks, total, half, ready)
+    run_blocks(0, lists[COUNT, 0], lists, held, staged, pairs, blocks, total, half, ready)
     for p in range(1, AUX_DEV):
 
-        @pl.when(p >= count[0, 0])
+        @pl.when(p >= lists[COUNT, 0])
         def _():
             rest(p).wait()
 
 
 def late_kernel(
-    place, count, picks, slots, late1, late2, late3, staged0, pairs0, held0, blocks0, total0,
+    lists, late1, late2, late3, staged0, pairs0, held0, blocks0, total0,
     staged, pairs, held, blocks, total, out, half,
 ):
     del staged0, pairs0, held0, blocks0, total0
     for at, src in enumerate((late1, late2, late3)):
         blocks[pl.ds(SOON + at * LATE, LATE)] = src[...]
     run_blocks(
-        count[0, 0], AUX_DEV, picks, slots, held, staged, pairs, blocks, total, half, lambda p: None
+        lists[COUNT, 0], AUX_DEV, lists, held, staged, pairs, blocks, total, half, lambda p: None
     )
-    put(AUX_DEV - 1, True, slots, total, staged)
-    done = staged[pl.ds(place[2] * SIDE_SLOTS, SIDE_SLOTS)]
+    put(AUX_DEV - 1, True, lists, total, staged)
+    done = staged[pl.ds(lists[EVEN, 0] * SIDE_SLOTS, SIDE_SLOTS)]
     out[...] = done.reshape(SIDE_SLOTS * ROWS, LANES).astype(jnp.bfloat16)
 
 
-def join_kernel(place, staged, came, out):
-    kept = staged[pl.ds((1 - place[2]) * SIDE_SLOTS, SIDE_SLOTS)].reshape(SIDE_SLOTS * ROWS, LANES)
+def join_kernel(lists, staged, came, out):
+    kept = staged[pl.ds((1 - lists[EVEN, 0]) * SIDE_SLOTS, SIDE_SLOTS)].reshape(SIDE_SLOTS * ROWS, LANES)
     out[...] = (kept + came[...].astype(jnp.float32)).astype(jnp.bfloat16)
 
 
-def join(place, staged, came):
+def join(lists, staged, came):
     return pl.pallas_call(
         join_kernel,
         out_shape=jax.ShapeDtypeStruct(came.shape, came.dtype),
@@ -368,7 +370,7 @@
         compiler_params=pltpu.CompilerParams(vmem_limit_bytes=4 * MIB),
         cost_estimate=cost(0, 2 * MIB),
         name="join",
-    )(place, staged, in_vmem(came))
+    )(lists, staged, in_vmem(came))
 
 
 STATE = [
@@ -382,32 +384,32 @@
 FLOPS = 2 * (MS * PA * BS * OCC * OCC * 4 + 2 * PA * OCC * (MS * BS) ** 2)
 
 
-def early_products(count, picks, slots, rows, tensor, staged, pairs, held):
+def early_products(lists, rows, tensor, staged, pairs, held):
     return pl.pallas_call(
         early_kernel,
         out_shape=STATE,
-        in_specs=[SMEM] * 3 + [VMEM] * 4 + [HBM] + [VMEM] * 3,
+        in_specs=[SMEM] + [VMEM] * 4 + [HBM] + [VMEM] * 3,
         out_specs=[VMEM] * 5,
-        input_output_aliases={8: 0, 9: 1, 10: 2},
+        input_output_aliases={6: 0, 7: 1, 8: 2},
         scratch_shapes=[HALF, pltpu.SemaphoreType.DMA((AUX_DEV,))],
         compiler_params=pltpu.CompilerParams(vmem_limit_bytes=8 * MIB),
         cost_estimate=cost(FLOPS, 8 * MIB),
         name="early_products",
-    )(count, picks, slots, *[in_vmem(r) for r in rows], in_hbm(tensor), staged, pairs, held)
-
-
-def late_products(place, count, picks, slots, late, state):
+    )(lists, *[in_vmem(r) for r in rows], in_hbm(tensor), staged, pairs, held)
+
+
+def late_products(lists, late, state):
     return pl.pallas_call(
         late_kernel,
         out_shape=STATE + [jax.ShapeDtypeStruct((SIDE_SLOTS * ROWS, LANES), jnp.bfloat16)],
-        in_specs=[SMEM] * 4 + [VMEM] * 8,
+        in_specs=[SMEM] + [VMEM] * 8,
         out_specs=[VMEM] * 6,
-        input_output_aliases={7: 0, 8: 1, 9: 2, 10: 3, 11: 4},
+        input_output_aliases={4: 0, 5: 1, 6: 2, 7: 3, 8: 4},
         scratch_shapes=[HALF],
         compiler_params=pltpu.CompilerParams(vmem_limit_bytes=8 * MIB),
         cost_estimate=cost(FLOPS, 8 * MIB),
         name="late_products",
-    )(place, count, picks, slots, *[in_vmem(r) for r in late], *state)
+    )(lists, *[in_vmem(r) for r in late], *state)
 
 
 def locate_kernel(place, tables0, tables1, tables2, tables3, where):
@@ -480,10 +482,10 @@
     got = [lax.ppermute(own, AXES, shifted(-j, True)) for j in (1, 2, 3)]
 
     place = jnp.stack([near, far, even.astype(jnp.int32), aux * ORB + orb]).astype(jnp.int32)
-    mine, *sent, picks, slots, count = plan(place, partners, pair_owner)
+    mine, *sent, lists = plan(place, partners, pair_owner)
     received = [lax.ppermute(sent[j - 1], AXES, shifted(j, False)) for j in (1, 2, 3)]
 
-    held, here, staged, pairs = stage(three_center, own, picks, slots, count)
+    held, here, staged, pairs = stage(three_center, own, lists)
     *early, shards = pack_early(received, here, got)
     early = [lax.ppermute(early[j - 1], AXES, shifted(-j, False)) for j in (1, 2, 3)]
     row0, *late, tables = pack_late(mine, received, shards)
@@ -491,11 +493,11 @@
     every = [tables] + [lax.ppermute(tables, AXES, shifted(j, True)) for j in (1, 2, 3)]
 
     state = early_products(
-        count, picks, slots, (row0, *early), three_center, staged, pairs, held
+        lists, (row0, *early), three_center, staged, pairs, held
     )
-    state = late_products(place, count, picks, slots, late, state)
+    state = late_products(lists, late, state)
     swap = [(device, device ^ 1) for device in range(DEVS)]
-    outgoing = join(place, state[0], lax.ppermute(state[5], AXES, swap))
+    outgoing = join(lists, state[0], lax.ppermute(state[5], AXES, swap))
     cores = [list(range(core, DEVS, 2)) for core in range(2)]
     incoming = lax.all_to_all(
         outgoing, AXES, split_axis=0, concat_axis=0, axis_index_groups=cores, tiled=True

time: 72.6 us -> 72.9 us (level)
  no operation moved by 1% of the time
where the time goes in v5:
time: 72.9 us; the launch traced here: 72.7 us
  starting transfers between devices  34.3 us (47%)
  Pallas kernels  24 us (33%)
  waiting for transfers between devices  12.8 us (18%)
  local copies, waits for them, and re-layouts  1.47 us (2%)
    all_to_all x1, starting transfers between devices, body(): lax.all_to_all(outgoing, AXES, split_axis=0, concat_axis=0, axis_index_gr...  9.5 us
    pallas_call x1, Pallas kernels, early_products(): pl.pallas_call(early_kernel, out_shape=STATE, in_specs=[SMEM] + [VMEM] *...  9.39 us
    ppermute x3, starting transfers between devices, body(): lax.ppermute(sent[j - 1], AXES, shifted(j, False))  6.05 us
    ppermute x3, starting transfers between devices, body(): got = [lax.ppermute(own, AXES, shifted(-j, True)) for j in (1, 2, 3)]  5.74 us
    ppermute x3, starting transfers between devices, body(): lax.ppermute(tables, AXES, shifted(j, True))  4.57 us
    ppermute x3, starting transfers between devices, body(): lax.ppermute(late[j - 1], AXES, shifted(-j, False))  4.18 us
    ppermute x3, starting transfers between devices, body(): lax.ppermute(early[j - 1], AXES, shifted(-j, False))  4.13 us
    ppermute x3, waiting for transfers between devices, body(): lax.ppermute(tables, AXES, shifted(j, True))  4.09 us
  transfers between devices with their start and end apart: 17, of which 8 were waited for; matrix products, arithmetic and copies ran while one was open for 1% of the time, Pallas kernels for 22%

profile of v5, /device:TPU:0, one launch (start us, length us, event | category | flops | bytes accessed | tf_op | source)
XLA Modules:
  0.0 72.7 jit_solution(3004953352116568559)
XLA Ops:
  0.0 1.6 %collective-permute-start.5 = (bf16[64,32,128]{2,1,0:T(8,128)(2,1)}, bf16[64,32,128]{2,1,0:T(8,128)(2,1)S(1)}, u32[]{:S(2)}, u32[]{:S(2)}) collective-permute-start(bf16[64,32,128]{2,1,0:T(8,128)(2,1)} %bitcast.8), channel_id=1, source_target_pairs={{0,8},{1,33},{2,10},{3,35},{4,12},{5,37},{6,14},{7,39},{8,16},{9,4... | collective-permute-start | bytes 1572872 | tf_op jit(solution)/shard_map/ppermute | solution.py:482
  1.6 2.7 %collective-permute-start.4 = (bf16[64,32,128]{2,1,0:T(8,128)(2,1)}, bf16[64,32,128]{2,1,0:T(8,128)(2,1)S(1)}, u32[]{:S(2)}, u32[]{:S(2)}) collective-permute-start(bf16[64,32,128]{2,1,0:T(8,128)(2,1)} %bitcast.9), channel_id=1, source_target_pairs={{0,16},{1,65},{2,18},{3,67},{4,20},{5,69},{6,22},{7,71},{8,24},{9,... | collective-permute-start | bytes 1572872 | tf_op jit(solution)/shard_map/ppermute | solution.py:482
  4.3 1.4 %collective-permute-start.3 = (bf16[64,32,128]{2,1,0:T(8,128)(2,1)}, bf16[64,32,128]{2,1,0:T(8,128)(2,1)S(1)}, u32[]{:S(2)}, u32[]{:S(2)}) collective-permute-start(bf16[64,32,128]{2,1,0:T(8,128)(2,1)} %bitcast.10), channel_id=1, source_target_pairs={{0,24},{1,97},{2,26},{3,99},{4,28},{5,101},{6,30},{7,103},{8,0},{9... | collective-permute-start | bytes 1572872 | tf_op jit(solution)/shard_map/ppermute | solution.py:482
  5.7 0.8 %copy.13.partners = s32[4,8,4]{2,1,0:T(8,128)S(1)} copy(s32[4,8,4]{1,2,0:T(4,128)} %param.6) | data formatting | bytes 1024 | tf_op args[2]
  6.5 0.1 pad_add_fusion.place
  6.6 0.0 copy-start
  6.6 0.7 copy-done
  7.3 1.1 %plan.1 = (s32[8,128]{1,0:T(8,128)S(1)}, s32[8,128]{1,0:T(8,128)S(1)}, s32[8,128]{1,0:T(8,128)S(1)}, s32[8,128]{1,0:T(8,128)S(1)}, s32[8,128]{1,0:T(8,128)S(1)}) custom-call(s32[4]{0:T(128)S(1)} %pad_add_fusion.place, s32[4,8,4]{2,1,0:T(8,128)S(1)} %copy.13.partners, s32[4,56]{1,0:T(4,128)S(1)} %copy-done), custom_call_target="tpu_custom_call" | custom-call | bytes 65536 | tf_op jit(solution)/shard_map/plan/pallas_call | solution.py:135
  8.3 1.6 %collective-permute-start = (s32[8,128]{1,0:T(8,128)S(1)}, s32[8,128]{1,0:T(8,128)S(1)}, u32[]{:S(2)}, u32[]{:S(2)}) collective-permute-start(s32[8,128]{1,0:T(8,128)S(1)} %get-tuple-element.31), channel_id=1, source_target_pairs={{0,32},{1,9},{2,34},{3,11},{4,36},{5,13},{6,38},{7,15},{8,40},{9,1... | collective-permute-start | bytes 12296 | tf_op jit(solution)/shard_map/ppermute | solution.py:486
  10.0 2.9 %collective-permute-start.1 = (s32[8,128]{1,0:T(8,128)S(1)}, s32[8,128]{1,0:T(8,128)S(1)}, u32[]{:S(2)}, u32[]{:S(2)}) collective-permute-start(s32[8,128]{1,0:T(8,128)S(1)} %get-tuple-element.32), channel_id=1, source_target_pairs={{0,64},{1,17},{2,66},{3,19},{4,68},{5,21},{6,70},{7,23},{8,72},{9,... | collective-permute-start | bytes 12296 | tf_op jit(solution)/shard_map/ppermute | solution.py:486
  12.9 0.7 %collective-permute-done.req1.tab1 = s32[8,128]{1,0:T(8,128)S(1)} collective-permute-done((s32[8,128]{1,0:T(8,128)S(1)}, s32[8,128]{1,0:T(8,128)S(1)}, u32[]{:S(2)}, u32[]{:S(2)}) %collective-permute-start) | collective-permute-done | bytes 4128 | tf_op jit(solution)/shard_map/ppermute | solution.py:486
  13.6 1.5 %collective-permute-start.2 = (s32[8,128]{1,0:T(8,128)S(1)}, s32[8,128]{1,0:T(8,128)S(1)}, u32[]{:S(2)}, u32[]{:S(2)}) collective-permute-start(s32[8,128]{1,0:T(8,128)S(1)} %get-tuple-element.33), channel_id=1, source_target_pairs={{0,96},{1,25},{2,98},{3,27},{4,100},{5,29},{6,102},{7,31},{8,104},... | collective-permute-start | bytes 12296 | tf_op jit(solution)/shard_map/ppermute | solution.py:486
  15.1 3.0 %stage.1 = (bf16[4,8,64,32,128]{4,3,2,1,0:T(8,128)(2,1)S(1)}, bf16[64,32,128]{2,1,0:T(8,128)(2,1)S(1)}, f32[385,8,128]{2,1,0:T(8,128)S(1)}, bf16[2,4,256,256]{3,2,1,0:T(8,128)(2,1)S(1)}) custom-call(bf16[4,8,64,32,128]{4,3,2,1,0:T(8,128)(2,1)} %tensor.3, bf16[64,32,128]{2,1,0:T(8,128)(2,1)} %bitcast.11, s32[8,128]{1,0:T(8,128)S(1)} %get-tuple-element.34.lists), custom_call_target="tpu_custom_call" | custom-call | bytes 5242880 | tf_op jit(solution)/shard_map/stage/pallas_call | solution.py:165
  18.1 0.0 collective-permute-done.1.req2.tab2
  18.1 0.0 collective-permute-done.2.req3.tab3
  18.1 0.0 collective-permute-done.5.got3
  18.2 0.0 collective-permute-done.4.got2
  18.2 0.0 collective-permute-done.3.got1
  18.2 1.2 %pack_early.1 = (bf16[32,32,128]{2,1,0:T(8,128)(2,1)S(1)}, bf16[32,32,128]{2,1,0:T(8,128)(2,1)S(1)}, bf16[32,32,128]{2,1,0:T(8,128)(2,1)S(1)}, bf16[256,32,128]{2,1,0:T(8,128)(2,1)S(1)}) custom-call(s32[8,128]{1,0:T(8,128)S(1)} %collective-permute-done.req1.tab1, s32[8,128]{1,0:T(8,128)S(1)} %collective-permute-done.1.req2.tab2, ...), custom_call_target="tpu_custom_call" | custom-call | bytes 4194304 | tf_op jit(solution)/shard_map/pack_early/pallas_call | solution.py:199
  19.4 2.7 %collective-permute-start.12 = (bf16[32,32,128]{2,1,0:T(8,128)(2,1)S(1)}, bf16[32,32,128]{2,1,0:T(8,128)(2,1)S(1)}, u32[]{:S(2)}, u32[]{:S(2)}) collective-permute-start(bf16[32,32,128]{2,1,0:T(8,128)(2,1)S(1)} %get-tuple-element.42), channel_id=1, source_target_pairs={{0,96},{1,25},{2,98},{3,27},{4,100},{5,29},{6,102},{7,31},{8,104},... | collective-permute-start | bytes 786440 | tf_op jit(solution)/shard_map/ppermute | solution.py:490
  22.0 0.2 collective-permute-start.13
  22.3 1.2 %collective-permute-start.14 = (bf16[32,32,128]{2,1,0:T(8,128)(2,1)S(1)}, bf16[32,32,128]{2,1,0:T(8,128)(2,1)S(1)}, u32[]{:S(2)}, u32[]{:S(2)}) collective-permute-start(bf16[32,32,128]{2,1,0:T(8,128)(2,1)S(1)} %get-tuple-element.44), channel_id=1, source_target_pairs={{0,32},{1,9},{2,34},{3,11},{4,36},{5,13},{6,38},{7,15},{8,40},{9,1... | collective-permute-start | bytes 786440 | tf_op jit(solution)/shard_map/ppermute | solution.py:490
  23.5 1.3 %pack_late.1 = (bf16[64,32,128]{2,1,0:T(8,128)(2,1)S(1)}, bf16[32,32,128]{2,1,0:T(8,128)(2,1)S(1)}, bf16[32,32,128]{2,1,0:T(8,128)(2,1)S(1)}, bf16[32,32,128]{2,1,0:T(8,128)(2,1)S(1)}, s32[4,8,128]{2,1,0:T(8,128)S(1)}) custom-call(s32[8,128]{1,0:T(8,128)S(1)} %get-tuple-element.30.req0.mine, s32[8,128]{1,0:T(8,128)S(1)} %collective-permute-done.req1.tab1, ...), custom_call_target="tpu_custom_call" | custom-call | bytes 2097152 | tf_op jit(solution)/shard_map/pack_late/pallas_call | solution.py:227
  24.8 2.1 %collective-permute-start.9 = (bf16[32,32,128]{2,1,0:T(8,128)(2,1)S(1)}, bf16[32,32,128]{2,1,0:T(8,128)(2,1)S(1)}, u32[]{:S(2)}, u32[]{:S(2)}) collective-permute-start(bf16[32,32,128]{2,1,0:T(8,128)(2,1)S(1)} %get-tuple-element.38), channel_id=1, source_target_pairs={{0,96},{1,25},{2,98},{3,27},{4,100},{5,29},{6,102},{7,31},{8,104},... | collective-permute-start | bytes 786440 | tf_op jit(solution)/shard_map/ppermute | solution.py:492
  26.9 2.1 %collective-permute-start.10 = (bf16[32,32,128]{2,1,0:T(8,128)(2,1)S(1)}, bf16[32,32,128]{2,1,0:T(8,128)(2,1)S(1)}, u32[]{:S(2)}, u32[]{:S(2)}) collective-permute-start(bf16[32,32,128]{2,1,0:T(8,128)(2,1)S(1)} %get-tuple-element.39), channel_id=1, source_target_pairs={{0,64},{1,17},{2,66},{3,19},{4,68},{5,21},{6,70},{7,23},{8,72},{9,... | collective-permute-start | bytes 786440 | tf_op jit(solution)/shard_map/ppermute | solution.py:492
  29.0 0.0 collective-permute-done.12.row1
  29.0 0.0 collective-permute-start.11
  29.0 1.0 %collective-permute-done.13.row2 = bf16[32,32,128]{2,1,0:T(8,128)(2,1)S(1)} collective-permute-done((bf16[32,32,128]{2,1,0:T(8,128)(2,1)S(1)}, bf16[32,32,128]{2,1,0:T(8,128)(2,1)S(1)}, u32[]{:S(2)}, u32[]{:S(2)}) %collective-permute-start.13) | collective-permute-done | bytes 262176 | tf_op jit(solution)/shard_map/ppermute | solution.py:490
  30.0 2.6 %collective-permute-done.14.row3 = bf16[32,32,128]{2,1,0:T(8,128)(2,1)S(1)} collective-permute-done((bf16[32,32,128]{2,1,0:T(8,128)(2,1)S(1)}, bf16[32,32,128]{2,1,0:T(8,128)(2,1)S(1)}, u32[]{:S(2)}, u32[]{:S(2)}) %collective-permute-start.14) | collective-permute-done | bytes 262176 | tf_op jit(solution)/shard_map/ppermute | solution.py:490
  32.7 9.4 %early_products.1 = (f32[385,8,128]{2,1,0:T(8,128)S(1)}, bf16[2,4,256,256]{3,2,1,0:T(8,128)(2,1)S(1)}, bf16[4,8,64,32,128]{4,3,2,1,0:T(8,128)(2,1)S(1)}, bf16[25...) custom-call(s32[8,128]{1,0:T(8,128)S(1)} %get-tuple-element.34.lists, ...), custom_call_target="tpu_custom_call", output_to_operand_aliasing={{0}: (6, {}), {1}: (7, {}), {2}: (8, {})} | custom-call | flops 4294967296 | bytes 8388608 | tf_op jit(solution)/shard_map/early_products/pallas_call | solution.py:388
  42.1 0.0 collective-permute-done.9.late1
  42.1 0.0 collective-permute-done.10.late2
  42.1 0.0 collective-permute-done.11.late3
  42.1 4.0 %late_products.1 = (f32[385,8,128]{2,1,0:T(8,128)S(1)}, bf16[2,4,256,256]{3,2,1,0:T(8,128)(2,1)S(1)}, bf16[4,8,64,32,128]{4,3,2,1,0:T(8,128)(2,1)S(1)}, bf16[256...) custom-call(s32[8,128]{1,0:T(8,128)S(1)} %get-tuple-element.34.lists, ...), custom_call_target="tpu_custom_call", output_to_operand_aliasing={{0}: (4, {}), {1}: (5, {}), {2}: (6, {}), {3}: (7, {}), {4}... | custom-call | flops 4294967296 | bytes 8388608 | tf_op jit(solution)/shard_map/late_products/pallas_call | solution.py:402
  46.0 0.1 collective-permute-start.15
  46.1 1.7 %collective-permute-done.15.came = bf16[1536,128]{1,0:T(8,128)(2,1)S(1)} collective-permute-done((bf16[1536,128]{1,0:T(8,128)(2,1)S(1)}, bf16[1536,128]{1,0:T(8,128)(2,1)S(1)}, u32[]{:S(2)}, u32[]{:S(2)}) %collective-permute-start.15) | collective-permute-done | bytes 393248 | tf_op jit(solution)/shard_map/ppermute | solution.py:500
  47.9 1.4 %join.1 = bf16[1536,128]{1,0:T(8,128)(2,1)} custom-call(s32[8,128]{1,0:T(8,128)S(1)} %get-tuple-element.34.lists, f32[385,8,128]{2,1,0:T(8,128)S(1)} %get-tuple-element.53.staged, bf16[1536,128]{1,0:T(8,128)(2,1)S(1)} %collective-permute-done.15.came), custom_call_target="tpu_custom_call" | custom-call | bytes 2097152 | tf_op jit(solution)/shard_map/join/pallas_call | solution.py:365
  49.3 9.5 %all-to-all-start = ((bf16[64,24,128]{2,1,0:T(8,128)(2,1)}), bf16[64,24,128]{2,1,0:T(8,128)(2,1)S(1)}, u32[]{:S(2)}, u32[]{:S(2)}) async-start(bf16[64,24,128]{2,1,0:T(8,128)(2,1)} %bitcast.5), calls=%async_computation | async-start | bytes 786432 | tf_op jit(solution)/shard_map/all_to_all | solution.py:502
  58.8 2.9 %collective-permute-start.8 = (s32[4,8,128]{2,1,0:T(8,128)S(1)}, s32[4,8,128]{2,1,0:T(8,128)S(1)}, u32[]{:S(2)}, u32[]{:S(2)}) collective-permute-start(s32[4,8,128]{2,1,0:T(8,128)S(1)} %get-tuple-element.37.tables0), channel_id=1, source_target_pairs={{0,24},{1,97},{2,26},{3,99},{4,28},{5,101},{6,30},{7,103},{8,0},{9... | collective-permute-start | bytes 49160 | tf_op jit(solution)/shard_map/ppermute | solution.py:493
  61.6 0.9 %collective-permute-start.7 = (s32[4,8,128]{2,1,0:T(8,128)S(1)}, s32[4,8,128]{2,1,0:T(8,128)S(1)}, u32[]{:S(2)}, u32[]{:S(2)}) collective-permute-start(s32[4,8,128]{2,1,0:T(8,128)S(1)} %get-tuple-element.37.tables0), channel_id=1, source_target_pairs={{0,16},{1,65},{2,18},{3,67},{4,20},{5,69},{6,22},{7,71},{8,24},{9,... | collective-permute-start | bytes 49160 | tf_op jit(solution)/shard_map/ppermute | solution.py:493
  62.5 0.9 %collective-permute-start.6 = (s32[4,8,128]{2,1,0:T(8,128)S(1)}, s32[4,8,128]{2,1,0:T(8,128)S(1)}, u32[]{:S(2)}, u32[]{:S(2)}) collective-permute-start(s32[4,8,128]{2,1,0:T(8,128)S(1)} %get-tuple-element.37.tables0), channel_id=1, source_target_pairs={{0,8},{1,33},{2,10},{3,35},{4,12},{5,37},{6,14},{7,39},{8,16},{9,4... | collective-permute-start | bytes 49160 | tf_op jit(solution)/shard_map/ppermute | solution.py:493
  63.3 1.7 %collective-permute-done.8.tables3 = s32[4,8,128]{2,1,0:T(8,128)S(1)} collective-permute-done((s32[4,8,128]{2,1,0:T(8,128)S(1)}, s32[4,8,128]{2,1,0:T(8,128)S(1)}, u32[]{:S(2)}, u32[]{:S(2)}) %collective-permute-start.8) | collective-permute-done | bytes 16416 | tf_op jit(solution)/shard_map/ppermute | solution.py:493
  65.0 1.9 %collective-permute-done.7.tables2 = s32[4,8,128]{2,1,0:T(8,128)S(1)} collective-permute-done((s32[4,8,128]{2,1,0:T(8,128)S(1)}, s32[4,8,128]{2,1,0:T(8,128)S(1)}, u32[]{:S(2)}, u32[]{:S(2)}) %collective-permute-start.7) | collective-permute-done | bytes 16416 | tf_op jit(solution)/shard_map/ppermute | solution.py:493
  66.9 0.6 collective-permute-done.6.tables1
  67.4 1.0 %locate.1.where = s32[16,128]{1,0:T(8,128)S(1)} custom-call(s32[4]{0:T(128)S(1)} %pad_add_fusion.place, s32[4,8,128]{2,1,0:T(8,128)S(1)} %get-tuple-element.37.tables0, s32[4,8,128]{2,1,0:T(8,128)S(1)} %collective-permute-done.6.tables1, s32[4,8,128]{2,1,0:T(8,128)S(1)} %collective-permute-done.7.tables2, s32[4,8,128]{2,1,0:T(8,128)S(1)} %collective-permute-done.8.tables3), custom_call_target="tpu_custom_call" | custom-call | bytes 65536 | tf_op jit(solution)/shard_map/locate/pallas_call | solution.py:435
  68.5 2.5 %all-to-all-done = bf16[64,24,128]{2,1,0:T(8,128)(2,1)S(1)} async-done(((bf16[64,24,128]{2,1,0:T(8,128)(2,1)}), bf16[64,24,128]{2,1,0:T(8,128)(2,1)S(1)}, u32[]{:S(2)}, u32[]{:S(2)}) %all-to-all-start) | async-done | bytes 393248 | tf_op jit(solution)/shard_map/all_to_all | solution.py:502
  71.0 1.7 %collect.1 = f32[16,1024]{1,0:T(8,128)} custom-call(s32[4]{0:T(128)S(1)} %pad_add_fusion.place, s32[16,128]{1,0:T(8,128)S(1)} %locate.1.where, bf16[1536,128]{1,0:T(8,128)(2,1)S(1)} %bitcast.7), custom_call_target="tpu_custom_call" | custom-call | tf_op jit(solution)/shard_map/collect/pallas_call | solution.py:464
Async XLA Ops:
  0.0 18.1 %collective-permute-start.5 = (bf16[64,32,128]{2,1,0:T(8,128)(2,1)}, bf16[64,32,128]{2,1,0:T(8,128)(2,1)S(1)}, u32[]{:S(2)}, u32[]{:S(2)}) collective-permute-start(bf16[64,32,128]{2,1,0:T(8,128)(2,1)} %bitcast.8), channel_id=1, source_target_pairs={{0,8},{1,33},{2,10},{3,35},{4,12},{5,37},{6,14},{7,39},{8,16},{9,4... | collective-permute-start | bytes 1572872 | tf_op jit(solution)/shard_map/ppermute | solution.py:482
  1.6 16.6 %collective-permute-start.4 = (bf16[64,32,128]{2,1,0:T(8,128)(2,1)}, bf16[64,32,128]{2,1,0:T(8,128)(2,1)S(1)}, u32[]{:S(2)}, u32[]{:S(2)}) collective-permute-start(bf16[64,32,128]{2,1,0:T(8,128)(2,1)} %bitcast.9), channel_id=1, source_target_pairs={{0,16},{1,65},{2,18},{3,67},{4,20},{5,69},{6,22},{7,71},{8,24},{9,... | collective-permute-start | bytes 1572872 | tf_op jit(solution)/shard_map/ppermute | solution.py:482
  4.3 13.9 %collective-permute-start.3 = (bf16[64,32,128]{2,1,0:T(8,128)(2,1)}, bf16[64,32,128]{2,1,0:T(8,128)(2,1)S(1)}, u32[]{:S(2)}, u32[]{:S(2)}) collective-permute-start(bf16[64,32,128]{2,1,0:T(8,128)(2,1)} %bitcast.10), channel_id=1, source_target_pairs={{0,24},{1,97},{2,26},{3,99},{4,28},{5,101},{6,30},{7,103},{8,0},{9... | collective-permute-start | bytes 1572872 | tf_op jit(solution)/shard_map/ppermute | solution.py:482
  6.6 0.7 copy-start
  8.3 5.3 %collective-permute-start = (s32[8,128]{1,0:T(8,128)S(1)}, s32[8,128]{1,0:T(8,128)S(1)}, u32[]{:S(2)}, u32[]{:S(2)}) collective-permute-start(s32[8,128]{1,0:T(8,128)S(1)} %get-tuple-element.31), channel_id=1, source_target_pairs={{0,32},{1,9},{2,34},{3,11},{4,36},{5,13},{6,38},{7,15},{8,40},{9,1... | collective-permute-start | bytes 12296 | tf_op jit(solution)/shard_map/ppermute | solution.py:486
  10.0 8.1 %collective-permute-start.1 = (s32[8,128]{1,0:T(8,128)S(1)}, s32[8,128]{1,0:T(8,128)S(1)}, u32[]{:S(2)}, u32[]{:S(2)}) collective-permute-start(s32[8,128]{1,0:T(8,128)S(1)} %get-tuple-element.32), channel_id=1, source_target_pairs={{0,64},{1,17},{2,66},{3,19},{4,68},{5,21},{6,70},{7,23},{8,72},{9,... | collective-permute-start | bytes 12296 | tf_op jit(solution)/shard_map/ppermute | solution.py:486
  13.6 4.5 %collective-permute-start.2 = (s32[8,128]{1,0:T(8,128)S(1)}, s32[8,128]{1,0:T(8,128)S(1)}, u32[]{:S(2)}, u32[]{:S(2)}) collective-permute-start(s32[8,128]{1,0:T(8,128)S(1)} %get-tuple-element.33), channel_id=1, source_target_pairs={{0,96},{1,25},{2,98},{3,27},{4,100},{5,29},{6,102},{7,31},{8,104},... | collective-permute-start | bytes 12296 | tf_op jit(solution)/shard_map/ppermute | solution.py:486
  19.4 9.6 %collective-permute-start.12 = (bf16[32,32,128]{2,1,0:T(8,128)(2,1)S(1)}, bf16[32,32,128]{2,1,0:T(8,128)(2,1)S(1)}, u32[]{:S(2)}, u32[]{:S(2)}) collective-permute-start(bf16[32,32,128]{2,1,0:T(8,128)(2,1)S(1)} %get-tuple-element.42), channel_id=1, source_target_pairs={{0,96},{1,25},{2,98},{3,27},{4,100},{5,29},{6,102},{7,31},{8,104},... | collective-permute-start | bytes 786440 | tf_op jit(solution)/shard_map/ppermute | solution.py:490
  22.0 8.0 %collective-permute-start.13 = (bf16[32,32,128]{2,1,0:T(8,128)(2,1)S(1)}, bf16[32,32,128]{2,1,0:T(8,128)(2,1)S(1)}, u32[]{:S(2)}, u32[]{:S(2)}) collective-permute-start(bf16[32,32,128]{2,1,0:T(8,128)(2,1)S(1)} %get-tuple-element.43), channel_id=1, source_target_pairs={{0,64},{1,17},{2,66},{3,19},{4,68},{5,21},{6,70},{7,23},{8,72},{9,... | collective-permute-start | bytes 786440 | tf_op jit(solution)/shard_map/ppermute | solution.py:490
  22.3 10.4 %collective-permute-start.14 = (bf16[32,32,128]{2,1,0:T(8,128)(2,1)S(1)}, bf16[32,32,128]{2,1,0:T(8,128)(2,1)S(1)}, u32[]{:S(2)}, u32[]{:S(2)}) collective-permute-start(bf16[32,32,128]{2,1,0:T(8,128)(2,1)S(1)} %get-tuple-element.44), channel_id=1, source_target_pairs={{0,32},{1,9},{2,34},{3,11},{4,36},{5,13},{6,38},{7,15},{8,40},{9,1... | collective-permute-start | bytes 786440 | tf_op jit(solution)/shard_map/ppermute | solution.py:490
  24.8 17.3 %collective-permute-start.9 = (bf16[32,32,128]{2,1,0:T(8,128)(2,1)S(1)}, bf16[32,32,128]{2,1,0:T(8,128)(2,1)S(1)}, u32[]{:S(2)}, u32[]{:S(2)}) collective-permute-start(bf16[32,32,128]{2,1,0:T(8,128)(2,1)S(1)} %get-tuple-element.38), channel_id=1, source_target_pairs={{0,96},{1,25},{2,98},{3,27},{4,100},{5,29},{6,102},{7,31},{8,104},... | collective-permute-start | bytes 786440 | tf_op jit(solution)/shard_map/ppermute | solution.py:492
  26.9 15.2 %collective-permute-start.10 = (bf16[32,32,128]{2,1,0:T(8,128)(2,1)S(1)}, bf16[32,32,128]{2,1,0:T(8,128)(2,1)S(1)}, u32[]{:S(2)}, u32[]{:S(2)}) collective-permute-start(bf16[32,32,128]{2,1,0:T(8,128)(2,1)S(1)} %get-tuple-element.39), channel_id=1, source_target_pairs={{0,64},{1,17},{2,66},{3,19},{4,68},{5,21},{6,70},{7,23},{8,72},{9,... | collective-permute-start | bytes 786440 | tf_op jit(solution)/shard_map/ppermute | solution.py:492
  29.0 13.1 %collective-permute-start.11 = (bf16[32,32,128]{2,1,0:T(8,128)(2,1)S(1)}, bf16[32,32,128]{2,1,0:T(8,128)(2,1)S(1)}, u32[]{:S(2)}, u32[]{:S(2)}) collective-permute-start(bf16[32,32,128]{2,1,0:T(8,128)(2,1)S(1)} %get-tuple-element.40), channel_id=1, source_target_pairs={{0,32},{1,9},{2,34},{3,11},{4,36},{5,13},{6,38},{7,15},{8,40},{9,1... | collective-permute-start | bytes 786440 | tf_op jit(solution)/shard_map/ppermute | solution.py:492
  46.0 1.8 %collective-permute-start.15 = (bf16[1536,128]{1,0:T(8,128)(2,1)S(1)}, bf16[1536,128]{1,0:T(8,128)(2,1)S(1)}, u32[]{:S(2)}, u32[]{:S(2)}) collective-permute-start(bf16[1536,128]{1,0:T(8,128)(2,1)S(1)} %get-tuple-element.54), channel_id=1, source_target_pairs={{0,1},{1,0},{2,3},{3,2},{4,5},{5,4},{6,7},{7,6},{8,9},{9,8},{10,11... | collective-permute-start | bytes 1179656 | tf_op jit(solution)/shard_map/ppermute | solution.py:500
  49.3 21.7 %all-to-all-start = ((bf16[64,24,128]{2,1,0:T(8,128)(2,1)}), bf16[64,24,128]{2,1,0:T(8,128)(2,1)S(1)}, u32[]{:S(2)}, u32[]{:S(2)}) async-start(bf16[64,24,128]{2,1,0:T(8,128)(2,1)} %bitcast.5), calls=%async_computation | async-start | bytes 786432 | tf_op jit(solution)/shard_map/all_to_all | solution.py:502
  58.8 6.2 %collective-permute-start.8 = (s32[4,8,128]{2,1,0:T(8,128)S(1)}, s32[4,8,128]{2,1,0:T(8,128)S(1)}, u32[]{:S(2)}, u32[]{:S(2)}) collective-permute-start(s32[4,8,128]{2,1,0:T(8,128)S(1)} %get-tuple-element.37.tables0), channel_id=1, source_target_pairs={{0,24},{1,97},{2,26},{3,99},{4,28},{5,101},{6,30},{7,103},{8,0},{9... | collective-permute-start | bytes 49160 | tf_op jit(solution)/shard_map/ppermute | solution.py:493
  61.6 5.2 %collective-permute-start.7 = (s32[4,8,128]{2,1,0:T(8,128)S(1)}, s32[4,8,128]{2,1,0:T(8,128)S(1)}, u32[]{:S(2)}, u32[]{:S(2)}) collective-permute-start(s32[4,8,128]{2,1,0:T(8,128)S(1)} %get-tuple-element.37.tables0), channel_id=1, source_target_pairs={{0,16},{1,65},{2,18},{3,67},{4,20},{5,69},{6,22},{7,71},{8,24},{9,... | collective-permute-start | bytes 49160 | tf_op jit(solution)/shard_map/ppermute | solution.py:493
  62.5 4.9 %collective-permute-start.6 = (s32[4,8,128]{2,1,0:T(8,128)S(1)}, s32[4,8,128]{2,1,0:T(8,128)S(1)}, u32[]{:S(2)}, u32[]{:S(2)}) collective-permute-start(s32[4,8,128]{2,1,0:T(8,128)S(1)} %get-tuple-element.37.tables0), channel_id=1, source_target_pairs={{0,8},{1,33},{2,10},{3,35},{4,12},{5,37},{6,14},{7,39},{8,16},{9,4... | collective-permute-start | bytes 49160 | tf_op jit(solution)/shard_map/ppermute | solution.py:493

commit v6 on v4

--- a/solution.py
+++ b/solution.py
@@ -145,36 +145,50 @@
 PAIRS = (2, MS // 2, 2 * OCC, 2 * OCC)
 
 
-def stage_kernel(tensor, own, picks, slots, count, held, own_out, staged, pairs, sems):
-    del picks, slots, count
-    copies = [
-        pltpu.make_async_copy(own, own_out, sems.at[0]),
-        pltpu.make_async_copy(tensor.at[0], held.at[0], sems.at[1]),
-    ]
-    for copy in copies:
-        copy.start()
+def stage_kernel(own, count, own_out, sem):
+    del count
+    copy = pltpu.make_async_copy(own, own_out, sem)
+    copy.start()
+    copy.wait()
+
+
+def stage(own, count):
+    return pl.pallas_call(
+        stage_kernel,
+        out_shape=pltpu.VMEM(own.shape, own.dtype),
+        in_specs=[HBM, VMEM],
+        out_specs=VMEM,
+        scratch_shapes=[pltpu.SemaphoreType.DMA],
+        compiler_params=pltpu.CompilerParams(vmem_limit_bytes=MIB),
+        cost_estimate=cost(0, MIB),
+        name="stage",
+    )(in_hbm(own), count)
+
+
+def head_kernel(tensor, after, held, staged, pairs, sem):
+    del after
+    copy = pltpu.make_async_copy(tensor.at[0], held.at[0], sem)
+    copy.start()
     staged[...] = jnp.zeros_like(staged)
     pairs[...] = jnp.zeros_like(pairs)
-    for copy in copies:
-        copy.wait()
-
-
-def stage(tensor, own, *lists):
-    return pl.pallas_call(
-        stage_kernel,
+    copy.wait()
+
+
+def head(tensor, after):
+    return pl.pallas_call(
+        head_kernel,
         out_shape=[
             pltpu.VMEM(tensor.shape, tensor.dtype),
-            pltpu.VMEM(own.shape, own.dtype),
             pltpu.VMEM(STAGED, jnp.float32),
             pltpu.VMEM(PAIRS, jnp.bfloat16),
         ],
-        in_specs=[HBM] * 2 + [SMEM] * 3,
-        out_specs=[VMEM] * 4,
-        scratch_shapes=[pltpu.SemaphoreType.DMA((2,))],
+        in_specs=[HBM, VMEM],
+        out_specs=[VMEM] * 3,
+        scratch_shapes=[pltpu.SemaphoreType.DMA],
         compiler_params=pltpu.CompilerParams(vmem_limit_bytes=MIB),
         cost_estimate=cost(0, 5 * MIB),
-        name="stage",
-    )(in_hbm(tensor), in_hbm(own), *lists)
+        name="head",
+    )(in_hbm(tensor), in_vmem(after))
 
 
 def pack_early_kernel(
@@ -483,10 +497,11 @@
     mine, *sent, picks, slots, count = plan(place, partners, pair_owner)
     received = [lax.ppermute(sent[j - 1], AXES, shifted(j, False)) for j in (1, 2, 3)]
 
-    held, here, staged, pairs = stage(three_center, own, picks, slots, count)
+    here = stage(own, count)
     *early, shards = pack_early(received, here, got)
     early = [lax.ppermute(early[j - 1], AXES, shifted(-j, False)) for j in (1, 2, 3)]
     row0, *late, tables = pack_late(mine, received, shards)
+    held, staged, pairs = head(three_center, row0)
     late = [lax.ppermute(late[j - 1], AXES, shifted(-j, False)) for j in (1, 2, 3)]
     every = [tables] + [lax.ppermute(tables, AXES, shifted(j, True)) for j in (1, 2, 3)]
 

time: 72.6 us -> 73.3 us (level)
  waiting for transfers between devices: 12.7 us -> 11.7 us
  starting transfers between devices: 34.3 us -> 35.2 us
  Pallas kernels: 23.6 us -> 24.5 us
    ppermute x3, waiting for transfers between devices: 3.67 us -> 1.44 us  [body(): lax.ppermute(early[j - 1], AXES, shifted(-j, False))]
    ppermute x3, waiting for transfers between devices: 0.75 us -> 1.78 us  [body(): lax.ppermute(sent[j - 1], AXES, shifted(j, False))]
    ppermute x3, starting transfers between devices: 4.12 us -> 4.93 us  [body(): lax.ppermute(early[j - 1], AXES, shifted(-j, False))]
    pallas_call x1 -> x2, Pallas kernels: 2.98 us -> 3.25 us  [the longest x1 2.2 us: head(): pl.pallas_call(head_kernel, out_shape=[pltpu.VMEM(tensor.shape, tensor.dt...]
  transfers between devices with their start and end apart: 17 -> 17, of which waited for: 8 -> 9; matrix products, arithmetic and copies ran while one was open for 1% -> 1% of each run, Pallas kernels for 22% -> 22%
where the time goes in v6:
time: 73.3 us; the launch traced here: 73 us
  starting transfers between devices  35.2 us (48%)
  Pallas kernels  24.5 us (33%)
  waiting for transfers between devices  11.7 us (16%)
  local copies, waits for them, and re-layouts  1.47 us (2%)
    all_to_all x1, starting transfers between devices, body(): lax.all_to_all(outgoing, AXES, split_axis=0, concat_axis=0, axis_index_gr...  9.93 us
    pallas_call x1, Pallas kernels, early_products(): pl.pallas_call(early_kernel, out_shape=STATE, in_specs=[SMEM] * 3 + [VMEM...  9.69 us
    ppermute x3, starting transfers between devices, body(): lax.ppermute(sent[j - 1], AXES, shifted(j, False))  6.05 us
    ppermute x3, starting transfers between devices, body(): got = [lax.ppermute(own, AXES, shifted(-j, True)) for j in (1, 2, 3)]  5.74 us
    ppermute x3, starting transfers between devices, body(): lax.ppermute(early[j - 1], AXES, shifted(-j, False))  4.93 us
    ppermute x3, starting transfers between devices, body(): lax.ppermute(tables, AXES, shifted(j, True))  4.57 us
    ppermute x3, waiting for transfers between devices, body(): lax.ppermute(tables, AXES, shifted(j, True))  4.09 us
    pallas_call x1, Pallas kernels, late_products(): pl.pallas_call(late_kernel, out_shape=STATE + [jax.ShapeDtypeStruct((SIDE...  4.01 us
  transfers between devices with their start and end apart: 17, of which 9 were waited for; matrix products, arithmetic and copies ran while one was open for 1% of the time, Pallas kernels for 22%

profile of v6, /device:TPU:0, one launch (start us, length us, event | category | flops | bytes accessed | tf_op | source)
XLA Modules:
  0.0 73.0 jit_solution(10800371897858710854)
XLA Ops:
  0.0 1.6 %collective-permute-start.5 = (bf16[64,32,128]{2,1,0:T(8,128)(2,1)}, bf16[64,32,128]{2,1,0:T(8,128)(2,1)S(1)}, u32[]{:S(2)}, u32[]{:S(2)}) collective-permute-start(bf16[64,32,128]{2,1,0:T(8,128)(2,1)} %bitcast.8), channel_id=1, source_target_pairs={{0,8},{1,33},{2,10},{3,35},{4,12},{5,37},{6,14},{7,39},{8,16},{9,4... | collective-permute-start | bytes 1572872 | tf_op jit(solution)/shard_map/ppermute | solution.py:494
  1.6 2.7 %collective-permute-start.4 = (bf16[64,32,128]{2,1,0:T(8,128)(2,1)}, bf16[64,32,128]{2,1,0:T(8,128)(2,1)S(1)}, u32[]{:S(2)}, u32[]{:S(2)}) collective-permute-start(bf16[64,32,128]{2,1,0:T(8,128)(2,1)} %bitcast.9), channel_id=1, source_target_pairs={{0,16},{1,65},{2,18},{3,67},{4,20},{5,69},{6,22},{7,71},{8,24},{9,... | collective-permute-start | bytes 1572872 | tf_op jit(solution)/shard_map/ppermute | solution.py:494
  4.3 1.4 %collective-permute-start.3 = (bf16[64,32,128]{2,1,0:T(8,128)(2,1)}, bf16[64,32,128]{2,1,0:T(8,128)(2,1)S(1)}, u32[]{:S(2)}, u32[]{:S(2)}) collective-permute-start(bf16[64,32,128]{2,1,0:T(8,128)(2,1)} %bitcast.10), channel_id=1, source_target_pairs={{0,24},{1,97},{2,26},{3,99},{4,28},{5,101},{6,30},{7,103},{8,0},{9... | collective-permute-start | bytes 1572872 | tf_op jit(solution)/shard_map/ppermute | solution.py:494
  5.7 0.8 %copy.13.partners = s32[4,8,4]{2,1,0:T(8,128)S(1)} copy(s32[4,8,4]{1,2,0:T(4,128)} %param.6) | data formatting | bytes 1024 | tf_op args[2]
  6.5 0.1 pad_add_fusion.place
  6.6 0.0 copy-start
  6.6 0.7 copy-done
  7.3 1.1 %plan.1 = (s32[8,128]{1,0:T(8,128)S(1)}, s32[8,128]{1,0:T(8,128)S(1)}, s32[8,128]{1,0:T(8,128)S(1)}, s32[8,128]{1,0:T(8,128)S(1)}, s32[1,128]{1,0:T(1,128)S(1)},...) custom-call(s32[4]{0:T(128)S(1)} %pad_add_fusion.place, s32[4,8,4]{2,1,0:T(8,128)S(1)} %copy.13.partners, s32[4,56]{1,0:T(4,128)S(1)} %copy-done), custom_call_target="tpu_custom_call" | custom-call | bytes 65536 | tf_op jit(solution)/shard_map/plan/pallas_call | solution.py:133
  8.3 1.6 %collective-permute-start = (s32[8,128]{1,0:T(8,128)S(1)}, s32[8,128]{1,0:T(8,128)S(1)}, u32[]{:S(2)}, u32[]{:S(2)}) collective-permute-start(s32[8,128]{1,0:T(8,128)S(1)} %get-tuple-element.32), channel_id=1, source_target_pairs={{0,32},{1,9},{2,34},{3,11},{4,36},{5,13},{6,38},{7,15},{8,40},{9,1... | collective-permute-start | bytes 12296 | tf_op jit(solution)/shard_map/ppermute | solution.py:498
  10.0 2.9 %collective-permute-start.1 = (s32[8,128]{1,0:T(8,128)S(1)}, s32[8,128]{1,0:T(8,128)S(1)}, u32[]{:S(2)}, u32[]{:S(2)}) collective-permute-start(s32[8,128]{1,0:T(8,128)S(1)} %get-tuple-element.33), channel_id=1, source_target_pairs={{0,64},{1,17},{2,66},{3,19},{4,68},{5,21},{6,70},{7,23},{8,72},{9,... | collective-permute-start | bytes 12296 | tf_op jit(solution)/shard_map/ppermute | solution.py:498
  12.9 0.7 %collective-permute-done.req1.tab1 = s32[8,128]{1,0:T(8,128)S(1)} collective-permute-done((s32[8,128]{1,0:T(8,128)S(1)}, s32[8,128]{1,0:T(8,128)S(1)}, u32[]{:S(2)}, u32[]{:S(2)}) %collective-permute-start) | collective-permute-done | bytes 4128 | tf_op jit(solution)/shard_map/ppermute | solution.py:498
  13.6 1.5 %collective-permute-start.2 = (s32[8,128]{1,0:T(8,128)S(1)}, s32[8,128]{1,0:T(8,128)S(1)}, u32[]{:S(2)}, u32[]{:S(2)}) collective-permute-start(s32[8,128]{1,0:T(8,128)S(1)} %get-tuple-element.34), channel_id=1, source_target_pairs={{0,96},{1,25},{2,98},{3,27},{4,100},{5,29},{6,102},{7,31},{8,104},... | collective-permute-start | bytes 12296 | tf_op jit(solution)/shard_map/ppermute | solution.py:498
  15.1 1.0 %stage.1.own = bf16[64,32,128]{2,1,0:T(8,128)(2,1)S(1)} custom-call(bf16[64,32,128]{2,1,0:T(8,128)(2,1)} %bitcast.11, s32[1,128]{1,0:T(1,128)S(1)} %get-tuple-element.35.count), custom_call_target="tpu_custom_call" | custom-call | bytes 1048576 | tf_op jit(solution)/shard_map/stage/pallas_call | solution.py:156
  16.2 0.0 collective-permute-done.1.req2.tab2
  16.2 1.0 %collective-permute-done.2.req3.tab3 = s32[8,128]{1,0:T(8,128)S(1)} collective-permute-done((s32[8,128]{1,0:T(8,128)S(1)}, s32[8,128]{1,0:T(8,128)S(1)}, u32[]{:S(2)}, u32[]{:S(2)}) %collective-permute-start.2) | collective-permute-done | bytes 4128 | tf_op jit(solution)/shard_map/ppermute | solution.py:498
  17.2 0.0 collective-permute-done.5.got3
  17.2 0.1 collective-permute-done.4.got2
  17.4 0.0 collective-permute-done.3.got1
  17.4 1.2 %pack_early.1 = (bf16[32,32,128]{2,1,0:T(8,128)(2,1)S(1)}, bf16[32,32,128]{2,1,0:T(8,128)(2,1)S(1)}, bf16[32,32,128]{2,1,0:T(8,128)(2,1)S(1)}, bf16[256,32,128]{2,1,0:T(8,128)(2,1)S(1)}) custom-call(s32[8,128]{1,0:T(8,128)S(1)} %collective-permute-done.req1.tab1, s32[8,128]{1,0:T(8,128)S(1)} %collective-permute-done.1.req2.tab2, ...), custom_call_target="tpu_custom_call" | custom-call | bytes 4194304 | tf_op jit(solution)/shard_map/pack_early/pallas_call | solution.py:211
  18.6 3.1 %collective-permute-start.12 = (bf16[32,32,128]{2,1,0:T(8,128)(2,1)S(1)}, bf16[32,32,128]{2,1,0:T(8,128)(2,1)S(1)}, u32[]{:S(2)}, u32[]{:S(2)}) collective-permute-start(bf16[32,32,128]{2,1,0:T(8,128)(2,1)S(1)} %get-tuple-element.44), channel_id=1, source_target_pairs={{0,96},{1,25},{2,98},{3,27},{4,100},{5,29},{6,102},{7,31},{8,104},... | collective-permute-start | bytes 786440 | tf_op jit(solution)/shard_map/ppermute | solution.py:502
  21.6 0.6 collective-permute-start.13
  22.3 1.2 %collective-permute-start.14 = (bf16[32,32,128]{2,1,0:T(8,128)(2,1)S(1)}, bf16[32,32,128]{2,1,0:T(8,128)(2,1)S(1)}, u32[]{:S(2)}, u32[]{:S(2)}) collective-permute-start(bf16[32,32,128]{2,1,0:T(8,128)(2,1)S(1)} %get-tuple-element.46), channel_id=1, source_target_pairs={{0,32},{1,9},{2,34},{3,11},{4,36},{5,13},{6,38},{7,15},{8,40},{9,1... | collective-permute-start | bytes 786440 | tf_op jit(solution)/shard_map/ppermute | solution.py:502
  23.5 1.3 %pack_late.1 = (bf16[64,32,128]{2,1,0:T(8,128)(2,1)S(1)}, bf16[32,32,128]{2,1,0:T(8,128)(2,1)S(1)}, bf16[32,32,128]{2,1,0:T(8,128)(2,1)S(1)}, bf16[32,32,128]{2,1,0:T(8,128)(2,1)S(1)}, s32[4,8,128]{2,1,0:T(8,128)S(1)}) custom-call(s32[8,128]{1,0:T(8,128)S(1)} %get-tuple-element.31.req0.mine, s32[8,128]{1,0:T(8,128)S(1)} %collective-permute-done.req1.tab1, ...), custom_call_target="tpu_custom_call" | custom-call | bytes 2097152 | tf_op jit(solution)/shard_map/pack_late/pallas_call | solution.py:239
  24.8 2.1 %collective-permute-start.9 = (bf16[32,32,128]{2,1,0:T(8,128)(2,1)S(1)}, bf16[32,32,128]{2,1,0:T(8,128)(2,1)S(1)}, u32[]{:S(2)}, u32[]{:S(2)}) collective-permute-start(bf16[32,32,128]{2,1,0:T(8,128)(2,1)S(1)} %get-tuple-element.40), channel_id=1, source_target_pairs={{0,96},{1,25},{2,98},{3,27},{4,100},{5,29},{6,102},{7,31},{8,104},... | collective-permute-start | bytes 786440 | tf_op jit(solution)/shard_map/ppermute | solution.py:505
  26.9 1.7 %collective-permute-start.10 = (bf16[32,32,128]{2,1,0:T(8,128)(2,1)S(1)}, bf16[32,32,128]{2,1,0:T(8,128)(2,1)S(1)}, u32[]{:S(2)}, u32[]{:S(2)}) collective-permute-start(bf16[32,32,128]{2,1,0:T(8,128)(2,1)S(1)} %get-tuple-element.41), channel_id=1, source_target_pairs={{0,64},{1,17},{2,66},{3,19},{4,68},{5,21},{6,70},{7,23},{8,72},{9,... | collective-permute-start | bytes 786440 | tf_op jit(solution)/shard_map/ppermute | solution.py:505
  28.6 2.2 %head.1 = (bf16[4,8,64,32,128]{4,3,2,1,0:T(8,128)(2,1)S(1)}, f32[385,8,128]{2,1,0:T(8,128)S(1)}, bf16[2,4,256,256]{3,2,1,0:T(8,128)(2,1)S(1)}) custom-call(bf16[4,8,64,32,128]{4,3,2,1,0:T(8,128)(2,1)} %tensor.3, bf16[64,32,128]{2,1,0:T(8,128)(2,1)S(1)} %get-tuple-element.43.after.row0), custom_call_target="tpu_custom_call" | custom-call | bytes 5242880 | tf_op jit(solution)/shard_map/head/pallas_call | solution.py:178
  30.8 0.0 collective-permute-done.12.row1
  30.8 0.1 collective-permute-start.11
  30.9 0.0 collective-permute-done.13.row2
  30.9 1.4 %collective-permute-done.14.row3 = bf16[32,32,128]{2,1,0:T(8,128)(2,1)S(1)} collective-permute-done((bf16[32,32,128]{2,1,0:T(8,128)(2,1)S(1)}, bf16[32,32,128]{2,1,0:T(8,128)(2,1)S(1)}, u32[]{:S(2)}, u32[]{:S(2)}) %collective-permute-start.14) | collective-permute-done | bytes 262176 | tf_op jit(solution)/shard_map/ppermute | solution.py:502
  32.3 9.7 %early_products.1 = (f32[385,8,128]{2,1,0:T(8,128)S(1)}, bf16[2,4,256,256]{3,2,1,0:T(8,128)(2,1)S(1)}, bf16[4,8,64,32,128]{4,3,2,1,0:T(8,128)(2,1)S(1)}, bf16[25...) custom-call(s32[1,128]{1,0:T(1,128)S(1)} %get-tuple-element.35.count, ...), custom_call_target="tpu_custom_call", output_to_operand_aliasing={{0}: (8, {}), {1}: (9, {}), {2}: (10, {})} | custom-call | flops 4294967296 | bytes 8388608 | tf_op jit(solution)/shard_map/early_products/pallas_call | solution.py:400
  42.0 0.0 collective-permute-done.9.late1
  42.0 0.0 collective-permute-done.10.late2
  42.0 0.0 collective-permute-done.11.late3
  42.1 4.0 %late_products.1 = (f32[385,8,128]{2,1,0:T(8,128)S(1)}, bf16[2,4,256,256]{3,2,1,0:T(8,128)(2,1)S(1)}, bf16[4,8,64,32,128]{4,3,2,1,0:T(8,128)(2,1)S(1)}, bf16[256...) custom-call(s32[4]{0:T(128)S(1)} %pad_add_fusion.place, ...), custom_call_target="tpu_custom_call", output_to_operand_aliasing={{0}: (7, {}), {1}: (8, {}), {2}: (9, {}), {3}: (10, {}), {4... | custom-call | flops 4294967296 | bytes 8388608 | tf_op jit(solution)/shard_map/late_products/pallas_call | solution.py:414
  46.1 0.1 collective-permute-start.15
  46.2 1.7 %collective-permute-done.15.came = bf16[1536,128]{1,0:T(8,128)(2,1)S(1)} collective-permute-done((bf16[1536,128]{1,0:T(8,128)(2,1)S(1)}, bf16[1536,128]{1,0:T(8,128)(2,1)S(1)}, u32[]{:S(2)}, u32[]{:S(2)}) %collective-permute-start.15) | collective-permute-done | bytes 393248 | tf_op jit(solution)/shard_map/ppermute | solution.py:513
  47.9 1.4 %join.1 = bf16[1536,128]{1,0:T(8,128)(2,1)} custom-call(s32[4]{0:T(128)S(1)} %pad_add_fusion.place, f32[385,8,128]{2,1,0:T(8,128)S(1)} %get-tuple-element.55.staged, bf16[1536,128]{1,0:T(8,128)(2,1)S(1)} %collective-permute-done.15.came), custom_call_target="tpu_custom_call" | custom-call | bytes 2097152 | tf_op jit(solution)/shard_map/join/pallas_call | solution.py:377
  49.2 9.9 %all-to-all-start = ((bf16[64,24,128]{2,1,0:T(8,128)(2,1)}), bf16[64,24,128]{2,1,0:T(8,128)(2,1)S(1)}, u32[]{:S(2)}, u32[]{:S(2)}) async-start(bf16[64,24,128]{2,1,0:T(8,128)(2,1)} %bitcast.5), calls=%async_computation | async-start | bytes 786432 | tf_op jit(solution)/shard_map/all_to_all | solution.py:515
  59.2 2.9 %collective-permute-start.8 = (s32[4,8,128]{2,1,0:T(8,128)S(1)}, s32[4,8,128]{2,1,0:T(8,128)S(1)}, u32[]{:S(2)}, u32[]{:S(2)}) collective-permute-start(s32[4,8,128]{2,1,0:T(8,128)S(1)} %get-tuple-element.37.tables0), channel_id=1, source_target_pairs={{0,24},{1,97},{2,26},{3,99},{4,28},{5,101},{6,30},{7,103},{8,0},{9... | collective-permute-start | bytes 49160 | tf_op jit(solution)/shard_map/ppermute | solution.py:506
  62.0 0.9 %collective-permute-start.7 = (s32[4,8,128]{2,1,0:T(8,128)S(1)}, s32[4,8,128]{2,1,0:T(8,128)S(1)}, u32[]{:S(2)}, u32[]{:S(2)}) collective-permute-start(s32[4,8,128]{2,1,0:T(8,128)S(1)} %get-tuple-element.37.tables0), channel_id=1, source_target_pairs={{0,16},{1,65},{2,18},{3,67},{4,20},{5,69},{6,22},{7,71},{8,24},{9,... | collective-permute-start | bytes 49160 | tf_op jit(solution)/shard_map/ppermute | solution.py:506
  62.9 0.9 %collective-permute-start.6 = (s32[4,8,128]{2,1,0:T(8,128)S(1)}, s32[4,8,128]{2,1,0:T(8,128)S(1)}, u32[]{:S(2)}, u32[]{:S(2)}) collective-permute-start(s32[4,8,128]{2,1,0:T(8,128)S(1)} %get-tuple-element.37.tables0), channel_id=1, source_target_pairs={{0,8},{1,33},{2,10},{3,35},{4,12},{5,37},{6,14},{7,39},{8,16},{9,4... | collective-permute-start | bytes 49160 | tf_op jit(solution)/shard_map/ppermute | solution.py:506
  63.7 1.7 %collective-permute-done.8.tables3 = s32[4,8,128]{2,1,0:T(8,128)S(1)} collective-permute-done((s32[4,8,128]{2,1,0:T(8,128)S(1)}, s32[4,8,128]{2,1,0:T(8,128)S(1)}, u32[]{:S(2)}, u32[]{:S(2)}) %collective-permute-start.8) | collective-permute-done | bytes 16416 | tf_op jit(solution)/shard_map/ppermute | solution.py:506
  65.4 1.9 %collective-permute-done.7.tables2 = s32[4,8,128]{2,1,0:T(8,128)S(1)} collective-permute-done((s32[4,8,128]{2,1,0:T(8,128)S(1)}, s32[4,8,128]{2,1,0:T(8,128)S(1)}, u32[]{:S(2)}, u32[]{:S(2)}) %collective-permute-start.7) | collective-permute-done | bytes 16416 | tf_op jit(solution)/shard_map/ppermute | solution.py:506
  67.3 0.6 collective-permute-done.6.tables1
  67.8 1.0 %locate.1.where = s32[16,128]{1,0:T(8,128)S(1)} custom-call(s32[4]{0:T(128)S(1)} %pad_add_fusion.place, s32[4,8,128]{2,1,0:T(8,128)S(1)} %get-tuple-element.37.tables0, s32[4,8,128]{2,1,0:T(8,128)S(1)} %collective-permute-done.6.tables1, s32[4,8,128]{2,1,0:T(8,128)S(1)} %collective-permute-done.7.tables2, s32[4,8,128]{2,1,0:T(8,128)S(1)} %collective-permute-done.8.tables3), custom_call_target="tpu_custom_call" | custom-call | bytes 65536 | tf_op jit(solution)/shard_map/locate/pallas_call | solution.py:447
  68.9 2.5 %all-to-all-done = bf16[64,24,128]{2,1,0:T(8,128)(2,1)S(1)} async-done(((bf16[64,24,128]{2,1,0:T(8,128)(2,1)}), bf16[64,24,128]{2,1,0:T(8,128)(2,1)S(1)}, u32[]{:S(2)}, u32[]{:S(2)}) %all-to-all-start) | async-done | bytes 393248 | tf_op jit(solution)/shard_map/all_to_all | solution.py:515
  71.4 1.7 %collect.1 = f32[16,1024]{1,0:T(8,128)} custom-call(s32[4]{0:T(128)S(1)} %pad_add_fusion.place, s32[16,128]{1,0:T(8,128)S(1)} %locate.1.where, bf16[1536,128]{1,0:T(8,128)(2,1)S(1)} %bitcast.7), custom_call_target="tpu_custom_call" | custom-call | tf_op jit(solution)/shard_map/collect/pallas_call | solution.py:476
Async XLA Ops:
  0.0 17.2 %collective-permute-start.5 = (bf16[64,32,128]{2,1,0:T(8,128)(2,1)}, bf16[64,32,128]{2,1,0:T(8,128)(2,1)S(1)}, u32[]{:S(2)}, u32[]{:S(2)}) collective-permute-start(bf16[64,32,128]{2,1,0:T(8,128)(2,1)} %bitcast.8), channel_id=1, source_target_pairs={{0,8},{1,33},{2,10},{3,35},{4,12},{5,37},{6,14},{7,39},{8,16},{9,4... | collective-permute-start | bytes 1572872 | tf_op jit(solution)/shard_map/ppermute | solution.py:494
  1.6 15.8 %collective-permute-start.4 = (bf16[64,32,128]{2,1,0:T(8,128)(2,1)}, bf16[64,32,128]{2,1,0:T(8,128)(2,1)S(1)}, u32[]{:S(2)}, u32[]{:S(2)}) collective-permute-start(bf16[64,32,128]{2,1,0:T(8,128)(2,1)} %bitcast.9), channel_id=1, source_target_pairs={{0,16},{1,65},{2,18},{3,67},{4,20},{5,69},{6,22},{7,71},{8,24},{9,... | collective-permute-start | bytes 1572872 | tf_op jit(solution)/shard_map/ppermute | solution.py:494
  4.3 13.1 %collective-permute-start.3 = (bf16[64,32,128]{2,1,0:T(8,128)(2,1)}, bf16[64,32,128]{2,1,0:T(8,128)(2,1)S(1)}, u32[]{:S(2)}, u32[]{:S(2)}) collective-permute-start(bf16[64,32,128]{2,1,0:T(8,128)(2,1)} %bitcast.10), channel_id=1, source_target_pairs={{0,24},{1,97},{2,26},{3,99},{4,28},{5,101},{6,30},{7,103},{8,0},{9... | collective-permute-start | bytes 1572872 | tf_op jit(solution)/shard_map/ppermute | solution.py:494
  6.6 0.7 copy-start
  8.3 5.3 %collective-permute-start = (s32[8,128]{1,0:T(8,128)S(1)}, s32[8,128]{1,0:T(8,128)S(1)}, u32[]{:S(2)}, u32[]{:S(2)}) collective-permute-start(s32[8,128]{1,0:T(8,128)S(1)} %get-tuple-element.32), channel_id=1, source_target_pairs={{0,32},{1,9},{2,34},{3,11},{4,36},{5,13},{6,38},{7,15},{8,40},{9,1... | collective-permute-start | bytes 12296 | tf_op jit(solution)/shard_map/ppermute | solution.py:498
  10.0 6.2 %collective-permute-start.1 = (s32[8,128]{1,0:T(8,128)S(1)}, s32[8,128]{1,0:T(8,128)S(1)}, u32[]{:S(2)}, u32[]{:S(2)}) collective-permute-start(s32[8,128]{1,0:T(8,128)S(1)} %get-tuple-element.33), channel_id=1, source_target_pairs={{0,64},{1,17},{2,66},{3,19},{4,68},{5,21},{6,70},{7,23},{8,72},{9,... | collective-permute-start | bytes 12296 | tf_op jit(solution)/shard_map/ppermute | solution.py:498
  13.6 3.6 %collective-permute-start.2 = (s32[8,128]{1,0:T(8,128)S(1)}, s32[8,128]{1,0:T(8,128)S(1)}, u32[]{:S(2)}, u32[]{:S(2)}) collective-permute-start(s32[8,128]{1,0:T(8,128)S(1)} %get-tuple-element.34), channel_id=1, source_target_pairs={{0,96},{1,25},{2,98},{3,27},{4,100},{5,29},{6,102},{7,31},{8,104},... | collective-permute-start | bytes 12296 | tf_op jit(solution)/shard_map/ppermute | solution.py:498
  18.6 12.2 %collective-permute-start.12 = (bf16[32,32,128]{2,1,0:T(8,128)(2,1)S(1)}, bf16[32,32,128]{2,1,0:T(8,128)(2,1)S(1)}, u32[]{:S(2)}, u32[]{:S(2)}) collective-permute-start(bf16[32,32,128]{2,1,0:T(8,128)(2,1)S(1)} %get-tuple-element.44), channel_id=1, source_target_pairs={{0,96},{1,25},{2,98},{3,27},{4,100},{5,29},{6,102},{7,31},{8,104},... | collective-permute-start | bytes 786440 | tf_op jit(solution)/shard_map/ppermute | solution.py:502
  21.6 9.2 %collective-permute-start.13 = (bf16[32,32,128]{2,1,0:T(8,128)(2,1)S(1)}, bf16[32,32,128]{2,1,0:T(8,128)(2,1)S(1)}, u32[]{:S(2)}, u32[]{:S(2)}) collective-permute-start(bf16[32,32,128]{2,1,0:T(8,128)(2,1)S(1)} %get-tuple-element.45), channel_id=1, source_target_pairs={{0,64},{1,17},{2,66},{3,19},{4,68},{5,21},{6,70},{7,23},{8,72},{9,... | collective-permute-start | bytes 786440 | tf_op jit(solution)/shard_map/ppermute | solution.py:502
  22.3 10.1 %collective-permute-start.14 = (bf16[32,32,128]{2,1,0:T(8,128)(2,1)S(1)}, bf16[32,32,128]{2,1,0:T(8,128)(2,1)S(1)}, u32[]{:S(2)}, u32[]{:S(2)}) collective-permute-start(bf16[32,32,128]{2,1,0:T(8,128)(2,1)S(1)} %get-tuple-element.46), channel_id=1, source_target_pairs={{0,32},{1,9},{2,34},{3,11},{4,36},{5,13},{6,38},{7,15},{8,40},{9,1... | collective-permute-start | bytes 786440 | tf_op jit(solution)/shard_map/ppermute | solution.py:502
  24.8 17.2 %collective-permute-start.9 = (bf16[32,32,128]{2,1,0:T(8,128)(2,1)S(1)}, bf16[32,32,128]{2,1,0:T(8,128)(2,1)S(1)}, u32[]{:S(2)}, u32[]{:S(2)}) collective-permute-start(bf16[32,32,128]{2,1,0:T(8,128)(2,1)S(1)} %get-tuple-element.40), channel_id=1, source_target_pairs={{0,96},{1,25},{2,98},{3,27},{4,100},{5,29},{6,102},{7,31},{8,104},... | collective-permute-start | bytes 786440 | tf_op jit(solution)/shard_map/ppermute | solution.py:505
  26.9 15.2 %collective-permute-start.10 = (bf16[32,32,128]{2,1,0:T(8,128)(2,1)S(1)}, bf16[32,32,128]{2,1,0:T(8,128)(2,1)S(1)}, u32[]{:S(2)}, u32[]{:S(2)}) collective-permute-start(bf16[32,32,128]{2,1,0:T(8,128)(2,1)S(1)} %get-tuple-element.41), channel_id=1, source_target_pairs={{0,64},{1,17},{2,66},{3,19},{4,68},{5,21},{6,70},{7,23},{8,72},{9,... | collective-permute-start | bytes 786440 | tf_op jit(solution)/shard_map/ppermute | solution.py:505
  30.8 11.3 %collective-permute-start.11 = (bf16[32,32,128]{2,1,0:T(8,128)(2,1)S(1)}, bf16[32,32,128]{2,1,0:T(8,128)(2,1)S(1)}, u32[]{:S(2)}, u32[]{:S(2)}) collective-permute-start(bf16[32,32,128]{2,1,0:T(8,128)(2,1)S(1)} %get-tuple-element.42), channel_id=1, source_target_pairs={{0,32},{1,9},{2,34},{3,11},{4,36},{5,13},{6,38},{7,15},{8,40},{9,1... | collective-permute-start | bytes 786440 | tf_op jit(solution)/shard_map/ppermute | solution.py:505
  46.1 1.8 %collective-permute-start.15 = (bf16[1536,128]{1,0:T(8,128)(2,1)S(1)}, bf16[1536,128]{1,0:T(8,128)(2,1)S(1)}, u32[]{:S(2)}, u32[]{:S(2)}) collective-permute-start(bf16[1536,128]{1,0:T(8,128)(2,1)S(1)} %get-tuple-element.56), channel_id=1, source_target_pairs={{0,1},{1,0},{2,3},{3,2},{4,5},{5,4},{6,7},{7,6},{8,9},{9,8},{10,11... | collective-permute-start | bytes 1179656 | tf_op jit(solution)/shard_map/ppermute | solution.py:513
  49.2 22.1 %all-to-all-start = ((bf16[64,24,128]{2,1,0:T(8,128)(2,1)}), bf16[64,24,128]{2,1,0:T(8,128)(2,1)S(1)}, u32[]{:S(2)}, u32[]{:S(2)}) async-start(bf16[64,24,128]{2,1,0:T(8,128)(2,1)} %bitcast.5), calls=%async_computation | async-start | bytes 786432 | tf_op jit(solution)/shard_map/all_to_all | solution.py:515
  59.2 6.2 %collective-permute-start.8 = (s32[4,8,128]{2,1,0:T(8,128)S(1)}, s32[4,8,128]{2,1,0:T(8,128)S(1)}, u32[]{:S(2)}, u32[]{:S(2)}) collective-permute-start(s32[4,8,128]{2,1,0:T(8,128)S(1)} %get-tuple-element.37.tables0), channel_id=1, source_target_pairs={{0,24},{1,97},{2,26},{3,99},{4,28},{5,101},{6,30},{7,103},{8,0},{9... | collective-permute-start | bytes 49160 | tf_op jit(solution)/shard_map/ppermute | solution.py:506
  62.0 5.2 %collective-permute-start.7 = (s32[4,8,128]{2,1,0:T(8,128)S(1)}, s32[4,8,128]{2,1,0:T(8,128)S(1)}, u32[]{:S(2)}, u32[]{:S(2)}) collective-permute-start(s32[4,8,128]{2,1,0:T(8,128)S(1)} %get-tuple-element.37.tables0), channel_id=1, source_target_pairs={{0,16},{1,65},{2,18},{3,67},{4,20},{5,69},{6,22},{7,71},{8,24},{9,... | collective-permute-start | bytes 49160 | tf_op jit(solution)/shard_map/ppermute | solution.py:506
  62.9 4.9 %collective-permute-start.6 = (s32[4,8,128]{2,1,0:T(8,128)S(1)}, s32[4,8,128]{2,1,0:T(8,128)S(1)}, u32[]{:S(2)}, u32[]{:S(2)}) collective-permute-start(s32[4,8,128]{2,1,0:T(8,128)S(1)} %get-tuple-element.37.tables0), channel_id=1, source_target_pairs={{0,8},{1,33},{2,10},{3,35},{4,12},{5,37},{6,14},{7,39},{8,16},{9,4... | collective-permute-start | bytes 49160 | tf_op jit(solution)/shard_map/ppermute | solution.py:506

commit v7 on v4

--- a/solution.py
+++ b/solution.py
@@ -493,6 +493,7 @@
     state = early_products(
         count, picks, slots, (row0, *early), three_center, staged, pairs, held
     )
+    every, state = lax.optimization_barrier((every, state))
     state = late_products(place, count, picks, slots, late, state)
     swap = [(device, device ^ 1) for device in range(DEVS)]
     outgoing = join(place, state[0], lax.ppermute(state[5], AXES, swap))

time: 72.6 us -> 77.1 us (1.062)
  starting transfers between devices: 34.3 us -> 37.3 us
  waiting for transfers between devices: 12.7 us -> 14.2 us
    all_to_all x1, waiting for transfers between devices: 2.51 us -> 11.2 us  [body(): lax.all_to_all(outgoing, AXES, split_axis=0, concat_axis=0, axis_index_gr...]
    ppermute x3, waiting for transfers between devices: 3.67 us -> 0.01 us  [body(): lax.ppermute(early[j - 1], AXES, shifted(-j, False))]
    ppermute x3, waiting for transfers between devices: 4.09 us -> 0.53 us  [body(): lax.ppermute(tables, AXES, shifted(j, True))]
    all_to_all x1, starting transfers between devices: 9.52 us -> 12.4 us  [body(): lax.all_to_all(outgoing, AXES, split_axis=0, concat_axis=0, axis_index_gr...]
  transfers between devices with their start and end apart: 17 -> 17, of which waited for: 8 -> 4; matrix products, arithmetic and copies ran while one was open for 1% -> 1% of each run, Pallas kernels for 22% -> 20%
where the time goes in v7:
time: 77.1 us; the launch traced here: 76.8 us
  starting transfers between devices  37.3 us (48%)
  Pallas kernels  23.6 us (31%)
  waiting for transfers between devices  14.2 us (18%)
  local copies, waits for them, and re-layouts  1.47 us (2%)
    all_to_all x1, starting transfers between devices, body(): lax.all_to_all(outgoing, AXES, split_axis=0, concat_axis=0, axis_index_gr...  12.4 us
    all_to_all x1, waiting for transfers between devices, body(): lax.all_to_all(outgoing, AXES, split_axis=0, concat_axis=0, axis_index_gr...  11.2 us
    pallas_call x1, Pallas kernels, early_products(): pl.pallas_call(early_kernel, out_shape=STATE, in_specs=[SMEM] * 3 + [VMEM...  9.2 us
    ppermute x3, starting transfers between devices, body(): lax.ppermute(sent[j - 1], AXES, shifted(j, False))  6.05 us
    ppermute x3, starting transfers between devices, body(): got = [lax.ppermute(own, AXES, shifted(-j, True)) for j in (1, 2, 3)]  5.74 us
    ppermute x3, starting transfers between devices, body(): lax.ppermute(tables, AXES, shifted(j, True))  4.93 us
    ppermute x3, starting transfers between devices, body(): lax.ppermute(early[j - 1], AXES, shifted(-j, False))  4.12 us
    ppermute x3, starting transfers between devices, body(): lax.ppermute(late[j - 1], AXES, shifted(-j, False))  4.01 us
  transfers between devices with their start and end apart: 17, of which 4 were waited for; matrix products, arithmetic and copies ran while one was open for 1% of the time, Pallas kernels for 20%

profile of v7, /device:TPU:0, one launch (start us, length us, event | category | flops | bytes accessed | tf_op | source)
XLA Modules:
  0.0 76.8 jit_solution(12028462449815140502)
XLA Ops:
  0.0 1.6 %collective-permute-start.5 = (bf16[64,32,128]{2,1,0:T(8,128)(2,1)}, bf16[64,32,128]{2,1,0:T(8,128)(2,1)S(1)}, u32[]{:S(2)}, u32[]{:S(2)}) collective-permute-start(bf16[64,32,128]{2,1,0:T(8,128)(2,1)} %bitcast.8), channel_id=1, source_target_pairs={{0,8},{1,33},{2,10},{3,35},{4,12},{5,37},{6,14},{7,39},{8,16},{9,4... | collective-permute-start | bytes 1572872 | tf_op jit(solution)/shard_map/ppermute | solution.py:480
  1.6 2.7 %collective-permute-start.4 = (bf16[64,32,128]{2,1,0:T(8,128)(2,1)}, bf16[64,32,128]{2,1,0:T(8,128)(2,1)S(1)}, u32[]{:S(2)}, u32[]{:S(2)}) collective-permute-start(bf16[64,32,128]{2,1,0:T(8,128)(2,1)} %bitcast.9), channel_id=1, source_target_pairs={{0,16},{1,65},{2,18},{3,67},{4,20},{5,69},{6,22},{7,71},{8,24},{9,... | collective-permute-start | bytes 1572872 | tf_op jit(solution)/shard_map/ppermute | solution.py:480
  4.3 1.4 %collective-permute-start.3 = (bf16[64,32,128]{2,1,0:T(8,128)(2,1)}, bf16[64,32,128]{2,1,0:T(8,128)(2,1)S(1)}, u32[]{:S(2)}, u32[]{:S(2)}) collective-permute-start(bf16[64,32,128]{2,1,0:T(8,128)(2,1)} %bitcast.10), channel_id=1, source_target_pairs={{0,24},{1,97},{2,26},{3,99},{4,28},{5,101},{6,30},{7,103},{8,0},{9... | collective-permute-start | bytes 1572872 | tf_op jit(solution)/shard_map/ppermute | solution.py:480
  5.7 0.8 %copy.13.partners = s32[4,8,4]{2,1,0:T(8,128)S(1)} copy(s32[4,8,4]{1,2,0:T(4,128)} %param.6) | data formatting | bytes 1024 | tf_op args[2]
  6.5 0.1 pad_add_fusion.place
  6.6 0.0 copy-start
  6.6 0.7 copy-done
  7.3 1.1 %plan.1 = (s32[8,128]{1,0:T(8,128)S(1)}, s32[8,128]{1,0:T(8,128)S(1)}, s32[8,128]{1,0:T(8,128)S(1)}, s32[8,128]{1,0:T(8,128)S(1)}, s32[1,128]{1,0:T(1,128)S(1)},...) custom-call(s32[4]{0:T(128)S(1)} %pad_add_fusion.place, s32[4,8,4]{2,1,0:T(8,128)S(1)} %copy.13.partners, s32[4,56]{1,0:T(4,128)S(1)} %copy-done), custom_call_target="tpu_custom_call" | custom-call | bytes 65536 | tf_op jit(solution)/shard_map/plan/pallas_call | solution.py:133
  8.3 1.6 %collective-permute-start = (s32[8,128]{1,0:T(8,128)S(1)}, s32[8,128]{1,0:T(8,128)S(1)}, u32[]{:S(2)}, u32[]{:S(2)}) collective-permute-start(s32[8,128]{1,0:T(8,128)S(1)} %get-tuple-element.42), channel_id=1, source_target_pairs={{0,32},{1,9},{2,34},{3,11},{4,36},{5,13},{6,38},{7,15},{8,40},{9,1... | collective-permute-start | bytes 12296 | tf_op jit(solution)/shard_map/ppermute | solution.py:484
  10.0 2.9 %collective-permute-start.1 = (s32[8,128]{1,0:T(8,128)S(1)}, s32[8,128]{1,0:T(8,128)S(1)}, u32[]{:S(2)}, u32[]{:S(2)}) collective-permute-start(s32[8,128]{1,0:T(8,128)S(1)} %get-tuple-element.43), channel_id=1, source_target_pairs={{0,64},{1,17},{2,66},{3,19},{4,68},{5,21},{6,70},{7,23},{8,72},{9,... | collective-permute-start | bytes 12296 | tf_op jit(solution)/shard_map/ppermute | solution.py:484
  12.9 0.7 collective-permute-done.req1.tab1
  13.6 1.5 %collective-permute-start.2 = (s32[8,128]{1,0:T(8,128)S(1)}, s32[8,128]{1,0:T(8,128)S(1)}, u32[]{:S(2)}, u32[]{:S(2)}) collective-permute-start(s32[8,128]{1,0:T(8,128)S(1)} %get-tuple-element.44), channel_id=1, source_target_pairs={{0,96},{1,25},{2,98},{3,27},{4,100},{5,29},{6,102},{7,31},{8,104},... | collective-permute-start | bytes 12296 | tf_op jit(solution)/shard_map/ppermute | solution.py:484
  15.1 3.0 %stage.1 = (bf16[4,8,64,32,128]{4,3,2,1,0:T(8,128)(2,1)S(1)}, bf16[64,32,128]{2,1,0:T(8,128)(2,1)S(1)}, f32[385,8,128]{2,1,0:T(8,128)S(1)}, bf16[2,4,256,256]{3,2,1,0:T(8,128)(2,1)S(1)}) custom-call(bf16[4,8,64,32,128]{4,3,2,1,0:T(8,128)(2,1)} %tensor.3, bf16[64,32,128]{2,1,0:T(8,128)(2,1)} %bitcast.11, s32[1,128]{1,0:T(1,128)S(1)} %get-tuple-element.45.picks, ...), custom_call_target="tpu_custom_call" | custom-call | bytes 5242880 | tf_op jit(solution)/shard_map/stage/pallas_call | solution.py:163
  18.1 0.0 collective-permute-done.1.req2.tab2
  18.1 0.0 collective-permute-done.2.req3.tab3
  18.2 0.0 collective-permute-done.5.got3
  18.2 0.0 collective-permute-done.4.got2
  18.2 0.0 collective-permute-done.3.got1
  18.2 1.2 %pack_early.1 = (bf16[32,32,128]{2,1,0:T(8,128)(2,1)S(1)}, bf16[32,32,128]{2,1,0:T(8,128)(2,1)S(1)}, bf16[32,32,128]{2,1,0:T(8,128)(2,1)S(1)}, bf16[256,32,128]{2,1,0:T(8,128)(2,1)S(1)}) custom-call(s32[8,128]{1,0:T(8,128)S(1)} %collective-permute-done.req1.tab1, s32[8,128]{1,0:T(8,128)S(1)} %collective-permute-done.1.req2.tab2, ...), custom_call_target="tpu_custom_call" | custom-call | bytes 4194304 | tf_op jit(solution)/shard_map/pack_early/pallas_call | solution.py:197
  19.4 2.7 %collective-permute-start.9 = (bf16[32,32,128]{2,1,0:T(8,128)(2,1)S(1)}, bf16[32,32,128]{2,1,0:T(8,128)(2,1)S(1)}, u32[]{:S(2)}, u32[]{:S(2)}) collective-permute-start(bf16[32,32,128]{2,1,0:T(8,128)(2,1)S(1)} %get-tuple-element.52), channel_id=1, source_target_pairs={{0,96},{1,25},{2,98},{3,27},{4,100},{5,29},{6,102},{7,31},{8,104},... | collective-permute-start | bytes 786440 | tf_op jit(solution)/shard_map/ppermute | solution.py:488
  22.1 0.2 collective-permute-start.10
  22.3 1.2 %collective-permute-start.11 = (bf16[32,32,128]{2,1,0:T(8,128)(2,1)S(1)}, bf16[32,32,128]{2,1,0:T(8,128)(2,1)S(1)}, u32[]{:S(2)}, u32[]{:S(2)}) collective-permute-start(bf16[32,32,128]{2,1,0:T(8,128)(2,1)S(1)} %get-tuple-element.54), channel_id=1, source_target_pairs={{0,32},{1,9},{2,34},{3,11},{4,36},{5,13},{6,38},{7,15},{8,40},{9,1... | collective-permute-start | bytes 786440 | tf_op jit(solution)/shard_map/ppermute | solution.py:488
  23.5 1.3 %pack_late.1 = (bf16[64,32,128]{2,1,0:T(8,128)(2,1)S(1)}, bf16[32,32,128]{2,1,0:T(8,128)(2,1)S(1)}, bf16[32,32,128]{2,1,0:T(8,128)(2,1)S(1)}, bf16[32,32,128]{2,1,0:T(8,128)(2,1)S(1)}, s32[4,8,128]{2,1,0:T(8,128)S(1)}) custom-call(s32[8,128]{1,0:T(8,128)S(1)} %get-tuple-element.41.req0.mine, s32[8,128]{1,0:T(8,128)S(1)} %collective-permute-done.req1.tab1, ...), custom_call_target="tpu_custom_call" | custom-call | bytes 2097152 | tf_op jit(solution)/shard_map/pack_late/pallas_call | solution.py:225
  24.8 2.9 %collective-permute-start.8 = (s32[4,8,128]{2,1,0:T(8,128)S(1)}, s32[4,8,128]{2,1,0:T(8,128)S(1)}, u32[]{:S(2)}, u32[]{:S(2)}) collective-permute-start(s32[4,8,128]{2,1,0:T(8,128)S(1)} %get-tuple-element.63.tables0), channel_id=1, source_target_pairs={{0,24},{1,97},{2,26},{3,99},{4,28},{5,101},{6,30},{7,103},{8,0},{9... | collective-permute-start | bytes 49160 | tf_op jit(solution)/shard_map/ppermute | solution.py:491
  27.7 0.9 %collective-permute-start.7 = (s32[4,8,128]{2,1,0:T(8,128)S(1)}, s32[4,8,128]{2,1,0:T(8,128)S(1)}, u32[]{:S(2)}, u32[]{:S(2)}) collective-permute-start(s32[4,8,128]{2,1,0:T(8,128)S(1)} %get-tuple-element.63.tables0), channel_id=1, source_target_pairs={{0,16},{1,65},{2,18},{3,67},{4,20},{5,69},{6,22},{7,71},{8,24},{9,... | collective-permute-start | bytes 49160 | tf_op jit(solution)/shard_map/ppermute | solution.py:491
  28.6 0.5 collective-permute-done.8.tables3
  29.1 1.1 %collective-permute-start.6 = (s32[4,8,128]{2,1,0:T(8,128)S(1)}, s32[4,8,128]{2,1,0:T(8,128)S(1)}, u32[]{:S(2)}, u32[]{:S(2)}) collective-permute-start(s32[4,8,128]{2,1,0:T(8,128)S(1)} %get-tuple-element.63.tables0), channel_id=1, source_target_pairs={{0,8},{1,33},{2,10},{3,35},{4,12},{5,37},{6,14},{7,39},{8,16},{9,4... | collective-permute-start | bytes 49160 | tf_op jit(solution)/shard_map/ppermute | solution.py:491
  30.3 0.0 collective-permute-done.9.row1
  30.3 2.5 %collective-permute-start.12 = (bf16[32,32,128]{2,1,0:T(8,128)(2,1)S(1)}, bf16[32,32,128]{2,1,0:T(8,128)(2,1)S(1)}, u32[]{:S(2)}, u32[]{:S(2)}) collective-permute-start(bf16[32,32,128]{2,1,0:T(8,128)(2,1)S(1)} %get-tuple-element.67), channel_id=1, source_target_pairs={{0,96},{1,25},{2,98},{3,27},{4,100},{5,29},{6,102},{7,31},{8,104},... | collective-permute-start | bytes 786440 | tf_op jit(solution)/shard_map/ppermute | solution.py:490
  32.8 0.0 collective-permute-done.10.row2
  32.8 1.5 %collective-permute-start.13 = (bf16[32,32,128]{2,1,0:T(8,128)(2,1)S(1)}, bf16[32,32,128]{2,1,0:T(8,128)(2,1)S(1)}, u32[]{:S(2)}, u32[]{:S(2)}) collective-permute-start(bf16[32,32,128]{2,1,0:T(8,128)(2,1)S(1)} %get-tuple-element.68), channel_id=1, source_target_pairs={{0,64},{1,17},{2,66},{3,19},{4,68},{5,21},{6,70},{7,23},{8,72},{9,... | collective-permute-start | bytes 786440 | tf_op jit(solution)/shard_map/ppermute | solution.py:490
  34.3 0.0 collective-permute-done.11.row3
  34.3 0.0 collective-permute-start.14
  34.3 9.2 %early_products.1 = (f32[385,8,128]{2,1,0:T(8,128)S(1)}, bf16[2,4,256,256]{3,2,1,0:T(8,128)(2,1)S(1)}, bf16[4,8,64,32,128]{4,3,2,1,0:T(8,128)(2,1)S(1)}, bf16[25...) custom-call(s32[1,128]{1,0:T(1,128)S(1)} %get-tuple-element.47.count, ...), custom_call_target="tpu_custom_call", output_to_operand_aliasing={{0}: (8, {}), {1}: (9, {}), {2}: (10, {})} | custom-call | flops 4294967296 | bytes 8388608 | tf_op jit(solution)/shard_map/early_products/pallas_call | solution.py:386
  43.5 0.0 collective-permute-done.7.tables2
  43.5 0.0 collective-permute-done.6.tables1
  43.5 0.0 collective-permute-done.12.late1
  43.5 0.0 collective-permute-done.13.late2
  43.5 0.0 collective-permute-done.14.late3
  43.5 3.9 %late_products.1 = (f32[385,8,128]{2,1,0:T(8,128)S(1)}, bf16[2,4,256,256]{3,2,1,0:T(8,128)(2,1)S(1)}, bf16[4,8,64,32,128]{4,3,2,1,0:T(8,128)(2,1)S(1)}, bf16[256...) custom-call(s32[4]{0:T(128)S(1)} %pad_add_fusion.place, ...), custom_call_target="tpu_custom_call", output_to_operand_aliasing={{0}: (7, {}), {1}: (8, {}), {2}: (9, {}), {3}: (10, {}), {4... | custom-call | flops 4294967296 | bytes 8388608 | tf_op jit(solution)/shard_map/late_products/pallas_call | solution.py:400
  47.4 0.1 collective-permute-start.15
  47.5 1.7 %collective-permute-done.15.came = bf16[1536,128]{1,0:T(8,128)(2,1)S(1)} collective-permute-done((bf16[1536,128]{1,0:T(8,128)(2,1)S(1)}, bf16[1536,128]{1,0:T(8,128)(2,1)S(1)}, u32[]{:S(2)}, u32[]{:S(2)}) %collective-permute-start.15) | collective-permute-done | bytes 393248 | tf_op jit(solution)/shard_map/ppermute | solution.py:499
  49.2 1.4 %join.1 = bf16[1536,128]{1,0:T(8,128)(2,1)} custom-call(s32[4]{0:T(128)S(1)} %pad_add_fusion.place, f32[385,8,128]{2,1,0:T(8,128)S(1)} %get-tuple-element.75.staged, bf16[1536,128]{1,0:T(8,128)(2,1)S(1)} %collective-permute-done.15.came), custom_call_target="tpu_custom_call" | custom-call | bytes 2097152 | tf_op jit(solution)/shard_map/join/pallas_call | solution.py:363
  50.6 12.4 %all-to-all-start = ((bf16[64,24,128]{2,1,0:T(8,128)(2,1)}), bf16[64,24,128]{2,1,0:T(8,128)(2,1)S(1)}, u32[]{:S(2)}, u32[]{:S(2)}) async-start(bf16[64,24,128]{2,1,0:T(8,128)(2,1)} %bitcast.5), calls=%async_computation | async-start | bytes 786432 | tf_op jit(solution)/shard_map/all_to_all | solution.py:501
  63.0 1.0 %locate.1.where = s32[16,128]{1,0:T(8,128)S(1)} custom-call(s32[4]{0:T(128)S(1)} %pad_add_fusion.place, s32[4,8,128]{2,1,0:T(8,128)S(1)} %get-tuple-element.63.tables0, s32[4,8,128]{2,1,0:T(8,128)S(1)} %collective-permute-done.6.tables1, s32[4,8,128]{2,1,0:T(8,128)S(1)} %collective-permute-done.7.tables2, s32[4,8,128]{2,1,0:T(8,128)S(1)} %collective-permute-done.8.tables3), custom_call_target="tpu_custom_call" | custom-call | bytes 65536 | tf_op jit(solution)/shard_map/locate/pallas_call | solution.py:433
  64.0 11.2 %all-to-all-done = bf16[64,24,128]{2,1,0:T(8,128)(2,1)S(1)} async-done(((bf16[64,24,128]{2,1,0:T(8,128)(2,1)}), bf16[64,24,128]{2,1,0:T(8,128)(2,1)S(1)}, u32[]{:S(2)}, u32[]{:S(2)}) %all-to-all-start) | async-done | bytes 393248 | tf_op jit(solution)/shard_map/all_to_all | solution.py:501
  75.2 1.6 %collect.1 = f32[16,1024]{1,0:T(8,128)} custom-call(s32[4]{0:T(128)S(1)} %pad_add_fusion.place, s32[16,128]{1,0:T(8,128)S(1)} %locate.1.where, bf16[1536,128]{1,0:T(8,128)(2,1)S(1)} %bitcast.7), custom_call_target="tpu_custom_call" | custom-call | tf_op jit(solution)/shard_map/collect/pallas_call | solution.py:462
Async XLA Ops:
  0.0 18.2 %collective-permute-start.5 = (bf16[64,32,128]{2,1,0:T(8,128)(2,1)}, bf16[64,32,128]{2,1,0:T(8,128)(2,1)S(1)}, u32[]{:S(2)}, u32[]{:S(2)}) collective-permute-start(bf16[64,32,128]{2,1,0:T(8,128)(2,1)} %bitcast.8), channel_id=1, source_target_pairs={{0,8},{1,33},{2,10},{3,35},{4,12},{5,37},{6,14},{7,39},{8,16},{9,4... | collective-permute-start | bytes 1572872 | tf_op jit(solution)/shard_map/ppermute | solution.py:480
  1.6 16.6 %collective-permute-start.4 = (bf16[64,32,128]{2,1,0:T(8,128)(2,1)}, bf16[64,32,128]{2,1,0:T(8,128)(2,1)S(1)}, u32[]{:S(2)}, u32[]{:S(2)}) collective-permute-start(bf16[64,32,128]{2,1,0:T(8,128)(2,1)} %bitcast.9), channel_id=1, source_target_pairs={{0,16},{1,65},{2,18},{3,67},{4,20},{5,69},{6,22},{7,71},{8,24},{9,... | collective-permute-start | bytes 1572872 | tf_op jit(solution)/shard_map/ppermute | solution.py:480
  4.3 13.9 %collective-permute-start.3 = (bf16[64,32,128]{2,1,0:T(8,128)(2,1)}, bf16[64,32,128]{2,1,0:T(8,128)(2,1)S(1)}, u32[]{:S(2)}, u32[]{:S(2)}) collective-permute-start(bf16[64,32,128]{2,1,0:T(8,128)(2,1)} %bitcast.10), channel_id=1, source_target_pairs={{0,24},{1,97},{2,26},{3,99},{4,28},{5,101},{6,30},{7,103},{8,0},{9... | collective-permute-start | bytes 1572872 | tf_op jit(solution)/shard_map/ppermute | solution.py:480
  6.6 0.7 copy-start
  8.3 5.3 %collective-permute-start = (s32[8,128]{1,0:T(8,128)S(1)}, s32[8,128]{1,0:T(8,128)S(1)}, u32[]{:S(2)}, u32[]{:S(2)}) collective-permute-start(s32[8,128]{1,0:T(8,128)S(1)} %get-tuple-element.42), channel_id=1, source_target_pairs={{0,32},{1,9},{2,34},{3,11},{4,36},{5,13},{6,38},{7,15},{8,40},{9,1... | collective-permute-start | bytes 12296 | tf_op jit(solution)/shard_map/ppermute | solution.py:484
  10.0 8.1 %collective-permute-start.1 = (s32[8,128]{1,0:T(8,128)S(1)}, s32[8,128]{1,0:T(8,128)S(1)}, u32[]{:S(2)}, u32[]{:S(2)}) collective-permute-start(s32[8,128]{1,0:T(8,128)S(1)} %get-tuple-element.43), channel_id=1, source_target_pairs={{0,64},{1,17},{2,66},{3,19},{4,68},{5,21},{6,70},{7,23},{8,72},{9,... | collective-permute-start | bytes 12296 | tf_op jit(solution)/shard_map/ppermute | solution.py:484
  13.6 4.5 %collective-permute-start.2 = (s32[8,128]{1,0:T(8,128)S(1)}, s32[8,128]{1,0:T(8,128)S(1)}, u32[]{:S(2)}, u32[]{:S(2)}) collective-permute-start(s32[8,128]{1,0:T(8,128)S(1)} %get-tuple-element.44), channel_id=1, source_target_pairs={{0,96},{1,25},{2,98},{3,27},{4,100},{5,29},{6,102},{7,31},{8,104},... | collective-permute-start | bytes 12296 | tf_op jit(solution)/shard_map/ppermute | solution.py:484
  19.4 10.9 %collective-permute-start.9 = (bf16[32,32,128]{2,1,0:T(8,128)(2,1)S(1)}, bf16[32,32,128]{2,1,0:T(8,128)(2,1)S(1)}, u32[]{:S(2)}, u32[]{:S(2)}) collective-permute-start(bf16[32,32,128]{2,1,0:T(8,128)(2,1)S(1)} %get-tuple-element.52), channel_id=1, source_target_pairs={{0,96},{1,25},{2,98},{3,27},{4,100},{5,29},{6,102},{7,31},{8,104},... | collective-permute-start | bytes 786440 | tf_op jit(solution)/shard_map/ppermute | solution.py:488
  22.1 10.7 %collective-permute-start.10 = (bf16[32,32,128]{2,1,0:T(8,128)(2,1)S(1)}, bf16[32,32,128]{2,1,0:T(8,128)(2,1)S(1)}, u32[]{:S(2)}, u32[]{:S(2)}) collective-permute-start(bf16[32,32,128]{2,1,0:T(8,128)(2,1)S(1)} %get-tuple-element.53), channel_id=1, source_target_pairs={{0,64},{1,17},{2,66},{3,19},{4,68},{5,21},{6,70},{7,23},{8,72},{9,... | collective-permute-start | bytes 786440 | tf_op jit(solution)/shard_map/ppermute | solution.py:488
  22.3 12.0 %collective-permute-start.11 = (bf16[32,32,128]{2,1,0:T(8,128)(2,1)S(1)}, bf16[32,32,128]{2,1,0:T(8,128)(2,1)S(1)}, u32[]{:S(2)}, u32[]{:S(2)}) collective-permute-start(bf16[32,32,128]{2,1,0:T(8,128)(2,1)S(1)} %get-tuple-element.54), channel_id=1, source_target_pairs={{0,32},{1,9},{2,34},{3,11},{4,36},{5,13},{6,38},{7,15},{8,40},{9,1... | collective-permute-start | bytes 786440 | tf_op jit(solution)/shard_map/ppermute | solution.py:488
  24.8 4.3 %collective-permute-start.8 = (s32[4,8,128]{2,1,0:T(8,128)S(1)}, s32[4,8,128]{2,1,0:T(8,128)S(1)}, u32[]{:S(2)}, u32[]{:S(2)}) collective-permute-start(s32[4,8,128]{2,1,0:T(8,128)S(1)} %get-tuple-element.63.tables0), channel_id=1, source_target_pairs={{0,24},{1,97},{2,26},{3,99},{4,28},{5,101},{6,30},{7,103},{8,0},{9... | collective-permute-start | bytes 49160 | tf_op jit(solution)/shard_map/ppermute | solution.py:491
  27.7 15.8 %collective-permute-start.7 = (s32[4,8,128]{2,1,0:T(8,128)S(1)}, s32[4,8,128]{2,1,0:T(8,128)S(1)}, u32[]{:S(2)}, u32[]{:S(2)}) collective-permute-start(s32[4,8,128]{2,1,0:T(8,128)S(1)} %get-tuple-element.63.tables0), channel_id=1, source_target_pairs={{0,16},{1,65},{2,18},{3,67},{4,20},{5,69},{6,22},{7,71},{8,24},{9,... | collective-permute-start | bytes 49160 | tf_op jit(solution)/shard_map/ppermute | solution.py:491
  29.1 14.4 %collective-permute-start.6 = (s32[4,8,128]{2,1,0:T(8,128)S(1)}, s32[4,8,128]{2,1,0:T(8,128)S(1)}, u32[]{:S(2)}, u32[]{:S(2)}) collective-permute-start(s32[4,8,128]{2,1,0:T(8,128)S(1)} %get-tuple-element.63.tables0), channel_id=1, source_target_pairs={{0,8},{1,33},{2,10},{3,35},{4,12},{5,37},{6,14},{7,39},{8,16},{9,4... | collective-permute-start | bytes 49160 | tf_op jit(solution)/shard_map/ppermute | solution.py:491
  30.3 13.2 %collective-permute-start.12 = (bf16[32,32,128]{2,1,0:T(8,128)(2,1)S(1)}, bf16[32,32,128]{2,1,0:T(8,128)(2,1)S(1)}, u32[]{:S(2)}, u32[]{:S(2)}) collective-permute-start(bf16[32,32,128]{2,1,0:T(8,128)(2,1)S(1)} %get-tuple-element.67), channel_id=1, source_target_pairs={{0,96},{1,25},{2,98},{3,27},{4,100},{5,29},{6,102},{7,31},{8,104},... | collective-permute-start | bytes 786440 | tf_op jit(solution)/shard_map/ppermute | solution.py:490
  32.8 10.7 %collective-permute-start.13 = (bf16[32,32,128]{2,1,0:T(8,128)(2,1)S(1)}, bf16[32,32,128]{2,1,0:T(8,128)(2,1)S(1)}, u32[]{:S(2)}, u32[]{:S(2)}) collective-permute-start(bf16[32,32,128]{2,1,0:T(8,128)(2,1)S(1)} %get-tuple-element.68), channel_id=1, source_target_pairs={{0,64},{1,17},{2,66},{3,19},{4,68},{5,21},{6,70},{7,23},{8,72},{9,... | collective-permute-start | bytes 786440 | tf_op jit(solution)/shard_map/ppermute | solution.py:490
  34.3 9.3 %collective-permute-start.14 = (bf16[32,32,128]{2,1,0:T(8,128)(2,1)S(1)}, bf16[32,32,128]{2,1,0:T(8,128)(2,1)S(1)}, u32[]{:S(2)}, u32[]{:S(2)}) collective-permute-start(bf16[32,32,128]{2,1,0:T(8,128)(2,1)S(1)} %get-tuple-element.69), channel_id=1, source_target_pairs={{0,32},{1,9},{2,34},{3,11},{4,36},{5,13},{6,38},{7,15},{8,40},{9,1... | collective-permute-start | bytes 786440 | tf_op jit(solution)/shard_map/ppermute | solution.py:490
  47.4 1.8 %collective-permute-start.15 = (bf16[1536,128]{1,0:T(8,128)(2,1)S(1)}, bf16[1536,128]{1,0:T(8,128)(2,1)S(1)}, u32[]{:S(2)}, u32[]{:S(2)}) collective-permute-start(bf16[1536,128]{1,0:T(8,128)(2,1)S(1)} %get-tuple-element.76), channel_id=1, source_target_pairs={{0,1},{1,0},{2,3},{3,2},{4,5},{5,4},{6,7},{7,6},{8,9},{9,8},{10,11... | collective-permute-start | bytes 1179656 | tf_op jit(solution)/shard_map/ppermute | solution.py:499
  50.6 24.6 %all-to-all-start = ((bf16[64,24,128]{2,1,0:T(8,128)(2,1)}), bf16[64,24,128]{2,1,0:T(8,128)(2,1)S(1)}, u32[]{:S(2)}, u32[]{:S(2)}) async-start(bf16[64,24,128]{2,1,0:T(8,128)(2,1)} %bitcast.5), calls=%async_computation | async-start | bytes 786432 | tf_op jit(solution)/shard_map/all_to_all | solution.py:501

commit v8 on v4

--- a/solution.py
+++ b/solution.py
@@ -184,7 +184,7 @@
         shards[pl.ds(at * BLK_DEV, BLK_DEV)] = src[...]
     for j, (req, out) in enumerate(((req1, out1), (req2, out2), (req3, out3))):
 
-        @pl.loop(0, EARLY, unroll=8)
+        @pl.loop(0, EARLY, unroll=32)
         def _(r):
             out[r] = shards[req[LIST_ROW, (j + 1) % 2 * ROW_CAP + r]]
 
@@ -212,11 +212,11 @@
         tables[at] = src[...]
     for j, (req, out) in enumerate(((req1, out1), (req2, out2), (req3, out3))):
 
-        @pl.loop(0, LATE, unroll=8)
+        @pl.loop(0, LATE, unroll=32)
         def _(r):
             out[r] = shards[req[LIST_ROW, (j + 1) % 2 * ROW_CAP + EARLY + r]]
 
-    @pl.loop(0, ROW_CAP, unroll=8)
+    @pl.loop(0, ROW_CAP, unroll=32)
     def _(r):
         out0[r] = shards[req0[LIST_ROW, r]]
 

time: 72.6 us -> 72.3 us (level)
    pallas_call x1, Pallas kernels: 3.85 us -> 0.97 us  [late_products(): pl.pallas_call(late_kernel, out_shape=STATE + [jax.ShapeDtypeStruct((SIDE...]
    pallas_call x1, Pallas kernels: 9.2 us -> 12 us  [early_products(): pl.pallas_call(early_kernel, out_shape=STATE, in_specs=[SMEM] * 3 + [VMEM...]
  transfers between devices with their start and end apart: 17 -> 17, of which waited for: 8 -> 9; matrix products, arithmetic and copies ran while one was open for 1% -> 1% of each run, Pallas kernels for 22% -> 25%
where the time goes in v8:
time: 72.3 us; the launch traced here: 72.1 us
  starting transfers between devices  34.4 us (48%)
  Pallas kernels  23 us (32%)
  waiting for transfers between devices  13 us (18%)
  local copies, waits for them, and re-layouts  1.47 us (2%)
    pallas_call x1, Pallas kernels, early_products(): pl.pallas_call(early_kernel, out_shape=STATE, in_specs=[SMEM] * 3 + [VMEM...  12 us
    all_to_all x1, starting transfers between devices, body(): lax.all_to_all(outgoing, AXES, split_axis=0, concat_axis=0, axis_index_gr...  9.6 us
    ppermute x3, starting transfers between devices, body(): lax.ppermute(sent[j - 1], AXES, shifted(j, False))  6.05 us
    ppermute x3, starting transfers between devices, body(): got = [lax.ppermute(own, AXES, shifted(-j, True)) for j in (1, 2, 3)]  5.74 us
    ppermute x3, starting transfers between devices, body(): lax.ppermute(tables, AXES, shifted(j, True))  4.57 us
    ppermute x3, starting transfers between devices, body(): lax.ppermute(late[j - 1], AXES, shifted(-j, False))  4.19 us
    ppermute x3, starting transfers between devices, body(): lax.ppermute(early[j - 1], AXES, shifted(-j, False))  4.12 us
    ppermute x3, waiting for transfers between devices, body(): lax.ppermute(tables, AXES, shifted(j, True))  4.09 us
  transfers between devices with their start and end apart: 17, of which 9 were waited for; matrix products, arithmetic and copies ran while one was open for 1% of the time, Pallas kernels for 25%

profile of v8, /device:TPU:0, one launch (start us, length us, event | category | flops | bytes accessed | tf_op | source)
XLA Modules:
  0.0 72.1 jit_solution(10459406603766300813)
XLA Ops:
  0.0 1.6 %collective-permute-start.5 = (bf16[64,32,128]{2,1,0:T(8,128)(2,1)}, bf16[64,32,128]{2,1,0:T(8,128)(2,1)S(1)}, u32[]{:S(2)}, u32[]{:S(2)}) collective-permute-start(bf16[64,32,128]{2,1,0:T(8,128)(2,1)} %bitcast.8), channel_id=1, source_target_pairs={{0,8},{1,33},{2,10},{3,35},{4,12},{5,37},{6,14},{7,39},{8,16},{9,4... | collective-permute-start | bytes 1572872 | tf_op jit(solution)/shard_map/ppermute | solution.py:480
  1.6 2.7 %collective-permute-start.4 = (bf16[64,32,128]{2,1,0:T(8,128)(2,1)}, bf16[64,32,128]{2,1,0:T(8,128)(2,1)S(1)}, u32[]{:S(2)}, u32[]{:S(2)}) collective-permute-start(bf16[64,32,128]{2,1,0:T(8,128)(2,1)} %bitcast.9), channel_id=1, source_target_pairs={{0,16},{1,65},{2,18},{3,67},{4,20},{5,69},{6,22},{7,71},{8,24},{9,... | collective-permute-start | bytes 1572872 | tf_op jit(solution)/shard_map/ppermute | solution.py:480
  4.3 1.4 %collective-permute-start.3 = (bf16[64,32,128]{2,1,0:T(8,128)(2,1)}, bf16[64,32,128]{2,1,0:T(8,128)(2,1)S(1)}, u32[]{:S(2)}, u32[]{:S(2)}) collective-permute-start(bf16[64,32,128]{2,1,0:T(8,128)(2,1)} %bitcast.10), channel_id=1, source_target_pairs={{0,24},{1,97},{2,26},{3,99},{4,28},{5,101},{6,30},{7,103},{8,0},{9... | collective-permute-start | bytes 1572872 | tf_op jit(solution)/shard_map/ppermute | solution.py:480
  5.7 0.8 %copy.13.partners = s32[4,8,4]{2,1,0:T(8,128)S(1)} copy(s32[4,8,4]{1,2,0:T(4,128)} %param.6) | data formatting | bytes 1024 | tf_op args[2]
  6.5 0.1 pad_add_fusion.place
  6.6 0.0 copy-start
  6.6 0.7 copy-done
  7.3 1.1 %plan.1 = (s32[8,128]{1,0:T(8,128)S(1)}, s32[8,128]{1,0:T(8,128)S(1)}, s32[8,128]{1,0:T(8,128)S(1)}, s32[8,128]{1,0:T(8,128)S(1)}, s32[1,128]{1,0:T(1,128)S(1)},...) custom-call(s32[4]{0:T(128)S(1)} %pad_add_fusion.place, s32[4,8,4]{2,1,0:T(8,128)S(1)} %copy.13.partners, s32[4,56]{1,0:T(4,128)S(1)} %copy-done), custom_call_target="tpu_custom_call" | custom-call | bytes 65536 | tf_op jit(solution)/shard_map/plan/pallas_call | solution.py:133
  8.3 1.6 %collective-permute-start = (s32[8,128]{1,0:T(8,128)S(1)}, s32[8,128]{1,0:T(8,128)S(1)}, u32[]{:S(2)}, u32[]{:S(2)}) collective-permute-start(s32[8,128]{1,0:T(8,128)S(1)} %get-tuple-element.33), channel_id=1, source_target_pairs={{0,32},{1,9},{2,34},{3,11},{4,36},{5,13},{6,38},{7,15},{8,40},{9,1... | collective-permute-start | bytes 12296 | tf_op jit(solution)/shard_map/ppermute | solution.py:484
  10.0 2.9 %collective-permute-start.1 = (s32[8,128]{1,0:T(8,128)S(1)}, s32[8,128]{1,0:T(8,128)S(1)}, u32[]{:S(2)}, u32[]{:S(2)}) collective-permute-start(s32[8,128]{1,0:T(8,128)S(1)} %get-tuple-element.34), channel_id=1, source_target_pairs={{0,64},{1,17},{2,66},{3,19},{4,68},{5,21},{6,70},{7,23},{8,72},{9,... | collective-permute-start | bytes 12296 | tf_op jit(solution)/shard_map/ppermute | solution.py:484
  12.9 0.7 %collective-permute-done.req1.tab1 = s32[8,128]{1,0:T(8,128)S(1)} collective-permute-done((s32[8,128]{1,0:T(8,128)S(1)}, s32[8,128]{1,0:T(8,128)S(1)}, u32[]{:S(2)}, u32[]{:S(2)}) %collective-permute-start) | collective-permute-done | bytes 4128 | tf_op jit(solution)/shard_map/ppermute | solution.py:484
  13.6 1.5 %collective-permute-start.2 = (s32[8,128]{1,0:T(8,128)S(1)}, s32[8,128]{1,0:T(8,128)S(1)}, u32[]{:S(2)}, u32[]{:S(2)}) collective-permute-start(s32[8,128]{1,0:T(8,128)S(1)} %get-tuple-element.35), channel_id=1, source_target_pairs={{0,96},{1,25},{2,98},{3,27},{4,100},{5,29},{6,102},{7,31},{8,104},... | collective-permute-start | bytes 12296 | tf_op jit(solution)/shard_map/ppermute | solution.py:484
  15.1 3.0 %stage.1 = (bf16[4,8,64,32,128]{4,3,2,1,0:T(8,128)(2,1)S(1)}, bf16[64,32,128]{2,1,0:T(8,128)(2,1)S(1)}, f32[385,8,128]{2,1,0:T(8,128)S(1)}, bf16[2,4,256,256]{3,2,1,0:T(8,128)(2,1)S(1)}) custom-call(bf16[4,8,64,32,128]{4,3,2,1,0:T(8,128)(2,1)} %tensor.3, bf16[64,32,128]{2,1,0:T(8,128)(2,1)} %bitcast.11, s32[1,128]{1,0:T(1,128)S(1)} %get-tuple-element.36.picks, ...), custom_call_target="tpu_custom_call" | custom-call | bytes 5242880 | tf_op jit(solution)/shard_map/stage/pallas_call | solution.py:163
  18.1 0.0 collective-permute-done.1.req2.tab2
  18.1 0.0 collective-permute-done.2.req3.tab3
  18.2 0.0 collective-permute-done.5.got3
  18.2 0.0 collective-permute-done.4.got2
  18.2 0.0 collective-permute-done.3.got1
  18.2 0.9 %pack_early.1 = (bf16[32,32,128]{2,1,0:T(8,128)(2,1)S(1)}, bf16[32,32,128]{2,1,0:T(8,128)(2,1)S(1)}, bf16[32,32,128]{2,1,0:T(8,128)(2,1)S(1)}, bf16[256,32,128]{2,1,0:T(8,128)(2,1)S(1)}) custom-call(s32[8,128]{1,0:T(8,128)S(1)} %collective-permute-done.req1.tab1, s32[8,128]{1,0:T(8,128)S(1)} %collective-permute-done.1.req2.tab2, ...), custom_call_target="tpu_custom_call" | custom-call | bytes 4194304 | tf_op jit(solution)/shard_map/pack_early/pallas_call | solution.py:197
  19.1 2.7 %collective-permute-start.12 = (bf16[32,32,128]{2,1,0:T(8,128)(2,1)S(1)}, bf16[32,32,128]{2,1,0:T(8,128)(2,1)S(1)}, u32[]{:S(2)}, u32[]{:S(2)}) collective-permute-start(bf16[32,32,128]{2,1,0:T(8,128)(2,1)S(1)} %get-tuple-element.46), channel_id=1, source_target_pairs={{0,96},{1,25},{2,98},{3,27},{4,100},{5,29},{6,102},{7,31},{8,104},... | collective-permute-start | bytes 786440 | tf_op jit(solution)/shard_map/ppermute | solution.py:488
  21.8 0.2 collective-permute-start.13
  22.0 1.2 %collective-permute-start.14 = (bf16[32,32,128]{2,1,0:T(8,128)(2,1)S(1)}, bf16[32,32,128]{2,1,0:T(8,128)(2,1)S(1)}, u32[]{:S(2)}, u32[]{:S(2)}) collective-permute-start(bf16[32,32,128]{2,1,0:T(8,128)(2,1)S(1)} %get-tuple-element.48), channel_id=1, source_target_pairs={{0,32},{1,9},{2,34},{3,11},{4,36},{5,13},{6,38},{7,15},{8,40},{9,1... | collective-permute-start | bytes 786440 | tf_op jit(solution)/shard_map/ppermute | solution.py:488
  23.2 1.0 %pack_late.1 = (bf16[64,32,128]{2,1,0:T(8,128)(2,1)S(1)}, bf16[32,32,128]{2,1,0:T(8,128)(2,1)S(1)}, bf16[32,32,128]{2,1,0:T(8,128)(2,1)S(1)}, bf16[32,32,128]{2,1,0:T(8,128)(2,1)S(1)}, s32[4,8,128]{2,1,0:T(8,128)S(1)}) custom-call(s32[8,128]{1,0:T(8,128)S(1)} %get-tuple-element.32.req0.mine, s32[8,128]{1,0:T(8,128)S(1)} %collective-permute-done.req1.tab1, ...), custom_call_target="tpu_custom_call" | custom-call | bytes 2097152 | tf_op jit(solution)/shard_map/pack_late/pallas_call | solution.py:225
  24.3 2.1 %collective-permute-start.9 = (bf16[32,32,128]{2,1,0:T(8,128)(2,1)S(1)}, bf16[32,32,128]{2,1,0:T(8,128)(2,1)S(1)}, u32[]{:S(2)}, u32[]{:S(2)}) collective-permute-start(bf16[32,32,128]{2,1,0:T(8,128)(2,1)S(1)} %get-tuple-element.42), channel_id=1, source_target_pairs={{0,96},{1,25},{2,98},{3,27},{4,100},{5,29},{6,102},{7,31},{8,104},... | collective-permute-start | bytes 786440 | tf_op jit(solution)/shard_map/ppermute | solution.py:490
  26.4 2.1 %collective-permute-start.10 = (bf16[32,32,128]{2,1,0:T(8,128)(2,1)S(1)}, bf16[32,32,128]{2,1,0:T(8,128)(2,1)S(1)}, u32[]{:S(2)}, u32[]{:S(2)}) collective-permute-start(bf16[32,32,128]{2,1,0:T(8,128)(2,1)S(1)} %get-tuple-element.43), channel_id=1, source_target_pairs={{0,64},{1,17},{2,66},{3,19},{4,68},{5,21},{6,70},{7,23},{8,72},{9,... | collective-permute-start | bytes 786440 | tf_op jit(solution)/shard_map/ppermute | solution.py:490
  28.5 0.1 collective-permute-done.12.row1
  28.5 0.0 collective-permute-start.11
  28.5 1.2 %collective-permute-done.13.row2 = bf16[32,32,128]{2,1,0:T(8,128)(2,1)S(1)} collective-permute-done((bf16[32,32,128]{2,1,0:T(8,128)(2,1)S(1)}, bf16[32,32,128]{2,1,0:T(8,128)(2,1)S(1)}, u32[]{:S(2)}, u32[]{:S(2)}) %collective-permute-start.13) | collective-permute-done | bytes 262176 | tf_op jit(solution)/shard_map/ppermute | solution.py:488
  29.8 2.6 %collective-permute-done.14.row3 = bf16[32,32,128]{2,1,0:T(8,128)(2,1)S(1)} collective-permute-done((bf16[32,32,128]{2,1,0:T(8,128)(2,1)S(1)}, bf16[32,32,128]{2,1,0:T(8,128)(2,1)S(1)}, u32[]{:S(2)}, u32[]{:S(2)}) %collective-permute-start.14) | collective-permute-done | bytes 262176 | tf_op jit(solution)/shard_map/ppermute | solution.py:488
  32.4 12.0 %early_products.1 = (f32[385,8,128]{2,1,0:T(8,128)S(1)}, bf16[2,4,256,256]{3,2,1,0:T(8,128)(2,1)S(1)}, bf16[4,8,64,32,128]{4,3,2,1,0:T(8,128)(2,1)S(1)}, bf16[25...) custom-call(s32[1,128]{1,0:T(1,128)S(1)} %get-tuple-element.38.count, ...), custom_call_target="tpu_custom_call", output_to_operand_aliasing={{0}: (8, {}), {1}: (9, {}), {2}: (10, {})} | custom-call | flops 4294967296 | bytes 8388608 | tf_op jit(solution)/shard_map/early_products/pallas_call | solution.py:386
  44.4 0.0 collective-permute-done.9.late1
  44.4 0.0 collective-permute-done.10.late2
  44.4 0.0 collective-permute-done.11.late3
  44.5 1.0 %late_products.1 = (f32[385,8,128]{2,1,0:T(8,128)S(1)}, bf16[2,4,256,256]{3,2,1,0:T(8,128)(2,1)S(1)}, bf16[4,8,64,32,128]{4,3,2,1,0:T(8,128)(2,1)S(1)}, bf16[256...) custom-call(s32[4]{0:T(128)S(1)} %pad_add_fusion.place, ...), custom_call_target="tpu_custom_call", output_to_operand_aliasing={{0}: (7, {}), {1}: (8, {}), {2}: (9, {}), {3}: (10, {}), {4... | custom-call | flops 4294967296 | bytes 8388608 | tf_op jit(solution)/shard_map/late_products/pallas_call | solution.py:400
  45.4 0.1 collective-permute-start.15
  45.5 1.7 %collective-permute-done.15.came = bf16[1536,128]{1,0:T(8,128)(2,1)S(1)} collective-permute-done((bf16[1536,128]{1,0:T(8,128)(2,1)S(1)}, bf16[1536,128]{1,0:T(8,128)(2,1)S(1)}, u32[]{:S(2)}, u32[]{:S(2)}) %collective-permute-start.15) | collective-permute-done | bytes 393248 | tf_op jit(solution)/shard_map/ppermute | solution.py:498
  47.2 1.4 %join.1 = bf16[1536,128]{1,0:T(8,128)(2,1)} custom-call(s32[4]{0:T(128)S(1)} %pad_add_fusion.place, f32[385,8,128]{2,1,0:T(8,128)S(1)} %get-tuple-element.57.staged, bf16[1536,128]{1,0:T(8,128)(2,1)S(1)} %collective-permute-done.15.came), custom_call_target="tpu_custom_call" | custom-call | bytes 2097152 | tf_op jit(solution)/shard_map/join/pallas_call | solution.py:363
  48.6 9.6 %all-to-all-start = ((bf16[64,24,128]{2,1,0:T(8,128)(2,1)}), bf16[64,24,128]{2,1,0:T(8,128)(2,1)S(1)}, u32[]{:S(2)}, u32[]{:S(2)}) async-start(bf16[64,24,128]{2,1,0:T(8,128)(2,1)} %bitcast.5), calls=%async_computation | async-start | bytes 786432 | tf_op jit(solution)/shard_map/all_to_all | solution.py:500
  58.2 2.9 %collective-permute-start.8 = (s32[4,8,128]{2,1,0:T(8,128)S(1)}, s32[4,8,128]{2,1,0:T(8,128)S(1)}, u32[]{:S(2)}, u32[]{:S(2)}) collective-permute-start(s32[4,8,128]{2,1,0:T(8,128)S(1)} %get-tuple-element.41.tables0), channel_id=1, source_target_pairs={{0,24},{1,97},{2,26},{3,99},{4,28},{5,101},{6,30},{7,103},{8,0},{9... | collective-permute-start | bytes 49160 | tf_op jit(solution)/shard_map/ppermute | solution.py:491
  61.1 0.9 %collective-permute-start.7 = (s32[4,8,128]{2,1,0:T(8,128)S(1)}, s32[4,8,128]{2,1,0:T(8,128)S(1)}, u32[]{:S(2)}, u32[]{:S(2)}) collective-permute-start(s32[4,8,128]{2,1,0:T(8,128)S(1)} %get-tuple-element.41.tables0), channel_id=1, source_target_pairs={{0,16},{1,65},{2,18},{3,67},{4,20},{5,69},{6,22},{7,71},{8,24},{9,... | collective-permute-start | bytes 49160 | tf_op jit(solution)/shard_map/ppermute | solution.py:491
  61.9 0.9 %collective-permute-start.6 = (s32[4,8,128]{2,1,0:T(8,128)S(1)}, s32[4,8,128]{2,1,0:T(8,128)S(1)}, u32[]{:S(2)}, u32[]{:S(2)}) collective-permute-start(s32[4,8,128]{2,1,0:T(8,128)S(1)} %get-tuple-element.41.tables0), channel_id=1, source_target_pairs={{0,8},{1,33},{2,10},{3,35},{4,12},{5,37},{6,14},{7,39},{8,16},{9,4... | collective-permute-start | bytes 49160 | tf_op jit(solution)/shard_map/ppermute | solution.py:491
  62.8 1.7 %collective-permute-done.8.tables3 = s32[4,8,128]{2,1,0:T(8,128)S(1)} collective-permute-done((s32[4,8,128]{2,1,0:T(8,128)S(1)}, s32[4,8,128]{2,1,0:T(8,128)S(1)}, u32[]{:S(2)}, u32[]{:S(2)}) %collective-permute-start.8) | collective-permute-done | bytes 16416 | tf_op jit(solution)/shard_map/ppermute | solution.py:491
  64.4 1.9 %collective-permute-done.7.tables2 = s32[4,8,128]{2,1,0:T(8,128)S(1)} collective-permute-done((s32[4,8,128]{2,1,0:T(8,128)S(1)}, s32[4,8,128]{2,1,0:T(8,128)S(1)}, u32[]{:S(2)}, u32[]{:S(2)}) %collective-permute-start.7) | collective-permute-done | bytes 16416 | tf_op jit(solution)/shard_map/ppermute | solution.py:491
  66.3 0.6 collective-permute-done.6.tables1
  66.9 1.0 %locate.1.where = s32[16,128]{1,0:T(8,128)S(1)} custom-call(s32[4]{0:T(128)S(1)} %pad_add_fusion.place, s32[4,8,128]{2,1,0:T(8,128)S(1)} %get-tuple-element.41.tables0, s32[4,8,128]{2,1,0:T(8,128)S(1)} %collective-permute-done.6.tables1, s32[4,8,128]{2,1,0:T(8,128)S(1)} %collective-permute-done.7.tables2, s32[4,8,128]{2,1,0:T(8,128)S(1)} %collective-permute-done.8.tables3), custom_call_target="tpu_custom_call" | custom-call | bytes 65536 | tf_op jit(solution)/shard_map/locate/pallas_call | solution.py:433
  67.9 2.5 %all-to-all-done = bf16[64,24,128]{2,1,0:T(8,128)(2,1)S(1)} async-done(((bf16[64,24,128]{2,1,0:T(8,128)(2,1)}), bf16[64,24,128]{2,1,0:T(8,128)(2,1)S(1)}, u32[]{:S(2)}, u32[]{:S(2)}) %all-to-all-start) | async-done | bytes 393248 | tf_op jit(solution)/shard_map/all_to_all | solution.py:500
  70.4 1.7 %collect.1 = f32[16,1024]{1,0:T(8,128)} custom-call(s32[4]{0:T(128)S(1)} %pad_add_fusion.place, s32[16,128]{1,0:T(8,128)S(1)} %locate.1.where, bf16[1536,128]{1,0:T(8,128)(2,1)S(1)} %bitcast.7), custom_call_target="tpu_custom_call" | custom-call | tf_op jit(solution)/shard_map/collect/pallas_call | solution.py:462
Async XLA Ops:
  0.0 18.2 %collective-permute-start.5 = (bf16[64,32,128]{2,1,0:T(8,128)(2,1)}, bf16[64,32,128]{2,1,0:T(8,128)(2,1)S(1)}, u32[]{:S(2)}, u32[]{:S(2)}) collective-permute-start(bf16[64,32,128]{2,1,0:T(8,128)(2,1)} %bitcast.8), channel_id=1, source_target_pairs={{0,8},{1,33},{2,10},{3,35},{4,12},{5,37},{6,14},{7,39},{8,16},{9,4... | collective-permute-start | bytes 1572872 | tf_op jit(solution)/shard_map/ppermute | solution.py:480
  1.6 16.6 %collective-permute-start.4 = (bf16[64,32,128]{2,1,0:T(8,128)(2,1)}, bf16[64,32,128]{2,1,0:T(8,128)(2,1)S(1)}, u32[]{:S(2)}, u32[]{:S(2)}) collective-permute-start(bf16[64,32,128]{2,1,0:T(8,128)(2,1)} %bitcast.9), channel_id=1, source_target_pairs={{0,16},{1,65},{2,18},{3,67},{4,20},{5,69},{6,22},{7,71},{8,24},{9,... | collective-permute-start | bytes 1572872 | tf_op jit(solution)/shard_map/ppermute | solution.py:480
  4.3 13.9 %collective-permute-start.3 = (bf16[64,32,128]{2,1,0:T(8,128)(2,1)}, bf16[64,32,128]{2,1,0:T(8,128)(2,1)S(1)}, u32[]{:S(2)}, u32[]{:S(2)}) collective-permute-start(bf16[64,32,128]{2,1,0:T(8,128)(2,1)} %bitcast.10), channel_id=1, source_target_pairs={{0,24},{1,97},{2,26},{3,99},{4,28},{5,101},{6,30},{7,103},{8,0},{9... | collective-permute-start | bytes 1572872 | tf_op jit(solution)/shard_map/ppermute | solution.py:480
  6.6 0.7 copy-start
  8.3 5.3 %collective-permute-start = (s32[8,128]{1,0:T(8,128)S(1)}, s32[8,128]{1,0:T(8,128)S(1)}, u32[]{:S(2)}, u32[]{:S(2)}) collective-permute-start(s32[8,128]{1,0:T(8,128)S(1)} %get-tuple-element.33), channel_id=1, source_target_pairs={{0,32},{1,9},{2,34},{3,11},{4,36},{5,13},{6,38},{7,15},{8,40},{9,1... | collective-permute-start | bytes 12296 | tf_op jit(solution)/shard_map/ppermute | solution.py:484
  10.0 8.1 %collective-permute-start.1 = (s32[8,128]{1,0:T(8,128)S(1)}, s32[8,128]{1,0:T(8,128)S(1)}, u32[]{:S(2)}, u32[]{:S(2)}) collective-permute-start(s32[8,128]{1,0:T(8,128)S(1)} %get-tuple-element.34), channel_id=1, source_target_pairs={{0,64},{1,17},{2,66},{3,19},{4,68},{5,21},{6,70},{7,23},{8,72},{9,... | collective-permute-start | bytes 12296 | tf_op jit(solution)/shard_map/ppermute | solution.py:484
  13.6 4.5 %collective-permute-start.2 = (s32[8,128]{1,0:T(8,128)S(1)}, s32[8,128]{1,0:T(8,128)S(1)}, u32[]{:S(2)}, u32[]{:S(2)}) collective-permute-start(s32[8,128]{1,0:T(8,128)S(1)} %get-tuple-element.35), channel_id=1, source_target_pairs={{0,96},{1,25},{2,98},{3,27},{4,100},{5,29},{6,102},{7,31},{8,104},... | collective-permute-start | bytes 12296 | tf_op jit(solution)/shard_map/ppermute | solution.py:484
  19.1 9.4 %collective-permute-start.12 = (bf16[32,32,128]{2,1,0:T(8,128)(2,1)S(1)}, bf16[32,32,128]{2,1,0:T(8,128)(2,1)S(1)}, u32[]{:S(2)}, u32[]{:S(2)}) collective-permute-start(bf16[32,32,128]{2,1,0:T(8,128)(2,1)S(1)} %get-tuple-element.46), channel_id=1, source_target_pairs={{0,96},{1,25},{2,98},{3,27},{4,100},{5,29},{6,102},{7,31},{8,104},... | collective-permute-start | bytes 786440 | tf_op jit(solution)/shard_map/ppermute | solution.py:488
  21.8 8.0 %collective-permute-start.13 = (bf16[32,32,128]{2,1,0:T(8,128)(2,1)S(1)}, bf16[32,32,128]{2,1,0:T(8,128)(2,1)S(1)}, u32[]{:S(2)}, u32[]{:S(2)}) collective-permute-start(bf16[32,32,128]{2,1,0:T(8,128)(2,1)S(1)} %get-tuple-element.47), channel_id=1, source_target_pairs={{0,64},{1,17},{2,66},{3,19},{4,68},{5,21},{6,70},{7,23},{8,72},{9,... | collective-permute-start | bytes 786440 | tf_op jit(solution)/shard_map/ppermute | solution.py:488
  22.0 10.4 %collective-permute-start.14 = (bf16[32,32,128]{2,1,0:T(8,128)(2,1)S(1)}, bf16[32,32,128]{2,1,0:T(8,128)(2,1)S(1)}, u32[]{:S(2)}, u32[]{:S(2)}) collective-permute-start(bf16[32,32,128]{2,1,0:T(8,128)(2,1)S(1)} %get-tuple-element.48), channel_id=1, source_target_pairs={{0,32},{1,9},{2,34},{3,11},{4,36},{5,13},{6,38},{7,15},{8,40},{9,1... | collective-permute-start | bytes 786440 | tf_op jit(solution)/shard_map/ppermute | solution.py:488
  24.3 20.1 %collective-permute-start.9 = (bf16[32,32,128]{2,1,0:T(8,128)(2,1)S(1)}, bf16[32,32,128]{2,1,0:T(8,128)(2,1)S(1)}, u32[]{:S(2)}, u32[]{:S(2)}) collective-permute-start(bf16[32,32,128]{2,1,0:T(8,128)(2,1)S(1)} %get-tuple-element.42), channel_id=1, source_target_pairs={{0,96},{1,25},{2,98},{3,27},{4,100},{5,29},{6,102},{7,31},{8,104},... | collective-permute-start | bytes 786440 | tf_op jit(solution)/shard_map/ppermute | solution.py:490
  26.4 18.1 %collective-permute-start.10 = (bf16[32,32,128]{2,1,0:T(8,128)(2,1)S(1)}, bf16[32,32,128]{2,1,0:T(8,128)(2,1)S(1)}, u32[]{:S(2)}, u32[]{:S(2)}) collective-permute-start(bf16[32,32,128]{2,1,0:T(8,128)(2,1)S(1)} %get-tuple-element.43), channel_id=1, source_target_pairs={{0,64},{1,17},{2,66},{3,19},{4,68},{5,21},{6,70},{7,23},{8,72},{9,... | collective-permute-start | bytes 786440 | tf_op jit(solution)/shard_map/ppermute | solution.py:490
  28.5 15.9 %collective-permute-start.11 = (bf16[32,32,128]{2,1,0:T(8,128)(2,1)S(1)}, bf16[32,32,128]{2,1,0:T(8,128)(2,1)S(1)}, u32[]{:S(2)}, u32[]{:S(2)}) collective-permute-start(bf16[32,32,128]{2,1,0:T(8,128)(2,1)S(1)} %get-tuple-element.44), channel_id=1, source_target_pairs={{0,32},{1,9},{2,34},{3,11},{4,36},{5,13},{6,38},{7,15},{8,40},{9,1... | collective-permute-start | bytes 786440 | tf_op jit(solution)/shard_map/ppermute | solution.py:490
  45.4 1.8 %collective-permute-start.15 = (bf16[1536,128]{1,0:T(8,128)(2,1)S(1)}, bf16[1536,128]{1,0:T(8,128)(2,1)S(1)}, u32[]{:S(2)}, u32[]{:S(2)}) collective-permute-start(bf16[1536,128]{1,0:T(8,128)(2,1)S(1)} %get-tuple-element.58), channel_id=1, source_target_pairs={{0,1},{1,0},{2,3},{3,2},{4,5},{5,4},{6,7},{7,6},{8,9},{9,8},{10,11... | collective-permute-start | bytes 1179656 | tf_op jit(solution)/shard_map/ppermute | solution.py:498
  48.6 21.8 %all-to-all-start = ((bf16[64,24,128]{2,1,0:T(8,128)(2,1)}), bf16[64,24,128]{2,1,0:T(8,128)(2,1)S(1)}, u32[]{:S(2)}, u32[]{:S(2)}) async-start(bf16[64,24,128]{2,1,0:T(8,128)(2,1)} %bitcast.5), calls=%async_computation | async-start | bytes 786432 | tf_op jit(solution)/shard_map/all_to_all | solution.py:500
  58.2 6.2 %collective-permute-start.8 = (s32[4,8,128]{2,1,0:T(8,128)S(1)}, s32[4,8,128]{2,1,0:T(8,128)S(1)}, u32[]{:S(2)}, u32[]{:S(2)}) collective-permute-start(s32[4,8,128]{2,1,0:T(8,128)S(1)} %get-tuple-element.41.tables0), channel_id=1, source_target_pairs={{0,24},{1,97},{2,26},{3,99},{4,28},{5,101},{6,30},{7,103},{8,0},{9... | collective-permute-start | bytes 49160 | tf_op jit(solution)/shard_map/ppermute | solution.py:491
  61.1 5.2 %collective-permute-start.7 = (s32[4,8,128]{2,1,0:T(8,128)S(1)}, s32[4,8,128]{2,1,0:T(8,128)S(1)}, u32[]{:S(2)}, u32[]{:S(2)}) collective-permute-start(s32[4,8,128]{2,1,0:T(8,128)S(1)} %get-tuple-element.41.tables0), channel_id=1, source_target_pairs={{0,16},{1,65},{2,18},{3,67},{4,20},{5,69},{6,22},{7,71},{8,24},{9,... | collective-permute-start | bytes 49160 | tf_op jit(solution)/shard_map/ppermute | solution.py:491
  61.9 4.9 %collective-permute-start.6 = (s32[4,8,128]{2,1,0:T(8,128)S(1)}, s32[4,8,128]{2,1,0:T(8,128)S(1)}, u32[]{:S(2)}, u32[]{:S(2)}) collective-permute-start(s32[4,8,128]{2,1,0:T(8,128)S(1)} %get-tuple-element.41.tables0), channel_id=1, source_target_pairs={{0,8},{1,33},{2,10},{3,35},{4,12},{5,37},{6,14},{7,39},{8,16},{9,4... | collective-permute-start | bytes 49160 | tf_op jit(solution)/shard_map/ppermute | solution.py:491
